TPU v7x, 512 devices: a whole 4x4x16 slice. The times are simulated.
512 devices in a mesh: dp: 32 (over z, core), tensor: 16 (over y, x).
Axes of the slice: x: 4, y: 4, z: 16, core: 2. Of those that a mesh axis runs over, the one named last changes fastest.
Arguments:
- gradients: bfloat16 [32, 512, 4096], P('dp', None, 'tensor'), may hold values from -12 to 12
- momentum: float32 [512, 4096], P('dp', 'tensor'), may hold values from -16 to 16
- weight: float32 [512, 4096], P('dp', 'tensor'), may hold values from -0.25 to 0.25
Outputs:
- new_momentum: float32 [512, 4096], P('dp', 'tensor')
- new_weight: float32 [512, 4096], P('dp', 'tensor')
- residual: float32 [512, 512], P('dp', 'tensor')
All inputs are finite; a program needn't handle non-finite values.
Results may differ from a plain program's by a relative error of at most 0.0003.
Values sent between devices are 32-bit elements; how exact they have to be, the bound alone decides.
No kernel may reach another device: no remote copies, remote signals or barrier semaphores. Data moves between devices by JAX's collectives and lax.ppermute only.
A program may use at most 64 MiB of HBM per device.

v0:
```python
import jax
import jax.numpy as jnp
from jax import lax
from jax.sharding import PartitionSpec as P

IN = 512
OUT = 4096
ITERS = 2


decay_rate = 0.95
learn_rate = 0.02
weight_decay = 0.1
epsilon = 1e-07
quintic_a = 3.4445
quintic_b = -4.775
quintic_c = 2.0315


def per_device(gradients, momentum, weight):
    highest = lax.Precision.HIGHEST
    row_count = momentum.shape[0]
    row_start = lax.axis_index("dp") * row_count
    local_grad = gradients[0].astype(jnp.float32)
    summed = lax.psum_scatter(local_grad, "dp", scatter_dimension=0, tiled=True)
    new_momentum = decay_rate * momentum + summed
    squares = lax.psum(jnp.sum(new_momentum * new_momentum), ("dp", "tensor"))
    local_start = new_momentum / (jnp.sqrt(squares) + epsilon)
    iterate = lax.all_gather(local_start, "dp", axis=0, tiled=True)
    for sweep in range(ITERS):
        partial_value = jnp.einsum("io,jo->ij", iterate, iterate, precision=highest)
        gram_mat = lax.psum(partial_value, "tensor")
        product_one = jnp.dot(gram_mat, iterate, precision=highest)
        product_two = jnp.dot(gram_mat, product_one, precision=highest)
        iterate = quintic_a * iterate + quintic_b * product_one + quintic_c * product_two
    scale_factor = 0.2 * jnp.sqrt(jnp.float32(max(IN, OUT)))
    own_rows = lax.dynamic_slice_in_dim(iterate, row_start, row_count, 0)
    new_weight = weight * (1.0 - learn_rate * weight_decay) - learn_rate * scale_factor * own_rows
    width_all = iterate.shape[0]
    col_count = width_all // lax.axis_size("tensor")
    col_start = lax.axis_index("tensor") * col_count
    final_gram = jnp.einsum("io,jo->ij", iterate, iterate, precision=highest)
    whole_gram = lax.psum(final_gram, "tensor")
    row_band = lax.dynamic_slice_in_dim(whole_gram, row_start, row_count, 0)
    row_block = lax.dynamic_slice_in_dim(row_band, col_start, col_count, 1)
    row_ids = row_start + lax.broadcasted_iota(jnp.int32, (row_count, col_count), 0)
    col_ids = col_start + lax.broadcasted_iota(jnp.int32, (row_count, col_count), 1)
    identity = jnp.where(row_ids == col_ids, jnp.float32(1.0), jnp.float32(0.0))
    residual = row_block - identity
    return (new_momentum, new_weight, residual)


def solution(mesh):
    return jax.shard_map(
        per_device,
        mesh=mesh,
        in_specs=(P("dp", None, "tensor"), P("dp", "tensor"), P("dp", "tensor")),
        out_specs=(P("dp", "tensor"), P("dp", "tensor"), P("dp", "tensor")),
        check_vma=False,
    )
```

profile of v0, /device:TPU:1, one launch (start us, length us, event | category | flops | bytes accessed | tf_op | source)
XLA Modules:
  0.0 623.7 jit_solution(2027876323697508737)
XLA Ops:
  7.2 0.0 reduce-scatter.2.cloned.1.call-start
  7.2 1.8 bitcast_convert_fusion
  9.0 0.0 copy-start.3
  9.0 0.0 reduce-scatter.2.cloned.1.call-update
  9.0 0.0 all-reduce.4.cloned.1.call-start
  9.1 111.3 %reduce-scatter.2.cloned.1.call-done = f32[16,256]{1,0:T(8,128)} async-done(((f32[512,256]{1,0:T(8,128)}), f32[16,256]{1,0:T(8,128)}) %reduce-scatter.2.cloned.1.call-update) | async-done | bytes 16400 | tf_op jit(solution)/shard_map/reduce_scatter | solution.py:25
  120.4 0.0 copy-done.3
  120.4 1.3 multiply_reduce_fusion
  121.7 0.0 copy-start.2
  121.7 105.8 %psum.28 = f32[]{:T(128)} all-reduce(f32[]{:T(128)} %get-tuple-element.3), channel_id=1, replica_groups=mesh['dp'=32,'tensor'=16] {'dp','tensor'}, use_global_device_ids=true, to_apply=%region_2.0 | all-reduce | flops 1 | bytes 8 | tf_op jit(solution)/shard_map/psum | solution.py:27
  228.2 0.0 copy-done.2
  228.2 29.0 %all_gather.3 = f32[512,256]{1,0:T(8,128)S(1)} all-gather(f32[16,256]{1,0:T(8,128)S(1)} %broadcast_divide_fusion), channel_id=1, replica_groups=mesh['dp'=32,'tensor'=16] {'dp'}, dimensions={0}, use_global_device_ids=true | all-gather | bytes 540672 | tf_op jit(solution)/shard_map/all_gather | solution.py:29
  257.3 2.1 fusion.2
  259.3 0.0 all-reduce.4.cloned.1.call-update
  259.4 0.0 all-reduce.6.cloned.1.call-start
  259.4 111.0 %all-reduce.4.cloned.1.call-done = f32[512,512]{1,0:T(8,128)} async-done(((f32[512,512]{1,0:T(8,128)}), f32[512,512]{1,0:T(8,128)}) %all-reduce.4.cloned.1.call-update) | async-done | bytes 1048592 | tf_op jit(solution)/shard_map/psum | solution.py:32
  370.4 0.0 copy-start
  370.4 2.3 fusion.3
  372.7 0.0 copy-done
  372.7 1.0 fusion
  373.7 2.1 fusion.4
  375.8 0.0 all-reduce.6.cloned.1.call-update
  375.8 0.0 all-reduce.8.cloned.1.call-start
  375.9 117.2 %all-reduce.6.cloned.1.call-done = f32[512,512]{1,0:T(8,128)} async-done(((f32[512,512]{1,0:T(8,128)}), f32[512,512]{1,0:T(8,128)}) %all-reduce.6.cloned.1.call-update) | async-done | bytes 1048592 | tf_op jit(solution)/shard_map/psum | solution.py:32
  493.1 0.0 copy-start.1
  493.1 2.3 fusion.5
  495.4 0.0 copy-done.1
  495.4 1.0 fusion.1
  496.4 2.1 fusion.6
  498.5 0.0 all-reduce.8.cloned.1.call-update
  498.5 0.0 copy-start.4
  498.6 0.7 copy-done.4
  499.3 0.6 multiply_subtract_fusion
  499.9 115.9 %all-reduce.8.cloned.1.call-done = f32[512,512]{1,0:T(8,128)} async-done(((f32[512,512]{1,0:T(8,128)}), f32[512,512]{1,0:T(8,128)}) %all-reduce.8.cloned.1.call-update) | async-done | bytes 1048592 | tf_op jit(solution)/shard_map/psum | solution.py:43
  615.8 1.4 select_subtract_fusion
  (3 shorter events, 0.0 us)
Async XLA Ops:
  7.2 113.2 %reduce-scatter.2.cloned.1.call-start = ((), (), s32[]{:S(2)}) async-start(), calls=%async_computation.1 | async-start | bytes 540672 | tf_op jit(solution)/shard_map/reduce_scatter | solution.py:25
  9.0 111.4 %copy-start.3 = (f32[16,256]{1,0:T(8,128)S(1)}, f32[16,256]{1,0:T(8,128)}, u32[]{:S(2)}) copy-start(f32[16,256]{1,0:T(8,128)} %param.4) | copy-start | bytes 49156
  9.0 361.4 %all-reduce.4.cloned.1.call-start = ((), (), s32[]{:S(2)}) async-start(), calls=%async_computation.2 | async-start | bytes 2097152 | tf_op jit(solution)/shard_map/psum | solution.py:32
  121.7 106.5 %copy-start.2 = (f32[16,256]{1,0:T(8,128)}, f32[16,256]{1,0:T(8,128)S(1)}, u32[]{:S(2)}) copy-start(f32[16,256]{1,0:T(8,128)S(1)} %get-tuple-element.4) | copy-start | bytes 49156
  259.4 233.8 %all-reduce.6.cloned.1.call-start = ((), (), s32[]{:S(2)}) async-start(), calls=%async_computation.3 | async-start | bytes 2097152 | tf_op jit(solution)/shard_map/psum | solution.py:32
  370.4 2.3 copy-start
  375.8 240.0 %all-reduce.8.cloned.1.call-start = ((), (), s32[]{:S(2)}) async-start(), calls=%async_computation.4 | async-start | bytes 2097152 | tf_op jit(solution)/shard_map/psum | solution.py:43
  493.1 2.3 copy-start.1
  498.5 0.7 copy-start.4
Sparse Core Ops, SparseCore 0:
  10.8 109.5 reduce-scatter.1
  259.5 110.8 all-reduce.3
  376.0 117.1 all-reduce.5
  498.7 117.0 all-reduce.7
where the time goes:
time: 625 us; the launch traced here: 624 us
  waiting for transfers between devices  456 us (73%)
  blocking collectives  135 us (22%)
  between operations  14.6 us (2%)
  matrix products  12.8 us (2%)
    psum x2, waiting for transfers between devices, per_device(): gram_mat = lax.psum(partial_value, 'tensor')  228 us
    psum x1, waiting for transfers between devices, per_device(): whole_gram = lax.psum(final_gram, 'tensor')  116 us
    reduce_scatter x1, waiting for transfers between devices, per_device(): summed = lax.psum_scatter(local_grad, 'dp', scatter_dimension=0, tiled=True)  111 us
    psum x1, blocking collectives, per_device(): squares = lax.psum(jnp.sum(new_momentum * new_momentum), ('dp', 'tensor'))  106 us
    all_gather x1, blocking collectives, per_device(): iterate = lax.all_gather(local_start, 'dp', axis=0, tiled=True)  29 us
  transfers between devices with their start and end apart: 4, of which 4 were waited for; matrix products, arithmetic and copies ran while one was open for 0% of the time, Pallas kernels for 0%

commit v1 on v0

v1 whole, which is shorter than its diff:
```python
import jax
import jax.numpy as jnp
from jax import lax
from jax.experimental import pallas as pl
from jax.experimental.pallas import tpu as pltpu
from jax.sharding import PartitionSpec as P

IN = 512
OUT = 4096

decay_rate = 0.95
learn_rate = 0.02
weight_decay = 0.1
epsilon = 1e-07
quintic_a = 3.4445
quintic_b = -4.775
quintic_c = 2.0315

f32 = jnp.float32
bf16 = jnp.bfloat16

CORE = [(i, i ^ 1) for i in range(32)]
NEAR = [[8 * far + 2 * near + core for near in range(4)] for far in range(4) for core in range(2)]
FAR = [[8 * far + 2 * near + core for far in range(4)] for near in range(4) for core in range(2)]

NT = (((1,), (1,)), ((), ()))
NN = (((1,), (0,)), ((), ()))


def place():
    index = lax.axis_index("dp")
    return index // 8, (index // 2) % 4, index % 2


def halves(value):
    high = value.astype(bf16)
    low = (value - high.astype(f32)).astype(bf16)
    return high, low


def mul3(left, right, dims):
    dot = lambda x, y: lax.dot_general(x, y, dims, preferred_element_type=f32)
    return dot(left[0], right[0]) + (dot(left[0], right[1]) + dot(left[1], right[0]))


def split_kernel(grad_ref, keep_ref, send_ref):
    _, _, core = place()
    for far in range(4):
        for near in range(4):
            keep_ref[near, far] = grad_ref[far, near, core].astype(f32)
            send_ref[near, far] = grad_ref[far, near, 1 - core].astype(f32)


def near_sum_kernel(parts_ref, momentum_ref, out_ref):
    mine, _, _ = place()
    for far in range(4):
        total = (parts_ref[0, far] + parts_ref[1, far]) + (parts_ref[2, far] + parts_ref[3, far])
        total = total + jnp.where(mine == far, f32(decay_rate), f32(0.0)) * momentum_ref[...]
        for other in range(4):
            out_ref[other, far] = total


def far_sum_kernel(parts_ref, out_ref, momentum_ref):
    mine, _, _ = place()
    for far in range(4):
        total = (parts_ref[0, far] + parts_ref[1, far]) + (parts_ref[2, far] + parts_ref[3, far])
        for other in range(4):
            out_ref[other, far] = total
    momentum_ref[...] = out_ref[0, mine]


def gram_kernel(mine_ref, other_ref, out_ref, rows_ref):
    _, _, core = place()
    rows_ref[core] = mine_ref[...]
    rows_ref[1 - core] = other_ref[...]
    own = halves(mine_ref[...])
    upper = tuple(part[:128] for part in own)
    lower = tuple(part[128:] for part in own)
    out_ref[0:128] = mul3(upper, upper, NT)
    out_ref[128:256] = mul3(upper, lower, NT)
    out_ref[256:384] = mul3(lower, lower, NT)
    left = halves(rows_ref[0])
    right = halves(rows_ref[1, pl.ds(pl.multiple_of(core * 128, 128), 128)])
    out_ref[384:640] = mul3(left, right, NT)


def tensor_sum_kernel(parts_ref, out_ref):
    total = parts_ref[0]
    for index in range(1, 16):
        total = total + parts_ref[index]
    for index in range(16):
        out_ref[index] = total


def diagonal(start_row, start_column, shape):
    rows = start_row + lax.broadcasted_iota(jnp.int32, shape, 0)
    columns = start_column + lax.broadcasted_iota(jnp.int32, shape, 1)
    return rows == columns


def final_kernel(mine_ref, other_ref, rows_ref, weight_ref, new_weight_ref, residual_ref, gram_ref, first_ref, next_ref):
    far, near, core = place()
    tensor = lax.axis_index("tensor")
    for which in range(2):
        pick = core == which
        block = lambda start, size: jnp.where(pick, mine_ref[start : start + size], other_ref[start : start + size])
        base = 256 * which
        corner = block(128, 128)
        gram_ref[base : base + 128, base : base + 128] = block(0, 128)
        gram_ref[base : base + 128, base + 128 : base + 256] = corner
        gram_ref[base + 128 : base + 256, base : base + 128] = corner.T
        gram_ref[base + 128 : base + 256, base + 128 : base + 256] = block(256, 128)
        cross = block(384, 256)
        start = 256 + 128 * which
        gram_ref[0:256, start : start + 128] = cross
        gram_ref[start : start + 128, 0:256] = cross.T
    unit = diagonal(0, 0, (IN, IN))
    whole = gram_ref[...]
    squares = jnp.sum(jnp.sum(jnp.where(unit, whole, 0.0), axis=1, keepdims=True), axis=0, keepdims=True)
    inverse = 1.0 / (jnp.sqrt(squares) + epsilon)
    gram = (whole * inverse) * inverse
    pair = halves(gram)
    first = quintic_b * gram + quintic_c * mul3(pair, pair, NN) + jnp.where(unit, f32(quintic_a), f32(0.0))
    first_ref[...] = first
    first_pair = halves(first)
    inner = mul3(first_pair, pair, NN)
    after = mul3(first_pair, halves(inner), NN)
    next_ref[...] = after
    after_pair = halves(after)
    mine = core * 256 + near * 64 + far * 16
    column_base = lax.rem(tensor, 4) * 64 + lax.div(tensor, 4) * 16
    starts = (mine, column_base, 256 + column_base)
    bands = [next_ref[pl.ds(pl.multiple_of(start, 16), 16)] for start in starts]
    slab = jnp.concatenate(bands, axis=0)
    units = jnp.concatenate([diagonal(start, 0, (16, IN)) for start in starts], axis=0)
    second = quintic_b * slab + quintic_c * mul3(halves(slab), after_pair, NN) + jnp.where(units, f32(quintic_a), f32(0.0))
    own = halves(second[0:16])
    total = mul3(own, first_pair, NN)
    rows = rows_ref[...].reshape(IN, 256)
    update = mul3(halves(total), halves(rows), NN) * inverse
    scale = learn_rate * 0.2 * float(max(IN, OUT)) ** 0.5
    new_weight_ref[...] = weight_ref[...] * (1.0 - learn_rate * weight_decay) - scale * update
    product = mul3(own, after_pair, NN)
    final = mul3(halves(product), halves(second[16:48]), NT)
    identity = diagonal((far * 8 + near * 2 + core) * 16, tensor * 32, (16, 32))
    residual_ref[...] = final - jnp.where(identity, f32(1.0), f32(0.0))


def call(kernel, outs, scratch=(), limit=None):
    params = pltpu.CompilerParams(vmem_limit_bytes=limit) if limit else None
    return pl.pallas_call(
        kernel,
        out_shape=tuple(jax.ShapeDtypeStruct(shape, f32) for shape in outs),
        scratch_shapes=list(scratch),
        compiler_params=params,
    )


def exchange(value, axis, groups=None):
    return lax.all_to_all(value, axis, 0, 0, tiled=True, axis_index_groups=groups)


def per_device(gradients, momentum, weight):
    chunks = (4, 4, 16, 256)
    keep, send = call(split_kernel, [chunks, chunks])(gradients.reshape(4, 4, 2, 16, 256))
    parts = keep + lax.ppermute(send, "dp", CORE)
    (spread,) = call(near_sum_kernel, [chunks])(exchange(parts, "dp", NEAR), momentum)
    spread, new_momentum = call(far_sum_kernel, [chunks, (16, 256)])(exchange(spread, "dp", FAR))
    mine = exchange(spread, "dp", NEAR).reshape(256, 256)
    other = lax.ppermute(mine, "dp", CORE)
    blocks, rows = call(gram_kernel, [(640, 128), (2, 256, 256)], limit=32 << 20)(mine, other)
    (spread,) = call(tensor_sum_kernel, [(16, 40, 128)])(exchange(blocks.reshape(16, 40, 128), "tensor"))
    mine = exchange(spread, "tensor").reshape(640, 128)
    other = lax.ppermute(mine, "dp", CORE)
    new_weight, residual = call(
        final_kernel,
        [(16, 256), (16, 32)],
        [pltpu.VMEM((IN, IN), f32)] * 3,
        limit=48 << 20,
    )(mine, other, rows, weight)
    return (new_momentum, new_weight, residual)


def solution(mesh):
    return jax.shard_map(
        per_device,
        mesh=mesh,
        in_specs=(P("dp", None, "tensor"), P("dp", "tensor"), P("dp", "tensor")),
        out_specs=(P("dp", "tensor"), P("dp", "tensor"), P("dp", "tensor")),
        check_vma=False,
    )
```

time: 625 us -> 113 us (0.18)
  waiting for transfers between devices: 456 us -> 3.72 us
  blocking collectives: 135 us -> 74.6 us
  starting transfers between devices: 0.16 us -> 20.1 us
  between operations: 14.6 us -> 0.67 us
  matrix products: 12.8 us -> 0 us
  Pallas kernels: 0 us -> 12.1 us
    psum x3 -> x0, waiting for transfers between devices: 344 us -> none  [the longest x2 228 us: per_device(): gram_mat = lax.psum(partial_value, 'tensor')]
    reduce_scatter x1 -> x0, waiting for transfers between devices: 111 us -> none  [per_device(): summed = lax.psum_scatter(local_grad, 'dp', scatter_dimension=0, tiled=True)]
    psum x1 -> x0, blocking collectives: 106 us -> none  [per_device(): squares = lax.psum(jnp.sum(new_momentum * new_momentum), ('dp', 'tensor'))]
    all_to_all x0 -> x5, blocking collectives: none -> 74.6 us  [exchange(): lax.all_to_all(value, axis, 0, 0, tiled=True, axis_index_groups=groups)]
    all_gather x1 -> x0, blocking collectives: 29 us -> none  [per_device(): iterate = lax.all_gather(local_start, 'dp', axis=0, tiled=True)]
    ppermute x0 -> x3, starting transfers between devices: none -> 20.1 us  [the longest x2 11.3 us: per_device(): other = lax.ppermute(mine, 'dp', CORE)]
    dot_general x7 -> x0, matrix products: 12.8 us -> none  [the longest x2 4.59 us: per_device(): product_one = jnp.dot(gram_mat, iterate, precision=highest)]
    pallas_call x0 -> x6, Pallas kernels: none -> 12.1 us  [the longest x1 4.84 us: per_device(): call(final_kernel, [(16, 256), (16, 32)], [pltpu.VMEM((IN, IN), f32)] * 3...]
  transfers between devices with their start and end apart: 4 -> 3, of which waited for: 4 -> 3; matrix products, arithmetic and copies ran while one was open for 0% -> 0% of each run, Pallas kernels for 0% -> 0%
where the time goes in v1:
time: 113 us; the launch traced here: 112 us
  blocking collectives  74.6 us (66%)
  starting transfers between devices  20.1 us (18%)
  Pallas kernels  12.1 us (11%)
  waiting for transfers between devices  3.72 us (3%)
    all_to_all x5, blocking collectives, exchange(): lax.all_to_all(value, axis, 0, 0, tiled=True, axis_index_groups=groups)  74.6 us
    ppermute x2, starting transfers between devices, per_device(): other = lax.ppermute(mine, 'dp', CORE)  11.3 us
    ppermute x1, starting transfers between devices, per_device(): parts = keep + lax.ppermute(send, 'dp', CORE)  8.77 us
    pallas_call x1, Pallas kernels, per_device(): call(final_kernel, [(16, 256), (16, 32)], [pltpu.VMEM((IN, IN), f32)] * 3...  4.84 us
    ppermute x2, waiting for transfers between devices, per_device(): other = lax.ppermute(mine, 'dp', CORE)  2.37 us
  transfers between devices with their start and end apart: 3, of which 3 were waited for; matrix products, arithmetic and copies ran while one was open for 0% of the time, Pallas kernels for 0%

profile of v1, /device:TPU:1, one launch (start us, length us, event | category | flops | bytes accessed | tf_op | source)
XLA Modules:
  0.0 112.1 jit_solution(1542457652505792119)
XLA Ops:
  0.6 1.8 %shard_map.58 = (f32[4,4,16,256]{3,2,1,0:T(8,128)}, f32[4,4,16,256]{3,2,1,0:T(8,128)}) custom-call(bf16[4,4,2,16,256]{4,3,2,1,0:T(8,128)(2,1)} %bitcast.9), custom_call_target="tpu_custom_call" | custom-call | tf_op jit(solution)/shard_map/pallas_call | solution.py:165
  2.4 8.8 %collective-permute-start = (f32[4,4,16,256]{3,2,1,0:T(8,128)}, f32[4,4,16,256]{3,2,1,0:T(8,128)S(1)}, u32[]{:S(2)}, u32[]{:S(2)}) collective-permute-start(f32[4,4,16,256]{3,2,1,0:T(8,128)} %get-tuple-element.12), channel_id=1, source_target_pairs={{0,16},{16,0},{32,48},{48,32},{64,80},{80,64},{96,112},{112,96},{1... | collective-permute-start | bytes 786440 | tf_op jit(solution)/shard_map/ppermute | solution.py:166
  11.2 1.4 %collective-permute-done = f32[4,4,16,256]{3,2,1,0:T(8,128)S(1)} collective-permute-done((f32[4,4,16,256]{3,2,1,0:T(8,128)}, f32[4,4,16,256]{3,2,1,0:T(8,128)S(1)}, u32[]{:S(2)}, u32[]{:S(2)}) %collective-permute-start) | collective-permute-done | bytes 262176 | tf_op jit(solution)/shard_map/ppermute | solution.py:166
  12.5 1.0 add.3
  13.5 11.3 %all_to_all.25.parts_ref = f32[4,4,16,256]{3,2,1,0:T(8,128)} all-to-all(f32[4,4,16,256]{3,2,1,0:T(8,128)S(1)} %add.3), channel_id=1, replica_groups={{0,32,64,96},{16,48,80,112},{128,160,192,224},{144,176,208,240},{256,28..., dimensions={0} | all-to-all | bytes 524288 | tf_op jit(solution)/shard_map/all_to_all | solution.py:160
  24.9 1.7 %shard_map.59 = f32[4,4,16,256]{3,2,1,0:T(8,128)} custom-call(f32[4,4,16,256]{3,2,1,0:T(8,128)} %all_to_all.25.parts_ref, f32[16,256]{1,0:T(8,128)} %momentum_ref.1), custom_call_target="tpu_custom_call" | custom-call | tf_op jit(solution)/shard_map/pallas_call | solution.py:167
  26.5 23.4 %all_to_all.26.parts_ref = f32[4,4,16,256]{3,2,1,0:T(8,128)} all-to-all(f32[4,4,16,256]{3,2,1,0:T(8,128)} %shard_map.59), channel_id=1, replica_groups={{0,128,256,384},{16,144,272,400},{32,160,288,416},{48,176,304,432},{64,..., dimensions={0} | all-to-all | bytes 524288 | tf_op jit(solution)/shard_map/all_to_all | solution.py:160
  49.9 1.7 %shard_map.60 = (f32[4,4,16,256]{3,2,1,0:T(8,128)}, f32[16,256]{1,0:T(8,128)}) custom-call(f32[4,4,16,256]{3,2,1,0:T(8,128)} %all_to_all.26.parts_ref), custom_call_target="tpu_custom_call" | custom-call | tf_op jit(solution)/shard_map/pallas_call | solution.py:168
  51.6 12.7 %all_to_all.27 = f32[4,4,16,256]{3,2,1,0:T(8,128)S(1)} all-to-all(f32[4,4,16,256]{3,2,1,0:T(8,128)} %get-tuple-element.14), channel_id=1, replica_groups={{0,32,64,96},{16,48,80,112},{128,160,192,224},{144,176,208,240},{256,28..., dimensions={0} | all-to-all | bytes 524288 | tf_op jit(solution)/shard_map/all_to_all | solution.py:160
  64.3 6.9 %collective-permute-start.1 = (f32[256,256]{1,0:T(8,128)S(1)}, f32[256,256]{1,0:T(8,128)S(1)}, u32[]{:S(2)}, u32[]{:S(2)}) collective-permute-start(f32[256,256]{1,0:T(8,128)S(1)} %bitcast.6), channel_id=1, source_target_pairs={{0,16},{16,0},{32,48},{48,32},{64,80},{80,64},{96,112},{112,96},{1... | collective-permute-start | bytes 786440 | tf_op jit(solution)/shard_map/ppermute | solution.py:170
  71.2 1.1 %collective-permute-done.1.other_ref = f32[256,256]{1,0:T(8,128)S(1)} collective-permute-done((f32[256,256]{1,0:T(8,128)S(1)}, f32[256,256]{1,0:T(8,128)S(1)}, u32[]{:S(2)}, u32[]{:S(2)}) %collective-permute-start.1) | collective-permute-done | bytes 262176 | tf_op jit(solution)/shard_map/ppermute | solution.py:170
  72.3 0.4 shard_map.61
  72.7 15.5 %all_to_all.28.parts_ref = f32[16,40,128]{2,1,0:T(8,128)} all-to-all(f32[16,40,128]{2,1,0:T(8,128)S(1)} %bitcast.8), channel_id=1, replica_groups=mesh['dp'=32,'tensor'=16] {'tensor'}, dimensions={0} | all-to-all | bytes 655360 | tf_op jit(solution)/shard_map/all_to_all | solution.py:160
  88.2 1.7 %shard_map.62 = f32[16,40,128]{2,1,0:T(8,128)} custom-call(f32[16,40,128]{2,1,0:T(8,128)} %all_to_all.28.parts_ref), custom_call_target="tpu_custom_call" | custom-call | tf_op jit(solution)/shard_map/pallas_call | solution.py:172
  90.0 0.0 copy-start
  90.0 11.7 %all_to_all.29 = f32[16,40,128]{2,1,0:T(8,128)S(1)} all-to-all(f32[16,40,128]{2,1,0:T(8,128)} %shard_map.62), channel_id=1, replica_groups=mesh['dp'=32,'tensor'=16] {'tensor'}, dimensions={0} | all-to-all | bytes 655360 | tf_op jit(solution)/shard_map/all_to_all | solution.py:160
  101.6 4.4 %collective-permute-start.2 = (f32[640,128]{1,0:T(8,128)S(1)}, f32[640,128]{1,0:T(8,128)S(1)}, u32[]{:S(2)}, u32[]{:S(2)}) collective-permute-start(f32[640,128]{1,0:T(8,128)S(1)} %bitcast.4), channel_id=1, source_target_pairs={{0,16},{16,0},{32,48},{48,32},{64,80},{80,64},{96,112},{112,96},{1... | collective-permute-start | bytes 983048 | tf_op jit(solution)/shard_map/ppermute | solution.py:174
  106.1 1.2 %collective-permute-done.2.other_ref = f32[640,128]{1,0:T(8,128)S(1)} collective-permute-done((f32[640,128]{1,0:T(8,128)S(1)}, f32[640,128]{1,0:T(8,128)S(1)}, u32[]{:S(2)}, u32[]{:S(2)}) %collective-permute-start.2) | collective-permute-done | bytes 327712 | tf_op jit(solution)/shard_map/ppermute | solution.py:174
  107.3 0.0 copy-done
  107.3 4.8 %shard_map.63 = (f32[16,256]{1,0:T(8,128)}, f32[16,32]{1,0:T(8,128)}) custom-call(f32[640,128]{1,0:T(8,128)S(1)} %bitcast.5, f32[640,128]{1,0:T(8,128)S(1)} %collective-permute-done.2.other_ref, f32[2,256,256]{2,1,0:T(8,128)S(1)} %get-tuple-element.16.rows_ref, f32[16,256]{1,0:T(8,128)S(1)} %copy-done), custom_call_target="tpu_custom_call" | custom-call | tf_op jit(solution)/shard_map/pallas_call | solution.py:175
Async XLA Ops:
  2.4 10.1 %collective-permute-start = (f32[4,4,16,256]{3,2,1,0:T(8,128)}, f32[4,4,16,256]{3,2,1,0:T(8,128)S(1)}, u32[]{:S(2)}, u32[]{:S(2)}) collective-permute-start(f32[4,4,16,256]{3,2,1,0:T(8,128)} %get-tuple-element.12), channel_id=1, source_target_pairs={{0,16},{16,0},{32,48},{48,32},{64,80},{80,64},{96,112},{112,96},{1... | collective-permute-start | bytes 786440 | tf_op jit(solution)/shard_map/ppermute | solution.py:166
  64.3 8.0 %collective-permute-start.1 = (f32[256,256]{1,0:T(8,128)S(1)}, f32[256,256]{1,0:T(8,128)S(1)}, u32[]{:S(2)}, u32[]{:S(2)}) collective-permute-start(f32[256,256]{1,0:T(8,128)S(1)} %bitcast.6), channel_id=1, source_target_pairs={{0,16},{16,0},{32,48},{48,32},{64,80},{80,64},{96,112},{112,96},{1... | collective-permute-start | bytes 786440 | tf_op jit(solution)/shard_map/ppermute | solution.py:170
  90.0 17.3 %copy-start = (f32[16,256]{1,0:T(8,128)S(1)}, f32[16,256]{1,0:T(8,128)}, u32[]{:S(2)}) copy-start(f32[16,256]{1,0:T(8,128)} %weight_ref.1) | copy-start | bytes 49156
  101.6 5.7 %collective-permute-start.2 = (f32[640,128]{1,0:T(8,128)S(1)}, f32[640,128]{1,0:T(8,128)S(1)}, u32[]{:S(2)}, u32[]{:S(2)}) collective-permute-start(f32[640,128]{1,0:T(8,128)S(1)} %bitcast.4), channel_id=1, source_target_pairs={{0,16},{16,0},{32,48},{48,32},{64,80},{80,64},{96,112},{112,96},{1... | collective-permute-start | bytes 983048 | tf_op jit(solution)/shard_map/ppermute | solution.py:174

commit v2 on v1

--- a/solution.py
+++ b/solution.py
@@ -43,12 +43,18 @@
     return dot(left[0], right[0]) + (dot(left[0], right[1]) + dot(left[1], right[0]))
 
 
-def split_kernel(grad_ref, keep_ref, send_ref):
+def send_kernel(grad_ref, send_ref):
     _, _, core = place()
     for far in range(4):
         for near in range(4):
-            keep_ref[near, far] = grad_ref[far, near, core].astype(f32)
             send_ref[near, far] = grad_ref[far, near, 1 - core].astype(f32)
+
+
+def core_sum_kernel(grad_ref, got_ref, out_ref):
+    _, _, core = place()
+    for far in range(4):
+        for near in range(4):
+            out_ref[near, far] = grad_ref[far, near, core].astype(f32) + got_ref[near, far]
 
 
 def near_sum_kernel(parts_ref, momentum_ref, out_ref):
@@ -146,13 +152,12 @@
     residual_ref[...] = final - jnp.where(identity, f32(1.0), f32(0.0))
 
 
-def call(kernel, outs, scratch=(), limit=None):
-    params = pltpu.CompilerParams(vmem_limit_bytes=limit) if limit else None
+def call(kernel, outs, scratch=(), limit=4 << 20):
     return pl.pallas_call(
         kernel,
         out_shape=tuple(jax.ShapeDtypeStruct(shape, f32) for shape in outs),
         scratch_shapes=list(scratch),
-        compiler_params=params,
+        compiler_params=pltpu.CompilerParams(vmem_limit_bytes=limit),
     )
 
 
@@ -162,13 +167,14 @@
 
 def per_device(gradients, momentum, weight):
     chunks = (4, 4, 16, 256)
-    keep, send = call(split_kernel, [chunks, chunks])(gradients.reshape(4, 4, 2, 16, 256))
-    parts = keep + lax.ppermute(send, "dp", CORE)
+    gradients = gradients.reshape(4, 4, 2, 16, 256)
+    (send,) = call(send_kernel, [chunks])(gradients)
+    (parts,) = call(core_sum_kernel, [chunks])(gradients, lax.ppermute(send, "dp", CORE))
     (spread,) = call(near_sum_kernel, [chunks])(exchange(parts, "dp", NEAR), momentum)
     spread, new_momentum = call(far_sum_kernel, [chunks, (16, 256)])(exchange(spread, "dp", FAR))
     mine = exchange(spread, "dp", NEAR).reshape(256, 256)
     other = lax.ppermute(mine, "dp", CORE)
-    blocks, rows = call(gram_kernel, [(640, 128), (2, 256, 256)], limit=32 << 20)(mine, other)
+    blocks, rows = call(gram_kernel, [(640, 128), (2, 256, 256)], limit=8 << 20)(mine, other)
     (spread,) = call(tensor_sum_kernel, [(16, 40, 128)])(exchange(blocks.reshape(16, 40, 128), "tensor"))
     mine = exchange(spread, "tensor").reshape(640, 128)
     other = lax.ppermute(mine, "dp", CORE)
@@ -176,7 +182,7 @@
         final_kernel,
         [(16, 256), (16, 32)],
         [pltpu.VMEM((IN, IN), f32)] * 3,
-        limit=48 << 20,
+        limit=24 << 20,
     )(mine, other, rows, weight)
     return (new_momentum, new_weight, residual)
 

time: 113 us -> 105 us (0.929)
  Pallas kernels: 12.1 us -> 6 us
  blocking collectives: 74.6 us -> 72.6 us
    all_to_all x5, blocking collectives: 74.6 us -> 72.6 us  [exchange(): lax.all_to_all(value, axis, 0, 0, tiled=True, axis_index_groups=groups)]
    pallas_call x2 -> x3, Pallas kernels: 2.19 us -> 0.46 us  [the longest x1 0.41 us: per_device(): call(gram_kernel, [(640, 128), (2, 256, 256)], limit=8 << 20)(mine, other)]
    pallas_call x1, Pallas kernels: 1.74 us -> 0.04 us  [per_device(): call(tensor_sum_kernel, [(16, 40, 128)])]
    pallas_call x1, Pallas kernels: 1.68 us -> 0.03 us  [per_device(): call(near_sum_kernel, [chunks])(exchange(parts, 'dp', NEAR), momentum)]
where the time goes in v2:
time: 105 us; the launch traced here: 104 us
  blocking collectives  72.6 us (69%)
  starting transfers between devices  20.3 us (19%)
  Pallas kernels  6 us (6%)
  waiting for transfers between devices  3.51 us (3%)
    all_to_all x5, blocking collectives, exchange(): lax.all_to_all(value, axis, 0, 0, tiled=True, axis_index_groups=groups)  72.6 us
    ppermute x2, starting transfers between devices, per_device(): other = lax.ppermute(mine, 'dp', CORE)  11.6 us
    ppermute x1, starting transfers between devices, per_device(): lax.ppermute(send, 'dp', CORE)  8.79 us
    pallas_call x1, Pallas kernels, per_device(): call(final_kernel, [(16, 256), (16, 32)], [pltpu.VMEM((IN, IN), f32)] * 3...  4.83 us
    ppermute x2, waiting for transfers between devices, per_device(): other = lax.ppermute(mine, 'dp', CORE)  2.37 us
  transfers between devices with their start and end apart: 3, of which 3 were waited for; matrix products, arithmetic and copies ran while one was open for 0% of the time, Pallas kernels for 0%

profile of v2, /device:TPU:1, one launch (start us, length us, event | category | flops | bytes accessed | tf_op | source)
XLA Modules:
  0.0 104.1 jit_solution(2400148082140404990)
XLA Ops:
  0.6 0.0 copy-start
  0.6 0.9 copy-done
  1.6 8.8 %collective-permute-start = (f32[4,4,16,256]{3,2,1,0:T(8,128)S(1)}, f32[4,4,16,256]{3,2,1,0:T(8,128)S(1)}, u32[]{:S(2)}, u32[]{:S(2)}) collective-permute-start(f32[4,4,16,256]{3,2,1,0:T(8,128)S(1)} %shard_map.58), channel_id=1, source_target_pairs={{0,16},{16,0},{32,48},{48,32},{64,80},{80,64},{96,112},{112,96},{1... | collective-permute-start | bytes 786440 | tf_op jit(solution)/shard_map/ppermute | solution.py:172
  10.4 1.1 %collective-permute-done.got_ref = f32[4,4,16,256]{3,2,1,0:T(8,128)S(1)} collective-permute-done((f32[4,4,16,256]{3,2,1,0:T(8,128)S(1)}, f32[4,4,16,256]{3,2,1,0:T(8,128)S(1)}, u32[]{:S(2)}, u32[]{:S(2)}) %collective-permute-start) | collective-permute-done | bytes 262176 | tf_op jit(solution)/shard_map/ppermute | solution.py:172
  11.6 0.0 copy-start.2
  11.6 10.7 %all_to_all.25.parts_ref = f32[4,4,16,256]{3,2,1,0:T(8,128)S(1)} all-to-all(f32[4,4,16,256]{3,2,1,0:T(8,128)S(1)} %shard_map.59), channel_id=1, replica_groups={{0,32,64,96},{16,48,80,112},{128,160,192,224},{144,176,208,240},{256,28..., dimensions={0} | all-to-all | bytes 524288 | tf_op jit(solution)/shard_map/all_to_all | solution.py:165
  22.2 0.0 copy-done.2
  22.3 23.3 %all_to_all.26.parts_ref = f32[4,4,16,256]{3,2,1,0:T(8,128)S(1)} all-to-all(f32[4,4,16,256]{3,2,1,0:T(8,128)S(1)} %shard_map.60), channel_id=1, replica_groups={{0,128,256,384},{16,144,272,400},{32,160,288,416},{48,176,304,432},{64,..., dimensions={0} | all-to-all | bytes 524288 | tf_op jit(solution)/shard_map/all_to_all | solution.py:165
  45.5 0.6 shard_map.61
  46.2 12.6 %all_to_all.27 = f32[4,4,16,256]{3,2,1,0:T(8,128)S(1)} all-to-all(f32[4,4,16,256]{3,2,1,0:T(8,128)S(1)} %get-tuple-element.10), channel_id=1, replica_groups={{0,32,64,96},{16,48,80,112},{128,160,192,224},{144,176,208,240},{256,28..., dimensions={0} | all-to-all | bytes 524288 | tf_op jit(solution)/shard_map/all_to_all | solution.py:165
  58.7 7.0 %collective-permute-start.1 = (f32[256,256]{1,0:T(8,128)S(1)}, f32[256,256]{1,0:T(8,128)S(1)}, u32[]{:S(2)}, u32[]{:S(2)}) collective-permute-start(f32[256,256]{1,0:T(8,128)S(1)} %bitcast.8), channel_id=1, source_target_pairs={{0,16},{16,0},{32,48},{48,32},{64,80},{80,64},{96,112},{112,96},{1... | collective-permute-start | bytes 786440 | tf_op jit(solution)/shard_map/ppermute | solution.py:176
  65.7 1.1 %collective-permute-done.1.other_ref = f32[256,256]{1,0:T(8,128)S(1)} collective-permute-done((f32[256,256]{1,0:T(8,128)S(1)}, f32[256,256]{1,0:T(8,128)S(1)}, u32[]{:S(2)}, u32[]{:S(2)}) %collective-permute-start.1) | collective-permute-done | bytes 262176 | tf_op jit(solution)/shard_map/ppermute | solution.py:176
  66.8 0.4 shard_map.62
  67.3 15.4 %all_to_all.28.parts_ref = f32[16,40,128]{2,1,0:T(8,128)S(1)} all-to-all(f32[16,40,128]{2,1,0:T(8,128)S(1)} %bitcast.10), channel_id=1, replica_groups=mesh['dp'=32,'tensor'=16] {'tensor'}, dimensions={0} | all-to-all | bytes 655360 | tf_op jit(solution)/shard_map/all_to_all | solution.py:165
  82.7 0.0 copy-start.1
  82.7 10.7 %all_to_all.29 = f32[16,40,128]{2,1,0:T(8,128)S(1)} all-to-all(f32[16,40,128]{2,1,0:T(8,128)S(1)} %shard_map.63), channel_id=1, replica_groups=mesh['dp'=32,'tensor'=16] {'tensor'}, dimensions={0} | all-to-all | bytes 655360 | tf_op jit(solution)/shard_map/all_to_all | solution.py:165
  93.4 4.6 %collective-permute-start.2 = (f32[640,128]{1,0:T(8,128)S(1)}, f32[640,128]{1,0:T(8,128)S(1)}, u32[]{:S(2)}, u32[]{:S(2)}) collective-permute-start(f32[640,128]{1,0:T(8,128)S(1)} %bitcast.4), channel_id=1, source_target_pairs={{0,16},{16,0},{32,48},{48,32},{64,80},{80,64},{96,112},{112,96},{1... | collective-permute-start | bytes 983048 | tf_op jit(solution)/shard_map/ppermute | solution.py:180
  98.0 1.2 %collective-permute-done.2.other_ref = f32[640,128]{1,0:T(8,128)S(1)} collective-permute-done((f32[640,128]{1,0:T(8,128)S(1)}, f32[640,128]{1,0:T(8,128)S(1)}, u32[]{:S(2)}, u32[]{:S(2)}) %collective-permute-start.2) | collective-permute-done | bytes 327712 | tf_op jit(solution)/shard_map/ppermute | solution.py:180
  99.3 0.0 copy-done.1
  99.3 4.8 %shard_map.64 = (f32[16,256]{1,0:T(8,128)}, f32[16,32]{1,0:T(8,128)}) custom-call(f32[640,128]{1,0:T(8,128)S(1)} %bitcast.5, f32[640,128]{1,0:T(8,128)S(1)} %collective-permute-done.2.other_ref, f32[2,256,256]{2,1,0:T(8,128)S(1)} %get-tuple-element.12.rows_ref, f32[16,256]{1,0:T(8,128)S(1)} %copy-done.1), custom_call_target="tpu_custom_call" | custom-call | tf_op jit(solution)/shard_map/pallas_call | solution.py:181
  (4 shorter events, 0.1 us)
Async XLA Ops:
  0.6 1.0 copy-start
  1.6 9.9 %collective-permute-start = (f32[4,4,16,256]{3,2,1,0:T(8,128)S(1)}, f32[4,4,16,256]{3,2,1,0:T(8,128)S(1)}, u32[]{:S(2)}, u32[]{:S(2)}) collective-permute-start(f32[4,4,16,256]{3,2,1,0:T(8,128)S(1)} %shard_map.58), channel_id=1, source_target_pairs={{0,16},{16,0},{32,48},{48,32},{64,80},{80,64},{96,112},{112,96},{1... | collective-permute-start | bytes 786440 | tf_op jit(solution)/shard_map/ppermute | solution.py:172
  11.6 10.7 %copy-start.2 = (f32[16,256]{1,0:T(8,128)S(1)}, f32[16,256]{1,0:T(8,128)}, u32[]{:S(2)}) copy-start(f32[16,256]{1,0:T(8,128)} %momentum_ref.1) | copy-start | bytes 49156
  58.7 8.1 %collective-permute-start.1 = (f32[256,256]{1,0:T(8,128)S(1)}, f32[256,256]{1,0:T(8,128)S(1)}, u32[]{:S(2)}, u32[]{:S(2)}) collective-permute-start(f32[256,256]{1,0:T(8,128)S(1)} %bitcast.8), channel_id=1, source_target_pairs={{0,16},{16,0},{32,48},{48,32},{64,80},{80,64},{96,112},{112,96},{1... | collective-permute-start | bytes 786440 | tf_op jit(solution)/shard_map/ppermute | solution.py:176
  82.7 16.6 %copy-start.1 = (f32[16,256]{1,0:T(8,128)S(1)}, f32[16,256]{1,0:T(8,128)}, u32[]{:S(2)}) copy-start(f32[16,256]{1,0:T(8,128)} %weight_ref.1) | copy-start | bytes 49156
  93.4 5.8 %collective-permute-start.2 = (f32[640,128]{1,0:T(8,128)S(1)}, f32[640,128]{1,0:T(8,128)S(1)}, u32[]{:S(2)}, u32[]{:S(2)}) collective-permute-start(f32[640,128]{1,0:T(8,128)S(1)} %bitcast.4), channel_id=1, source_target_pairs={{0,16},{16,0},{32,48},{48,32},{64,80},{80,64},{96,112},{112,96},{1... | collective-permute-start | bytes 983048 | tf_op jit(solution)/shard_map/ppermute | solution.py:180

commit v3 on v2

--- a/solution.py
+++ b/solution.py
@@ -20,8 +20,7 @@
 bf16 = jnp.bfloat16
 
 CORE = [(i, i ^ 1) for i in range(32)]
-NEAR = [[8 * far + 2 * near + core for near in range(4)] for far in range(4) for core in range(2)]
-FAR = [[8 * far + 2 * near + core for far in range(4)] for near in range(4) for core in range(2)]
+CHIPS = [[2 * chip + core for chip in range(16)] for core in range(2)]
 
 NT = (((1,), (1,)), ((), ()))
 NN = (((1,), (0,)), ((), ()))
@@ -29,7 +28,7 @@
 
 def place():
     index = lax.axis_index("dp")
-    return index // 8, (index // 2) % 4, index % 2
+    return index // 2, index % 2
 
 
 def halves(value):
@@ -44,39 +43,29 @@
 
 
 def send_kernel(grad_ref, send_ref):
-    _, _, core = place()
-    for far in range(4):
-        for near in range(4):
-            send_ref[near, far] = grad_ref[far, near, 1 - core].astype(f32)
+    _, core = place()
+    for chip in range(16):
+        send_ref[chip] = grad_ref[chip, 1 - core].astype(f32)
 
 
 def core_sum_kernel(grad_ref, got_ref, out_ref):
-    _, _, core = place()
-    for far in range(4):
-        for near in range(4):
-            out_ref[near, far] = grad_ref[far, near, core].astype(f32) + got_ref[near, far]
+    _, core = place()
+    for chip in range(16):
+        out_ref[chip] = grad_ref[chip, core].astype(f32) + got_ref[chip]
 
 
-def near_sum_kernel(parts_ref, momentum_ref, out_ref):
-    mine, _, _ = place()
-    for far in range(4):
-        total = (parts_ref[0, far] + parts_ref[1, far]) + (parts_ref[2, far] + parts_ref[3, far])
-        total = total + jnp.where(mine == far, f32(decay_rate), f32(0.0)) * momentum_ref[...]
-        for other in range(4):
-            out_ref[other, far] = total
-
-
-def far_sum_kernel(parts_ref, out_ref, momentum_ref):
-    mine, _, _ = place()
-    for far in range(4):
-        total = (parts_ref[0, far] + parts_ref[1, far]) + (parts_ref[2, far] + parts_ref[3, far])
-        for other in range(4):
-            out_ref[other, far] = total
-    momentum_ref[...] = out_ref[0, mine]
+def chip_sum_kernel(parts_ref, momentum_ref, out_ref, new_momentum_ref):
+    total = parts_ref[0]
+    for chip in range(1, 16):
+        total = total + parts_ref[chip]
+    total = decay_rate * momentum_ref[...] + total
+    new_momentum_ref[...] = total
+    for chip in range(16):
+        out_ref[chip] = total
 
 
 def gram_kernel(mine_ref, other_ref, out_ref, rows_ref):
-    _, _, core = place()
+    _, core = place()
     rows_ref[core] = mine_ref[...]
     rows_ref[1 - core] = other_ref[...]
     own = halves(mine_ref[...])
@@ -105,7 +94,7 @@
 
 
 def final_kernel(mine_ref, other_ref, rows_ref, weight_ref, new_weight_ref, residual_ref, gram_ref, first_ref, next_ref):
-    far, near, core = place()
+    chip, core = place()
     tensor = lax.axis_index("tensor")
     for which in range(2):
         pick = core == which
@@ -133,9 +122,7 @@
     after = mul3(first_pair, halves(inner), NN)
     next_ref[...] = after
     after_pair = halves(after)
-    mine = core * 256 + near * 64 + far * 16
-    column_base = lax.rem(tensor, 4) * 64 + lax.div(tensor, 4) * 16
-    starts = (mine, column_base, 256 + column_base)
+    starts = (core * 256 + chip * 16, tensor * 16, 256 + tensor * 16)
     bands = [next_ref[pl.ds(pl.multiple_of(start, 16), 16)] for start in starts]
     slab = jnp.concatenate(bands, axis=0)
     units = jnp.concatenate([diagonal(start, 0, (16, IN)) for start in starts], axis=0)
@@ -148,7 +135,7 @@
     new_weight_ref[...] = weight_ref[...] * (1.0 - learn_rate * weight_decay) - scale * update
     product = mul3(own, after_pair, NN)
     final = mul3(halves(product), halves(second[16:48]), NT)
-    identity = diagonal((far * 8 + near * 2 + core) * 16, tensor * 32, (16, 32))
+    identity = diagonal((chip * 2 + core) * 16, tensor * 32, (16, 32))
     residual_ref[...] = final - jnp.where(identity, f32(1.0), f32(0.0))
 
 
@@ -166,13 +153,12 @@
 
 
 def per_device(gradients, momentum, weight):
-    chunks = (4, 4, 16, 256)
-    gradients = gradients.reshape(4, 4, 2, 16, 256)
+    chunks = (16, 16, 256)
+    gradients = gradients.reshape(16, 2, 16, 256)
     (send,) = call(send_kernel, [chunks])(gradients)
     (parts,) = call(core_sum_kernel, [chunks])(gradients, lax.ppermute(send, "dp", CORE))
-    (spread,) = call(near_sum_kernel, [chunks])(exchange(parts, "dp", NEAR), momentum)
-    spread, new_momentum = call(far_sum_kernel, [chunks, (16, 256)])(exchange(spread, "dp", FAR))
-    mine = exchange(spread, "dp", NEAR).reshape(256, 256)
+    spread, new_momentum = call(chip_sum_kernel, [chunks, (16, 256)])(exchange(parts, "dp", CHIPS), momentum)
+    mine = exchange(spread, "dp", CHIPS).reshape(256, 256)
     other = lax.ppermute(mine, "dp", CORE)
     blocks, rows = call(gram_kernel, [(640, 128), (2, 256, 256)], limit=8 << 20)(mine, other)
     (spread,) = call(tensor_sum_kernel, [(16, 40, 128)])(exchange(blocks.reshape(16, 40, 128), "tensor"))

time: 105 us -> 106 us (level)
    all_to_all x5 -> x4, blocking collectives: 72.6 us -> 72.9 us  [exchange(): lax.all_to_all(value, axis, 0, 0, tiled=True, axis_index_groups=groups)]
where the time goes in v3:
time: 106 us; the launch traced here: 105 us
  blocking collectives  72.9 us (69%)
  starting transfers between devices  21 us (20%)
  Pallas kernels  5.98 us (6%)
  waiting for transfers between devices  3.51 us (3%)
    all_to_all x4, blocking collectives, exchange(): lax.all_to_all(value, axis, 0, 0, tiled=True, axis_index_groups=groups)  72.9 us
    ppermute x2, starting transfers between devices, per_device(): other = lax.ppermute(mine, 'dp', CORE)  12.2 us
    ppermute x1, starting transfers between devices, per_device(): lax.ppermute(send, 'dp', CORE)  8.79 us
    pallas_call x1, Pallas kernels, per_device(): call(final_kernel, [(16, 256), (16, 32)], [pltpu.VMEM((IN, IN), f32)] * 3...  4.83 us
    ppermute x2, waiting for transfers between devices, per_device(): other = lax.ppermute(mine, 'dp', CORE)  2.37 us
  transfers between devices with their start and end apart: 3, of which 3 were waited for; matrix products, arithmetic and copies ran while one was open for 0% of the time, Pallas kernels for 0%

profile of v3, /device:TPU:1, one launch (start us, length us, event | category | flops | bytes accessed | tf_op | source)
XLA Modules:
  0.0 105.1 jit_solution(11476473456269686178)
XLA Ops:
  0.6 0.0 copy-start
  0.6 0.9 copy-done
  1.6 8.8 %collective-permute-start = (f32[16,16,256]{2,1,0:T(8,128)S(1)}, f32[16,16,256]{2,1,0:T(8,128)S(1)}, u32[]{:S(2)}, u32[]{:S(2)}) collective-permute-start(f32[16,16,256]{2,1,0:T(8,128)S(1)} %shard_map.58), channel_id=1, source_target_pairs={{0,16},{16,0},{32,48},{48,32},{64,80},{80,64},{96,112},{112,96},{1... | collective-permute-start | bytes 786440 | tf_op jit(solution)/shard_map/ppermute | solution.py:159
  10.4 1.1 %collective-permute-done.got_ref = f32[16,16,256]{2,1,0:T(8,128)S(1)} collective-permute-done((f32[16,16,256]{2,1,0:T(8,128)S(1)}, f32[16,16,256]{2,1,0:T(8,128)S(1)}, u32[]{:S(2)}, u32[]{:S(2)}) %collective-permute-start) | collective-permute-done | bytes 262176 | tf_op jit(solution)/shard_map/ppermute | solution.py:159
  11.6 0.0 copy-start.2
  11.6 23.4 %all_to_all.20.parts_ref = f32[16,16,256]{2,1,0:T(8,128)S(1)} all-to-all(f32[16,16,256]{2,1,0:T(8,128)S(1)} %shard_map.59), channel_id=1, replica_groups={{0,32,64,96,128,160,192,224,256,288,320,352,384,416,448,480},{16,48,80,..., dimensions={0} | all-to-all | bytes 524288 | tf_op jit(solution)/shard_map/all_to_all | solution.py:152
  34.9 0.0 copy-done.2
  34.9 0.7 shard_map.60
  35.6 23.4 %all_to_all.21 = f32[16,16,256]{2,1,0:T(8,128)S(1)} all-to-all(f32[16,16,256]{2,1,0:T(8,128)S(1)} %get-tuple-element.10), channel_id=1, replica_groups={{0,32,64,96,128,160,192,224,256,288,320,352,384,416,448,480},{16,48,80,..., dimensions={0} | all-to-all | bytes 524288 | tf_op jit(solution)/shard_map/all_to_all | solution.py:152
  59.0 7.6 %collective-permute-start.1 = (f32[256,256]{1,0:T(8,128)S(1)}, f32[256,256]{1,0:T(8,128)S(1)}, u32[]{:S(2)}, u32[]{:S(2)}) collective-permute-start(f32[256,256]{1,0:T(8,128)S(1)} %bitcast.8), channel_id=1, source_target_pairs={{0,16},{16,0},{32,48},{48,32},{64,80},{80,64},{96,112},{112,96},{1... | collective-permute-start | bytes 786440 | tf_op jit(solution)/shard_map/ppermute | solution.py:162
  66.7 1.1 %collective-permute-done.1.other_ref = f32[256,256]{1,0:T(8,128)S(1)} collective-permute-done((f32[256,256]{1,0:T(8,128)S(1)}, f32[256,256]{1,0:T(8,128)S(1)}, u32[]{:S(2)}, u32[]{:S(2)}) %collective-permute-start.1) | collective-permute-done | bytes 262176 | tf_op jit(solution)/shard_map/ppermute | solution.py:162
  67.8 0.4 shard_map.61
  68.2 15.4 %all_to_all.22.parts_ref = f32[16,40,128]{2,1,0:T(8,128)S(1)} all-to-all(f32[16,40,128]{2,1,0:T(8,128)S(1)} %bitcast.10), channel_id=1, replica_groups=mesh['dp'=32,'tensor'=16] {'tensor'}, dimensions={0} | all-to-all | bytes 655360 | tf_op jit(solution)/shard_map/all_to_all | solution.py:152
  83.7 0.0 copy-start.1
  83.7 10.7 %all_to_all.23 = f32[16,40,128]{2,1,0:T(8,128)S(1)} all-to-all(f32[16,40,128]{2,1,0:T(8,128)S(1)} %shard_map.62), channel_id=1, replica_groups=mesh['dp'=32,'tensor'=16] {'tensor'}, dimensions={0} | all-to-all | bytes 655360 | tf_op jit(solution)/shard_map/all_to_all | solution.py:152
  94.4 4.6 %collective-permute-start.2 = (f32[640,128]{1,0:T(8,128)S(1)}, f32[640,128]{1,0:T(8,128)S(1)}, u32[]{:S(2)}, u32[]{:S(2)}) collective-permute-start(f32[640,128]{1,0:T(8,128)S(1)} %bitcast.4), channel_id=1, source_target_pairs={{0,16},{16,0},{32,48},{48,32},{64,80},{80,64},{96,112},{112,96},{1... | collective-permute-start | bytes 983048 | tf_op jit(solution)/shard_map/ppermute | solution.py:166
  99.0 1.2 %collective-permute-done.2.other_ref = f32[640,128]{1,0:T(8,128)S(1)} collective-permute-done((f32[640,128]{1,0:T(8,128)S(1)}, f32[640,128]{1,0:T(8,128)S(1)}, u32[]{:S(2)}, u32[]{:S(2)}) %collective-permute-start.2) | collective-permute-done | bytes 327712 | tf_op jit(solution)/shard_map/ppermute | solution.py:166
  100.2 0.0 copy-done.1
  100.2 4.8 %shard_map.63 = (f32[16,256]{1,0:T(8,128)}, f32[16,32]{1,0:T(8,128)}) custom-call(f32[640,128]{1,0:T(8,128)S(1)} %bitcast.5, f32[640,128]{1,0:T(8,128)S(1)} %collective-permute-done.2.other_ref, f32[2,256,256]{2,1,0:T(8,128)S(1)} %get-tuple-element.12.rows_ref, f32[16,256]{1,0:T(8,128)S(1)} %copy-done.1), custom_call_target="tpu_custom_call" | custom-call | tf_op jit(solution)/shard_map/pallas_call | solution.py:167
  (3 shorter events, 0.1 us)
Async XLA Ops:
  0.6 1.0 copy-start
  1.6 9.9 %collective-permute-start = (f32[16,16,256]{2,1,0:T(8,128)S(1)}, f32[16,16,256]{2,1,0:T(8,128)S(1)}, u32[]{:S(2)}, u32[]{:S(2)}) collective-permute-start(f32[16,16,256]{2,1,0:T(8,128)S(1)} %shard_map.58), channel_id=1, source_target_pairs={{0,16},{16,0},{32,48},{48,32},{64,80},{80,64},{96,112},{112,96},{1... | collective-permute-start | bytes 786440 | tf_op jit(solution)/shard_map/ppermute | solution.py:159
  11.6 23.4 %copy-start.2 = (f32[16,256]{1,0:T(8,128)S(1)}, f32[16,256]{1,0:T(8,128)}, u32[]{:S(2)}) copy-start(f32[16,256]{1,0:T(8,128)} %momentum_ref.1) | copy-start | bytes 49156
  59.0 8.8 %collective-permute-start.1 = (f32[256,256]{1,0:T(8,128)S(1)}, f32[256,256]{1,0:T(8,128)S(1)}, u32[]{:S(2)}, u32[]{:S(2)}) collective-permute-start(f32[256,256]{1,0:T(8,128)S(1)} %bitcast.8), channel_id=1, source_target_pairs={{0,16},{16,0},{32,48},{48,32},{64,80},{80,64},{96,112},{112,96},{1... | collective-permute-start | bytes 786440 | tf_op jit(solution)/shard_map/ppermute | solution.py:162
  83.7 16.6 %copy-start.1 = (f32[16,256]{1,0:T(8,128)S(1)}, f32[16,256]{1,0:T(8,128)}, u32[]{:S(2)}) copy-start(f32[16,256]{1,0:T(8,128)} %weight_ref.1) | copy-start | bytes 49156
  94.4 5.8 %collective-permute-start.2 = (f32[640,128]{1,0:T(8,128)S(1)}, f32[640,128]{1,0:T(8,128)S(1)}, u32[]{:S(2)}, u32[]{:S(2)}) collective-permute-start(f32[640,128]{1,0:T(8,128)S(1)} %bitcast.4), channel_id=1, source_target_pairs={{0,16},{16,0},{32,48},{48,32},{64,80},{80,64},{96,112},{112,96},{1... | collective-permute-start | bytes 983048 | tf_op jit(solution)/shard_map/ppermute | solution.py:166

commit v4 on v2

--- a/solution.py
+++ b/solution.py
@@ -19,9 +19,18 @@
 f32 = jnp.float32
 bf16 = jnp.bfloat16
 
+
+def chip_of(near, far, core):
+    return (4 * far + near + 2 * core) % 16
+
+
+def index_of(near, far, core):
+    return 2 * chip_of(near, far, core) + core
+
+
 CORE = [(i, i ^ 1) for i in range(32)]
-NEAR = [[8 * far + 2 * near + core for near in range(4)] for far in range(4) for core in range(2)]
-FAR = [[8 * far + 2 * near + core for far in range(4)] for near in range(4) for core in range(2)]
+NEAR = [[index_of(near, far, core) for near in range(4)] for far in range(4) for core in range(2)]
+FAR = [[index_of(near, far, core) for far in range(4)] for near in range(4) for core in range(2)]
 
 NT = (((1,), (1,)), ((), ()))
 NN = (((1,), (0,)), ((), ()))
@@ -29,7 +38,9 @@
 
 def place():
     index = lax.axis_index("dp")
-    return index // 8, (index // 2) % 4, index % 2
+    core = lax.rem(index, 2)
+    spot = lax.rem(lax.div(index, 2) + 16 - 2 * core, 16)
+    return lax.rem(spot, 4), lax.div(spot, 4), core
 
 
 def halves(value):
@@ -45,20 +56,22 @@
 
 def send_kernel(grad_ref, send_ref):
     _, _, core = place()
-    for far in range(4):
-        for near in range(4):
-            send_ref[near, far] = grad_ref[far, near, 1 - core].astype(f32)
+    other = 1 - core
+    for near in range(4):
+        for far in range(4):
+            send_ref[near, far] = grad_ref[lax.rem(4 * far + near + 2 * other, 16), other].astype(f32)
 
 
 def core_sum_kernel(grad_ref, got_ref, out_ref):
     _, _, core = place()
-    for far in range(4):
-        for near in range(4):
-            out_ref[near, far] = grad_ref[far, near, core].astype(f32) + got_ref[near, far]
+    for near in range(4):
+        for far in range(4):
+            rows = grad_ref[lax.rem(4 * far + near + 2 * core, 16), core].astype(f32)
+            out_ref[near, far] = rows + got_ref[near, far]
 
 
 def near_sum_kernel(parts_ref, momentum_ref, out_ref):
-    mine, _, _ = place()
+    _, mine, _ = place()
     for far in range(4):
         total = (parts_ref[0, far] + parts_ref[1, far]) + (parts_ref[2, far] + parts_ref[3, far])
         total = total + jnp.where(mine == far, f32(decay_rate), f32(0.0)) * momentum_ref[...]
@@ -66,13 +79,11 @@
             out_ref[other, far] = total
 
 
-def far_sum_kernel(parts_ref, out_ref, momentum_ref):
-    mine, _, _ = place()
+def far_sum_kernel(parts_ref, out_ref):
     for far in range(4):
         total = (parts_ref[0, far] + parts_ref[1, far]) + (parts_ref[2, far] + parts_ref[3, far])
         for other in range(4):
             out_ref[other, far] = total
-    momentum_ref[...] = out_ref[0, mine]
 
 
 def gram_kernel(mine_ref, other_ref, out_ref, rows_ref):
@@ -104,9 +115,11 @@
     return rows == columns
 
 
-def final_kernel(mine_ref, other_ref, rows_ref, weight_ref, new_weight_ref, residual_ref, gram_ref, first_ref, next_ref):
-    far, near, core = place()
+def final_kernel(mine_ref, other_ref, rows_ref, weight_ref, new_momentum_ref, new_weight_ref, residual_ref, gram_ref, first_ref, next_ref):
+    near, far, core = place()
     tensor = lax.axis_index("tensor")
+    spot = near * 64 + far * 16
+    new_momentum_ref[...] = rows_ref[core, pl.ds(pl.multiple_of(spot, 16), 16)]
     for which in range(2):
         pick = core == which
         block = lambda start, size: jnp.where(pick, mine_ref[start : start + size], other_ref[start : start + size])
@@ -133,9 +146,10 @@
     after = mul3(first_pair, halves(inner), NN)
     next_ref[...] = after
     after_pair = halves(after)
-    mine = core * 256 + near * 64 + far * 16
-    column_base = lax.rem(tensor, 4) * 64 + lax.div(tensor, 4) * 16
-    starts = (mine, column_base, 256 + column_base)
+    starts = [core * 256 + spot]
+    for which in range(2):
+        column = lax.rem(tensor + 16 - 2 * which, 16)
+        starts.append(256 * which + lax.rem(column, 4) * 64 + lax.div(column, 4) * 16)
     bands = [next_ref[pl.ds(pl.multiple_of(start, 16), 16)] for start in starts]
     slab = jnp.concatenate(bands, axis=0)
     units = jnp.concatenate([diagonal(start, 0, (16, IN)) for start in starts], axis=0)
@@ -148,7 +162,7 @@
     new_weight_ref[...] = weight_ref[...] * (1.0 - learn_rate * weight_decay) - scale * update
     product = mul3(own, after_pair, NN)
     final = mul3(halves(product), halves(second[16:48]), NT)
-    identity = diagonal((far * 8 + near * 2 + core) * 16, tensor * 32, (16, 32))
+    identity = diagonal(lax.axis_index("dp") * 16, tensor * 32, (16, 32))
     residual_ref[...] = final - jnp.where(identity, f32(1.0), f32(0.0))
 
 
@@ -167,24 +181,23 @@
 
 def per_device(gradients, momentum, weight):
     chunks = (4, 4, 16, 256)
-    gradients = gradients.reshape(4, 4, 2, 16, 256)
+    gradients = gradients.reshape(16, 2, 16, 256)
     (send,) = call(send_kernel, [chunks])(gradients)
     (parts,) = call(core_sum_kernel, [chunks])(gradients, lax.ppermute(send, "dp", CORE))
     (spread,) = call(near_sum_kernel, [chunks])(exchange(parts, "dp", NEAR), momentum)
-    spread, new_momentum = call(far_sum_kernel, [chunks, (16, 256)])(exchange(spread, "dp", FAR))
+    (spread,) = call(far_sum_kernel, [chunks])(exchange(spread, "dp", FAR))
     mine = exchange(spread, "dp", NEAR).reshape(256, 256)
     other = lax.ppermute(mine, "dp", CORE)
     blocks, rows = call(gram_kernel, [(640, 128), (2, 256, 256)], limit=8 << 20)(mine, other)
     (spread,) = call(tensor_sum_kernel, [(16, 40, 128)])(exchange(blocks.reshape(16, 40, 128), "tensor"))
     mine = exchange(spread, "tensor").reshape(640, 128)
     other = lax.ppermute(mine, "dp", CORE)
-    new_weight, residual = call(
+    return call(
         final_kernel,
-        [(16, 256), (16, 32)],
+        [(16, 256), (16, 256), (16, 32)],
         [pltpu.VMEM((IN, IN), f32)] * 3,
         limit=24 << 20,
     )(mine, other, rows, weight)
-    return (new_momentum, new_weight, residual)
 
 
 def solution(mesh):

time: 105 us -> 105 us (level)
  starting transfers between devices: 20.3 us -> 22.9 us
  blocking collectives: 72.6 us -> 71 us
    ppermute x2, starting transfers between devices: 11.6 us -> 14.1 us  [per_device(): other = lax.ppermute(mine, 'dp', CORE)]
    all_to_all x5, blocking collectives: 72.6 us -> 71 us  [exchange(): lax.all_to_all(value, axis, 0, 0, tiled=True, axis_index_groups=groups)]
where the time goes in v4:
time: 105 us
  blocking collectives  71 us (68%)
  starting transfers between devices  22.9 us (22%)
  Pallas kernels  5.41 us (5%)
  waiting for transfers between devices  3.51 us (3%)
    all_to_all x5, blocking collectives, exchange(): lax.all_to_all(value, axis, 0, 0, tiled=True, axis_index_groups=groups)  71 us
    ppermute x2, starting transfers between devices, per_device(): other = lax.ppermute(mine, 'dp', CORE)  14.1 us
    ppermute x1, starting transfers between devices, per_device(): lax.ppermute(send, 'dp', CORE)  8.79 us
    pallas_call x1, Pallas kernels, per_device(): call(final_kernel, [(16, 256), (16, 256), (16, 32)], [pltpu.VMEM((IN, IN)...  4.83 us
    ppermute x2, waiting for transfers between devices, per_device(): other = lax.ppermute(mine, 'dp', CORE)  2.37 us
  transfers between devices with their start and end apart: 3, of which 3 were waited for; matrix products, arithmetic and copies ran while one was open for 0% of the time, Pallas kernels for 0%

profile of v4, /device:TPU:1, one launch (start us, length us, event | category | flops | bytes accessed | tf_op | source)
XLA Modules:
  0.0 104.5 jit_solution(6124664468722610250)
XLA Ops:
  0.6 0.0 copy-start
  0.6 0.9 copy-done
  1.6 8.8 %collective-permute-start = (f32[4,4,16,256]{3,2,1,0:T(8,128)S(1)}, f32[4,4,16,256]{3,2,1,0:T(8,128)S(1)}, u32[]{:S(2)}, u32[]{:S(2)}) collective-permute-start(f32[4,4,16,256]{3,2,1,0:T(8,128)S(1)} %shard_map.58), channel_id=1, source_target_pairs={{0,16},{16,0},{32,48},{48,32},{64,80},{80,64},{96,112},{112,96},{1... | collective-permute-start | bytes 786440 | tf_op jit(solution)/shard_map/ppermute | solution.py:186
  10.4 1.1 %collective-permute-done.got_ref = f32[4,4,16,256]{3,2,1,0:T(8,128)S(1)} collective-permute-done((f32[4,4,16,256]{3,2,1,0:T(8,128)S(1)}, f32[4,4,16,256]{3,2,1,0:T(8,128)S(1)}, u32[]{:S(2)}, u32[]{:S(2)}) %collective-permute-start) | collective-permute-done | bytes 262176 | tf_op jit(solution)/shard_map/ppermute | solution.py:186
  11.6 0.0 copy-start.2
  11.6 11.0 %all_to_all.25.parts_ref = f32[4,4,16,256]{3,2,1,0:T(8,128)S(1)} all-to-all(f32[4,4,16,256]{3,2,1,0:T(8,128)S(1)} %shard_map.59), channel_id=1, replica_groups={{0,32,64,96},{80,112,144,176},{128,160,192,224},{208,240,272,304},{256,..., dimensions={0} | all-to-all | bytes 524288 | tf_op jit(solution)/shard_map/all_to_all | solution.py:179
  22.6 0.0 copy-done.2
  22.6 23.8 %all_to_all.26.parts_ref = f32[4,4,16,256]{3,2,1,0:T(8,128)S(1)} all-to-all(f32[4,4,16,256]{3,2,1,0:T(8,128)S(1)} %shard_map.60), channel_id=1, replica_groups={{0,128,256,384},{80,208,336,464},{32,160,288,416},{112,240,368,496},{64..., dimensions={0} | all-to-all | bytes 524288 | tf_op jit(solution)/shard_map/all_to_all | solution.py:179
  46.4 10.1 %all_to_all.27 = f32[4,4,16,256]{3,2,1,0:T(8,128)S(1)} all-to-all(f32[4,4,16,256]{3,2,1,0:T(8,128)S(1)} %shard_map.61), channel_id=1, replica_groups={{0,32,64,96},{80,112,144,176},{128,160,192,224},{208,240,272,304},{256,..., dimensions={0} | all-to-all | bytes 524288 | tf_op jit(solution)/shard_map/all_to_all | solution.py:179
  56.6 9.6 %collective-permute-start.1 = (f32[256,256]{1,0:T(8,128)S(1)}, f32[256,256]{1,0:T(8,128)S(1)}, u32[]{:S(2)}, u32[]{:S(2)}) collective-permute-start(f32[256,256]{1,0:T(8,128)S(1)} %bitcast.8), channel_id=1, source_target_pairs={{0,16},{16,0},{32,48},{48,32},{64,80},{80,64},{96,112},{112,96},{1... | collective-permute-start | bytes 786440 | tf_op jit(solution)/shard_map/ppermute | solution.py:190
  66.1 1.1 %collective-permute-done.1.other_ref = f32[256,256]{1,0:T(8,128)S(1)} collective-permute-done((f32[256,256]{1,0:T(8,128)S(1)}, f32[256,256]{1,0:T(8,128)S(1)}, u32[]{:S(2)}, u32[]{:S(2)}) %collective-permute-start.1) | collective-permute-done | bytes 262176 | tf_op jit(solution)/shard_map/ppermute | solution.py:190
  67.3 0.4 shard_map.62
  67.7 15.4 %all_to_all.28.parts_ref = f32[16,40,128]{2,1,0:T(8,128)S(1)} all-to-all(f32[16,40,128]{2,1,0:T(8,128)S(1)} %bitcast.10), channel_id=1, replica_groups=mesh['dp'=32,'tensor'=16] {'tensor'}, dimensions={0} | all-to-all | bytes 655360 | tf_op jit(solution)/shard_map/all_to_all | solution.py:179
  83.1 0.0 copy-start.1
  83.1 10.7 %all_to_all.29 = f32[16,40,128]{2,1,0:T(8,128)S(1)} all-to-all(f32[16,40,128]{2,1,0:T(8,128)S(1)} %shard_map.63), channel_id=1, replica_groups=mesh['dp'=32,'tensor'=16] {'tensor'}, dimensions={0} | all-to-all | bytes 655360 | tf_op jit(solution)/shard_map/all_to_all | solution.py:179
  93.8 4.6 %collective-permute-start.2 = (f32[640,128]{1,0:T(8,128)S(1)}, f32[640,128]{1,0:T(8,128)S(1)}, u32[]{:S(2)}, u32[]{:S(2)}) collective-permute-start(f32[640,128]{1,0:T(8,128)S(1)} %bitcast.4), channel_id=1, source_target_pairs={{0,16},{16,0},{32,48},{48,32},{64,80},{80,64},{96,112},{112,96},{1... | collective-permute-start | bytes 983048 | tf_op jit(solution)/shard_map/ppermute | solution.py:194
  98.4 1.2 %collective-permute-done.2.other_ref = f32[640,128]{1,0:T(8,128)S(1)} collective-permute-done((f32[640,128]{1,0:T(8,128)S(1)}, f32[640,128]{1,0:T(8,128)S(1)}, u32[]{:S(2)}, u32[]{:S(2)}) %collective-permute-start.2) | collective-permute-done | bytes 327712 | tf_op jit(solution)/shard_map/ppermute | solution.py:194
  99.7 0.0 copy-done.1
  99.7 4.8 %shard_map.64 = (f32[16,256]{1,0:T(8,128)}, f32[16,256]{1,0:T(8,128)}, f32[16,32]{1,0:T(8,128)}) custom-call(f32[640,128]{1,0:T(8,128)S(1)} %bitcast.5, f32[640,128]{1,0:T(8,128)S(1)} %collective-permute-done.2.other_ref, f32[2,256,256]{2,1,0:T(8,128)S(1)} %get-tuple-element.6.rows_ref, f32[16,256]{1,0:T(8,128)S(1)} %copy-done.1), custom_call_target="tpu_custom_call" | custom-call | tf_op jit(solution)/shard_map/pallas_call | solution.py:195
  (5 shorter events, 0.2 us)
Async XLA Ops:
  0.6 1.0 copy-start
  1.6 9.9 %collective-permute-start = (f32[4,4,16,256]{3,2,1,0:T(8,128)S(1)}, f32[4,4,16,256]{3,2,1,0:T(8,128)S(1)}, u32[]{:S(2)}, u32[]{:S(2)}) collective-permute-start(f32[4,4,16,256]{3,2,1,0:T(8,128)S(1)} %shard_map.58), channel_id=1, source_target_pairs={{0,16},{16,0},{32,48},{48,32},{64,80},{80,64},{96,112},{112,96},{1... | collective-permute-start | bytes 786440 | tf_op jit(solution)/shard_map/ppermute | solution.py:186
  11.6 11.0 %copy-start.2 = (f32[16,256]{1,0:T(8,128)S(1)}, f32[16,256]{1,0:T(8,128)}, u32[]{:S(2)}) copy-start(f32[16,256]{1,0:T(8,128)} %momentum_ref.1) | copy-start | bytes 49156
  56.6 10.7 %collective-permute-start.1 = (f32[256,256]{1,0:T(8,128)S(1)}, f32[256,256]{1,0:T(8,128)S(1)}, u32[]{:S(2)}, u32[]{:S(2)}) collective-permute-start(f32[256,256]{1,0:T(8,128)S(1)} %bitcast.8), channel_id=1, source_target_pairs={{0,16},{16,0},{32,48},{48,32},{64,80},{80,64},{96,112},{112,96},{1... | collective-permute-start | bytes 786440 | tf_op jit(solution)/shard_map/ppermute | solution.py:190
  83.1 16.6 %copy-start.1 = (f32[16,256]{1,0:T(8,128)S(1)}, f32[16,256]{1,0:T(8,128)}, u32[]{:S(2)}) copy-start(f32[16,256]{1,0:T(8,128)} %weight_ref.1) | copy-start | bytes 49156
  93.8 5.8 %collective-permute-start.2 = (f32[640,128]{1,0:T(8,128)S(1)}, f32[640,128]{1,0:T(8,128)S(1)}, u32[]{:S(2)}, u32[]{:S(2)}) collective-permute-start(f32[640,128]{1,0:T(8,128)S(1)} %bitcast.4), channel_id=1, source_target_pairs={{0,16},{16,0},{32,48},{48,32},{64,80},{80,64},{96,112},{112,96},{1... | collective-permute-start | bytes 983048 | tf_op jit(solution)/shard_map/ppermute | solution.py:194

commit v5 on v4

--- a/solution.py
+++ b/solution.py
@@ -19,18 +19,9 @@
 f32 = jnp.float32
 bf16 = jnp.bfloat16
 
-
-def chip_of(near, far, core):
-    return (4 * far + near + 2 * core) % 16
-
-
-def index_of(near, far, core):
-    return 2 * chip_of(near, far, core) + core
-
-
 CORE = [(i, i ^ 1) for i in range(32)]
-NEAR = [[index_of(near, far, core) for near in range(4)] for far in range(4) for core in range(2)]
-FAR = [[index_of(near, far, core) for far in range(4)] for near in range(4) for core in range(2)]
+NEAR = [[8 * far + 2 * near + core for near in range(4)] for far in range(4) for core in range(2)]
+FAR = [[(i, i ^ (8 * step)) for i in range(32)] for step in (1, 2, 3)]
 
 NT = (((1,), (1,)), ((), ()))
 NN = (((1,), (0,)), ((), ()))
@@ -38,9 +29,7 @@
 
 def place():
     index = lax.axis_index("dp")
-    core = lax.rem(index, 2)
-    spot = lax.rem(lax.div(index, 2) + 16 - 2 * core, 16)
-    return lax.rem(spot, 4), lax.div(spot, 4), core
+    return lax.rem(lax.div(index, 2), 4), lax.div(index, 8), lax.rem(index, 2)
 
 
 def halves(value):
@@ -56,32 +45,28 @@
 
 def send_kernel(grad_ref, send_ref):
     _, _, core = place()
-    other = 1 - core
     for near in range(4):
         for far in range(4):
-            send_ref[near, far] = grad_ref[lax.rem(4 * far + near + 2 * other, 16), other].astype(f32)
+            send_ref[near, far] = grad_ref[far, near, 1 - core].astype(f32)
 
 
 def core_sum_kernel(grad_ref, got_ref, out_ref):
     _, _, core = place()
     for near in range(4):
         for far in range(4):
-            rows = grad_ref[lax.rem(4 * far + near + 2 * core, 16), core].astype(f32)
-            out_ref[near, far] = rows + got_ref[near, far]
+            out_ref[near, far] = grad_ref[far, near, core].astype(f32) + got_ref[near, far]
 
 
 def near_sum_kernel(parts_ref, momentum_ref, out_ref):
     _, mine, _ = place()
     for far in range(4):
         total = (parts_ref[0, far] + parts_ref[1, far]) + (parts_ref[2, far] + parts_ref[3, far])
-        total = total + jnp.where(mine == far, f32(decay_rate), f32(0.0)) * momentum_ref[...]
-        for other in range(4):
-            out_ref[other, far] = total
+        out_ref[far] = total + jnp.where(mine == far, f32(decay_rate), f32(0.0)) * momentum_ref[...]
 
 
-def far_sum_kernel(parts_ref, out_ref):
+def far_sum_kernel(own_ref, first_ref, second_ref, third_ref, out_ref):
     for far in range(4):
-        total = (parts_ref[0, far] + parts_ref[1, far]) + (parts_ref[2, far] + parts_ref[3, far])
+        total = (own_ref[far] + first_ref[far]) + (second_ref[far] + third_ref[far])
         for other in range(4):
             out_ref[other, far] = total
 
@@ -148,8 +133,7 @@
     after_pair = halves(after)
     starts = [core * 256 + spot]
     for which in range(2):
-        column = lax.rem(tensor + 16 - 2 * which, 16)
-        starts.append(256 * which + lax.rem(column, 4) * 64 + lax.div(column, 4) * 16)
+        starts.append(256 * which + lax.rem(tensor, 4) * 64 + lax.div(tensor, 4) * 16)
     bands = [next_ref[pl.ds(pl.multiple_of(start, 16), 16)] for start in starts]
     slab = jnp.concatenate(bands, axis=0)
     units = jnp.concatenate([diagonal(start, 0, (16, IN)) for start in starts], axis=0)
@@ -181,11 +165,12 @@
 
 def per_device(gradients, momentum, weight):
     chunks = (4, 4, 16, 256)
-    gradients = gradients.reshape(16, 2, 16, 256)
+    gradients = gradients.reshape(4, 4, 2, 16, 256)
     (send,) = call(send_kernel, [chunks])(gradients)
     (parts,) = call(core_sum_kernel, [chunks])(gradients, lax.ppermute(send, "dp", CORE))
-    (spread,) = call(near_sum_kernel, [chunks])(exchange(parts, "dp", NEAR), momentum)
-    (spread,) = call(far_sum_kernel, [chunks])(exchange(spread, "dp", FAR))
+    (parts,) = call(near_sum_kernel, [chunks[1:]])(exchange(parts, "dp", NEAR), momentum)
+    others = [lax.ppermute(parts, "dp", pairs) for pairs in FAR]
+    (spread,) = call(far_sum_kernel, [chunks])(parts, *others)
     mine = exchange(spread, "dp", NEAR).reshape(256, 256)
     other = lax.ppermute(mine, "dp", CORE)
     blocks, rows = call(gram_kernel, [(640, 128), (2, 256, 256)], limit=8 << 20)(mine, other)

time: 105 us -> 102 us (0.971)
  blocking collectives: 71 us -> 45.7 us
  starting transfers between devices: 22.9 us -> 35.3 us
  waiting for transfers between devices: 3.51 us -> 13.3 us
    all_to_all x5 -> x4, blocking collectives: 71 us -> 45.7 us  [exchange(): lax.all_to_all(value, axis, 0, 0, tiled=True, axis_index_groups=groups)]
    ppermute x0 -> x3, starting transfers between devices: none -> 16.2 us  [per_device(): others = [lax.ppermute(parts, 'dp', pairs) for pairs in FAR]]
    ppermute x0 -> x3, waiting for transfers between devices: none -> 9.75 us  [per_device(): others = [lax.ppermute(parts, 'dp', pairs) for pairs in FAR]]
    ppermute x2, starting transfers between devices: 14.1 us -> 10.4 us  [per_device(): other = lax.ppermute(mine, 'dp', CORE)]
  transfers between devices with their start and end apart: 3 -> 6, of which waited for: 3 -> 4; matrix products, arithmetic and copies ran while one was open for 0% -> 0% of each run, Pallas kernels for 0% -> 0%
where the time goes in v5:
time: 102 us; the launch traced here: 101 us
  blocking collectives  45.7 us (45%)
  starting transfers between devices  35.3 us (35%)
  waiting for transfers between devices  13.3 us (13%)
  Pallas kernels  5.38 us (5%)
    all_to_all x4, blocking collectives, exchange(): lax.all_to_all(value, axis, 0, 0, tiled=True, axis_index_groups=groups)  45.7 us
    ppermute x3, starting transfers between devices, per_device(): others = [lax.ppermute(parts, 'dp', pairs) for pairs in FAR]  16.2 us
    ppermute x2, starting transfers between devices, per_device(): other = lax.ppermute(mine, 'dp', CORE)  10.4 us
    ppermute x3, waiting for transfers between devices, per_device(): others = [lax.ppermute(parts, 'dp', pairs) for pairs in FAR]  9.75 us
    ppermute x1, starting transfers between devices, per_device(): lax.ppermute(send, 'dp', CORE)  8.79 us
    pallas_call x1, Pallas kernels, per_device(): call(final_kernel, [(16, 256), (16, 256), (16, 32)], [pltpu.VMEM((IN, IN)...  4.84 us
    ppermute x2, waiting for transfers between devices, per_device(): other = lax.ppermute(mine, 'dp', CORE)  2.37 us
  transfers between devices with their start and end apart: 6, of which 4 were waited for; matrix products, arithmetic and copies ran while one was open for 0% of the time, Pallas kernels for 0%

profile of v5, /device:TPU:1, one launch (start us, length us, event | category | flops | bytes accessed | tf_op | source)
XLA Modules:
  0.0 101.4 jit_solution(1896784126436676214)
XLA Ops:
  0.6 0.0 copy-start
  0.6 0.9 copy-done
  1.6 8.8 %collective-permute-start = (f32[4,4,16,256]{3,2,1,0:T(8,128)S(1)}, f32[4,4,16,256]{3,2,1,0:T(8,128)S(1)}, u32[]{:S(2)}, u32[]{:S(2)}) collective-permute-start(f32[4,4,16,256]{3,2,1,0:T(8,128)S(1)} %shard_map.58), channel_id=1, source_target_pairs={{0,16},{16,0},{32,48},{48,32},{64,80},{80,64},{96,112},{112,96},{1... | collective-permute-start | bytes 786440 | tf_op jit(solution)/shard_map/ppermute | solution.py:170
  10.4 1.1 %collective-permute-done.got_ref = f32[4,4,16,256]{3,2,1,0:T(8,128)S(1)} collective-permute-done((f32[4,4,16,256]{3,2,1,0:T(8,128)S(1)}, f32[4,4,16,256]{3,2,1,0:T(8,128)S(1)}, u32[]{:S(2)}, u32[]{:S(2)}) %collective-permute-start) | collective-permute-done | bytes 262176 | tf_op jit(solution)/shard_map/ppermute | solution.py:170
  11.6 0.0 copy-start.2
  11.6 10.7 %all_to_all.20.parts_ref = f32[4,4,16,256]{3,2,1,0:T(8,128)S(1)} all-to-all(f32[4,4,16,256]{3,2,1,0:T(8,128)S(1)} %shard_map.59), channel_id=1, replica_groups={{0,32,64,96},{16,48,80,112},{128,160,192,224},{144,176,208,240},{256,28..., dimensions={0} | all-to-all | bytes 524288 | tf_op jit(solution)/shard_map/all_to_all | solution.py:163
  22.2 0.0 copy-done.2
  22.3 6.2 %collective-permute-start.3 = (f32[4,16,256]{2,1,0:T(8,128)S(1)}, f32[4,16,256]{2,1,0:T(8,128)S(1)}, u32[]{:S(2)}, u32[]{:S(2)}) collective-permute-start(f32[4,16,256]{2,1,0:T(8,128)S(1)} %shard_map.60.own_ref), channel_id=1, source_target_pairs={{0,384},{16,400},{32,416},{48,432},{64,448},{80,464},{96,480},{112... | collective-permute-start | bytes 196616 | tf_op jit(solution)/shard_map/ppermute | solution.py:172
  28.4 6.1 %collective-permute-start.2 = (f32[4,16,256]{2,1,0:T(8,128)S(1)}, f32[4,16,256]{2,1,0:T(8,128)S(1)}, u32[]{:S(2)}, u32[]{:S(2)}) collective-permute-start(f32[4,16,256]{2,1,0:T(8,128)S(1)} %shard_map.60.own_ref), channel_id=1, source_target_pairs={{0,256},{16,272},{32,288},{48,304},{64,320},{80,336},{96,352},{112... | collective-permute-start | bytes 196616 | tf_op jit(solution)/shard_map/ppermute | solution.py:172
  34.5 4.0 %collective-permute-start.1 = (f32[4,16,256]{2,1,0:T(8,128)S(1)}, f32[4,16,256]{2,1,0:T(8,128)S(1)}, u32[]{:S(2)}, u32[]{:S(2)}) collective-permute-start(f32[4,16,256]{2,1,0:T(8,128)S(1)} %shard_map.60.own_ref), channel_id=1, source_target_pairs={{0,128},{16,144},{32,160},{48,176},{64,192},{80,208},{96,224},{112... | collective-permute-start | bytes 196616 | tf_op jit(solution)/shard_map/ppermute | solution.py:172
  38.5 0.0 collective-permute-done.3.third_ref
  38.5 9.7 %collective-permute-done.2.second_ref = f32[4,16,256]{2,1,0:T(8,128)S(1)} collective-permute-done((f32[4,16,256]{2,1,0:T(8,128)S(1)}, f32[4,16,256]{2,1,0:T(8,128)S(1)}, u32[]{:S(2)}, u32[]{:S(2)}) %collective-permute-start.2) | collective-permute-done | bytes 65568 | tf_op jit(solution)/shard_map/ppermute | solution.py:172
  48.2 0.0 collective-permute-done.1.first_ref
  48.3 8.9 %all_to_all.21 = f32[4,4,16,256]{3,2,1,0:T(8,128)S(1)} all-to-all(f32[4,4,16,256]{3,2,1,0:T(8,128)S(1)} %shard_map.61), channel_id=1, replica_groups={{0,32,64,96},{16,48,80,112},{128,160,192,224},{144,176,208,240},{256,28..., dimensions={0} | all-to-all | bytes 524288 | tf_op jit(solution)/shard_map/all_to_all | solution.py:163
  57.2 5.8 %collective-permute-start.4 = (f32[256,256]{1,0:T(8,128)S(1)}, f32[256,256]{1,0:T(8,128)S(1)}, u32[]{:S(2)}, u32[]{:S(2)}) collective-permute-start(f32[256,256]{1,0:T(8,128)S(1)} %bitcast.8), channel_id=1, source_target_pairs={{0,16},{16,0},{32,48},{48,32},{64,80},{80,64},{96,112},{112,96},{1... | collective-permute-start | bytes 786440 | tf_op jit(solution)/shard_map/ppermute | solution.py:175
  63.0 1.1 %collective-permute-done.4.other_ref = f32[256,256]{1,0:T(8,128)S(1)} collective-permute-done((f32[256,256]{1,0:T(8,128)S(1)}, f32[256,256]{1,0:T(8,128)S(1)}, u32[]{:S(2)}, u32[]{:S(2)}) %collective-permute-start.4) | collective-permute-done | bytes 262176 | tf_op jit(solution)/shard_map/ppermute | solution.py:175
  64.1 0.4 shard_map.62
  64.5 15.4 %all_to_all.22.parts_ref = f32[16,40,128]{2,1,0:T(8,128)S(1)} all-to-all(f32[16,40,128]{2,1,0:T(8,128)S(1)} %bitcast.10), channel_id=1, replica_groups=mesh['dp'=32,'tensor'=16] {'tensor'}, dimensions={0} | all-to-all | bytes 655360 | tf_op jit(solution)/shard_map/all_to_all | solution.py:163
  80.0 0.0 copy-start.1
  80.0 10.7 %all_to_all.23 = f32[16,40,128]{2,1,0:T(8,128)S(1)} all-to-all(f32[16,40,128]{2,1,0:T(8,128)S(1)} %shard_map.63), channel_id=1, replica_groups=mesh['dp'=32,'tensor'=16] {'tensor'}, dimensions={0} | all-to-all | bytes 655360 | tf_op jit(solution)/shard_map/all_to_all | solution.py:163
  90.7 4.6 %collective-permute-start.5 = (f32[640,128]{1,0:T(8,128)S(1)}, f32[640,128]{1,0:T(8,128)S(1)}, u32[]{:S(2)}, u32[]{:S(2)}) collective-permute-start(f32[640,128]{1,0:T(8,128)S(1)} %bitcast.4), channel_id=1, source_target_pairs={{0,16},{16,0},{32,48},{48,32},{64,80},{80,64},{96,112},{112,96},{1... | collective-permute-start | bytes 983048 | tf_op jit(solution)/shard_map/ppermute | solution.py:179
  95.3 1.2 %collective-permute-done.5.other_ref = f32[640,128]{1,0:T(8,128)S(1)} collective-permute-done((f32[640,128]{1,0:T(8,128)S(1)}, f32[640,128]{1,0:T(8,128)S(1)}, u32[]{:S(2)}, u32[]{:S(2)}) %collective-permute-start.5) | collective-permute-done | bytes 327712 | tf_op jit(solution)/shard_map/ppermute | solution.py:179
  96.5 0.0 copy-done.1
  96.5 4.8 %shard_map.64 = (f32[16,256]{1,0:T(8,128)}, f32[16,256]{1,0:T(8,128)}, f32[16,32]{1,0:T(8,128)}) custom-call(f32[640,128]{1,0:T(8,128)S(1)} %bitcast.5, f32[640,128]{1,0:T(8,128)S(1)} %collective-permute-done.5.other_ref, f32[2,256,256]{2,1,0:T(8,128)S(1)} %get-tuple-element.6.rows_ref, f32[16,256]{1,0:T(8,128)S(1)} %copy-done.1), custom_call_target="tpu_custom_call" | custom-call | tf_op jit(solution)/shard_map/pallas_call | solution.py:180
  (5 shorter events, 0.1 us)
Async XLA Ops:
  0.6 1.0 copy-start
  1.6 9.9 %collective-permute-start = (f32[4,4,16,256]{3,2,1,0:T(8,128)S(1)}, f32[4,4,16,256]{3,2,1,0:T(8,128)S(1)}, u32[]{:S(2)}, u32[]{:S(2)}) collective-permute-start(f32[4,4,16,256]{3,2,1,0:T(8,128)S(1)} %shard_map.58), channel_id=1, source_target_pairs={{0,16},{16,0},{32,48},{48,32},{64,80},{80,64},{96,112},{112,96},{1... | collective-permute-start | bytes 786440 | tf_op jit(solution)/shard_map/ppermute | solution.py:170
  11.6 10.7 %copy-start.2 = (f32[16,256]{1,0:T(8,128)S(1)}, f32[16,256]{1,0:T(8,128)}, u32[]{:S(2)}) copy-start(f32[16,256]{1,0:T(8,128)} %momentum_ref.1) | copy-start | bytes 49156
  22.3 16.2 %collective-permute-start.3 = (f32[4,16,256]{2,1,0:T(8,128)S(1)}, f32[4,16,256]{2,1,0:T(8,128)S(1)}, u32[]{:S(2)}, u32[]{:S(2)}) collective-permute-start(f32[4,16,256]{2,1,0:T(8,128)S(1)} %shard_map.60.own_ref), channel_id=1, source_target_pairs={{0,384},{16,400},{32,416},{48,432},{64,448},{80,464},{96,480},{112... | collective-permute-start | bytes 196616 | tf_op jit(solution)/shard_map/ppermute | solution.py:172
  28.4 19.8 %collective-permute-start.2 = (f32[4,16,256]{2,1,0:T(8,128)S(1)}, f32[4,16,256]{2,1,0:T(8,128)S(1)}, u32[]{:S(2)}, u32[]{:S(2)}) collective-permute-start(f32[4,16,256]{2,1,0:T(8,128)S(1)} %shard_map.60.own_ref), channel_id=1, source_target_pairs={{0,256},{16,272},{32,288},{48,304},{64,320},{80,336},{96,352},{112... | collective-permute-start | bytes 196616 | tf_op jit(solution)/shard_map/ppermute | solution.py:172
  34.5 13.7 %collective-permute-start.1 = (f32[4,16,256]{2,1,0:T(8,128)S(1)}, f32[4,16,256]{2,1,0:T(8,128)S(1)}, u32[]{:S(2)}, u32[]{:S(2)}) collective-permute-start(f32[4,16,256]{2,1,0:T(8,128)S(1)} %shard_map.60.own_ref), channel_id=1, source_target_pairs={{0,128},{16,144},{32,160},{48,176},{64,192},{80,208},{96,224},{112... | collective-permute-start | bytes 196616 | tf_op jit(solution)/shard_map/ppermute | solution.py:172
  57.2 6.9 %collective-permute-start.4 = (f32[256,256]{1,0:T(8,128)S(1)}, f32[256,256]{1,0:T(8,128)S(1)}, u32[]{:S(2)}, u32[]{:S(2)}) collective-permute-start(f32[256,256]{1,0:T(8,128)S(1)} %bitcast.8), channel_id=1, source_target_pairs={{0,16},{16,0},{32,48},{48,32},{64,80},{80,64},{96,112},{112,96},{1... | collective-permute-start | bytes 786440 | tf_op jit(solution)/shard_map/ppermute | solution.py:175
  80.0 16.6 %copy-start.1 = (f32[16,256]{1,0:T(8,128)S(1)}, f32[16,256]{1,0:T(8,128)}, u32[]{:S(2)}) copy-start(f32[16,256]{1,0:T(8,128)} %weight_ref.1) | copy-start | bytes 49156
  90.7 5.8 %collective-permute-start.5 = (f32[640,128]{1,0:T(8,128)S(1)}, f32[640,128]{1,0:T(8,128)S(1)}, u32[]{:S(2)}, u32[]{:S(2)}) collective-permute-start(f32[640,128]{1,0:T(8,128)S(1)} %bitcast.4), channel_id=1, source_target_pairs={{0,16},{16,0},{32,48},{48,32},{64,80},{80,64},{96,112},{112,96},{1... | collective-permute-start | bytes 983048 | tf_op jit(solution)/shard_map/ppermute | solution.py:179

commit v6 on v5

--- a/solution.py
+++ b/solution.py
@@ -21,7 +21,7 @@
 
 CORE = [(i, i ^ 1) for i in range(32)]
 NEAR = [[8 * far + 2 * near + core for near in range(4)] for far in range(4) for core in range(2)]
-FAR = [[(i, i ^ (8 * step)) for i in range(32)] for step in (1, 2, 3)]
+FAR = [[(i, i ^ (8 * step)) for i in range(32)] for step in (1, 3, 2)]
 
 NT = (((1,), (1,)), ((), ()))
 NN = (((1,), (0,)), ((), ()))
@@ -64,7 +64,7 @@
         out_ref[far] = total + jnp.where(mine == far, f32(decay_rate), f32(0.0)) * momentum_ref[...]
 
 
-def far_sum_kernel(own_ref, first_ref, second_ref, third_ref, out_ref):
+def far_sum_kernel(own_ref, first_ref, third_ref, second_ref, out_ref):
     for far in range(4):
         total = (own_ref[far] + first_ref[far]) + (second_ref[far] + third_ref[far])
         for other in range(4):

time: 102 us -> 100 us (0.980)
  waiting for transfers between devices: 13.3 us -> 10.1 us
    ppermute x3, waiting for transfers between devices: 9.75 us -> 6.6 us  [per_device(): others = [lax.ppermute(parts, 'dp', pairs) for pairs in FAR]]
where the time goes in v6:
time: 100 us; the launch traced here: 99.9 us
  blocking collectives  46.6 us (47%)
  starting transfers between devices  36.2 us (36%)
  waiting for transfers between devices  10.1 us (10%)
  Pallas kernels  5.38 us (5%)
    all_to_all x4, blocking collectives, exchange(): lax.all_to_all(value, axis, 0, 0, tiled=True, axis_index_groups=groups)  46.6 us
    ppermute x3, starting transfers between devices, per_device(): others = [lax.ppermute(parts, 'dp', pairs) for pairs in FAR]  16.2 us
    ppermute x2, starting transfers between devices, per_device(): other = lax.ppermute(mine, 'dp', CORE)  11.2 us
    ppermute x1, starting transfers between devices, per_device(): lax.ppermute(send, 'dp', CORE)  8.79 us
    ppermute x3, waiting for transfers between devices, per_device(): others = [lax.ppermute(parts, 'dp', pairs) for pairs in FAR]  6.6 us
    pallas_call x1, Pallas kernels, per_device(): call(final_kernel, [(16, 256), (16, 256), (16, 32)], [pltpu.VMEM((IN, IN)...  4.84 us
    ppermute x2, waiting for transfers between devices, per_device(): other = lax.ppermute(mine, 'dp', CORE)  2.37 us
  transfers between devices with their start and end apart: 6, of which 4 were waited for; matrix products, arithmetic and copies ran while one was open for 0% of the time, Pallas kernels for 0%

profile of v6, /device:TPU:1, one launch (start us, length us, event | category | flops | bytes accessed | tf_op | source)
XLA Modules:
  0.0 99.9 jit_solution(9528964262268226753)
XLA Ops:
  0.6 0.0 copy-start
  0.6 0.9 copy-done
  1.6 8.8 %collective-permute-start = (f32[4,4,16,256]{3,2,1,0:T(8,128)S(1)}, f32[4,4,16,256]{3,2,1,0:T(8,128)S(1)}, u32[]{:S(2)}, u32[]{:S(2)}) collective-permute-start(f32[4,4,16,256]{3,2,1,0:T(8,128)S(1)} %shard_map.58), channel_id=1, source_target_pairs={{0,16},{16,0},{32,48},{48,32},{64,80},{80,64},{96,112},{112,96},{1... | collective-permute-start | bytes 786440 | tf_op jit(solution)/shard_map/ppermute | solution.py:170
  10.4 1.1 %collective-permute-done.got_ref = f32[4,4,16,256]{3,2,1,0:T(8,128)S(1)} collective-permute-done((f32[4,4,16,256]{3,2,1,0:T(8,128)S(1)}, f32[4,4,16,256]{3,2,1,0:T(8,128)S(1)}, u32[]{:S(2)}, u32[]{:S(2)}) %collective-permute-start) | collective-permute-done | bytes 262176 | tf_op jit(solution)/shard_map/ppermute | solution.py:170
  11.6 0.0 copy-start.2
  11.6 10.7 %all_to_all.20.parts_ref = f32[4,4,16,256]{3,2,1,0:T(8,128)S(1)} all-to-all(f32[4,4,16,256]{3,2,1,0:T(8,128)S(1)} %shard_map.59), channel_id=1, replica_groups={{0,32,64,96},{16,48,80,112},{128,160,192,224},{144,176,208,240},{256,28..., dimensions={0} | all-to-all | bytes 524288 | tf_op jit(solution)/shard_map/all_to_all | solution.py:163
  22.2 0.0 copy-done.2
  22.3 9.1 %collective-permute-start.3 = (f32[4,16,256]{2,1,0:T(8,128)S(1)}, f32[4,16,256]{2,1,0:T(8,128)S(1)}, u32[]{:S(2)}, u32[]{:S(2)}) collective-permute-start(f32[4,16,256]{2,1,0:T(8,128)S(1)} %shard_map.60.own_ref), channel_id=1, source_target_pairs={{0,256},{16,272},{32,288},{48,304},{64,320},{80,336},{96,352},{112... | collective-permute-start | bytes 196616 | tf_op jit(solution)/shard_map/ppermute | solution.py:172
  31.4 3.1 %collective-permute-start.2 = (f32[4,16,256]{2,1,0:T(8,128)S(1)}, f32[4,16,256]{2,1,0:T(8,128)S(1)}, u32[]{:S(2)}, u32[]{:S(2)}) collective-permute-start(f32[4,16,256]{2,1,0:T(8,128)S(1)} %shard_map.60.own_ref), channel_id=1, source_target_pairs={{0,384},{16,400},{32,416},{48,432},{64,448},{80,464},{96,480},{112... | collective-permute-start | bytes 196616 | tf_op jit(solution)/shard_map/ppermute | solution.py:172
  34.5 4.0 %collective-permute-start.1 = (f32[4,16,256]{2,1,0:T(8,128)S(1)}, f32[4,16,256]{2,1,0:T(8,128)S(1)}, u32[]{:S(2)}, u32[]{:S(2)}) collective-permute-start(f32[4,16,256]{2,1,0:T(8,128)S(1)} %shard_map.60.own_ref), channel_id=1, source_target_pairs={{0,128},{16,144},{32,160},{48,176},{64,192},{80,208},{96,224},{112... | collective-permute-start | bytes 196616 | tf_op jit(solution)/shard_map/ppermute | solution.py:172
  38.5 0.0 collective-permute-done.3.second_ref
  38.5 6.6 %collective-permute-done.2.third_ref = f32[4,16,256]{2,1,0:T(8,128)S(1)} collective-permute-done((f32[4,16,256]{2,1,0:T(8,128)S(1)}, f32[4,16,256]{2,1,0:T(8,128)S(1)}, u32[]{:S(2)}, u32[]{:S(2)}) %collective-permute-start.2) | collective-permute-done | bytes 65568 | tf_op jit(solution)/shard_map/ppermute | solution.py:172
  45.1 0.0 collective-permute-done.1.first_ref
  45.1 9.7 %all_to_all.21 = f32[4,4,16,256]{3,2,1,0:T(8,128)S(1)} all-to-all(f32[4,4,16,256]{3,2,1,0:T(8,128)S(1)} %shard_map.61), channel_id=1, replica_groups={{0,32,64,96},{16,48,80,112},{128,160,192,224},{144,176,208,240},{256,28..., dimensions={0} | all-to-all | bytes 524288 | tf_op jit(solution)/shard_map/all_to_all | solution.py:163
  54.8 6.6 %collective-permute-start.4 = (f32[256,256]{1,0:T(8,128)S(1)}, f32[256,256]{1,0:T(8,128)S(1)}, u32[]{:S(2)}, u32[]{:S(2)}) collective-permute-start(f32[256,256]{1,0:T(8,128)S(1)} %bitcast.8), channel_id=1, source_target_pairs={{0,16},{16,0},{32,48},{48,32},{64,80},{80,64},{96,112},{112,96},{1... | collective-permute-start | bytes 786440 | tf_op jit(solution)/shard_map/ppermute | solution.py:175
  61.4 1.1 %collective-permute-done.4.other_ref = f32[256,256]{1,0:T(8,128)S(1)} collective-permute-done((f32[256,256]{1,0:T(8,128)S(1)}, f32[256,256]{1,0:T(8,128)S(1)}, u32[]{:S(2)}, u32[]{:S(2)}) %collective-permute-start.4) | collective-permute-done | bytes 262176 | tf_op jit(solution)/shard_map/ppermute | solution.py:175
  62.6 0.4 shard_map.62
  63.0 15.5 %all_to_all.22.parts_ref = f32[16,40,128]{2,1,0:T(8,128)S(1)} all-to-all(f32[16,40,128]{2,1,0:T(8,128)S(1)} %bitcast.10), channel_id=1, replica_groups=mesh['dp'=32,'tensor'=16] {'tensor'}, dimensions={0} | all-to-all | bytes 655360 | tf_op jit(solution)/shard_map/all_to_all | solution.py:163
  78.5 0.0 copy-start.1
  78.5 10.7 %all_to_all.23 = f32[16,40,128]{2,1,0:T(8,128)S(1)} all-to-all(f32[16,40,128]{2,1,0:T(8,128)S(1)} %shard_map.63), channel_id=1, replica_groups=mesh['dp'=32,'tensor'=16] {'tensor'}, dimensions={0} | all-to-all | bytes 655360 | tf_op jit(solution)/shard_map/all_to_all | solution.py:163
  89.2 4.6 %collective-permute-start.5 = (f32[640,128]{1,0:T(8,128)S(1)}, f32[640,128]{1,0:T(8,128)S(1)}, u32[]{:S(2)}, u32[]{:S(2)}) collective-permute-start(f32[640,128]{1,0:T(8,128)S(1)} %bitcast.4), channel_id=1, source_target_pairs={{0,16},{16,0},{32,48},{48,32},{64,80},{80,64},{96,112},{112,96},{1... | collective-permute-start | bytes 983048 | tf_op jit(solution)/shard_map/ppermute | solution.py:179
  93.8 1.2 %collective-permute-done.5.other_ref = f32[640,128]{1,0:T(8,128)S(1)} collective-permute-done((f32[640,128]{1,0:T(8,128)S(1)}, f32[640,128]{1,0:T(8,128)S(1)}, u32[]{:S(2)}, u32[]{:S(2)}) %collective-permute-start.5) | collective-permute-done | bytes 327712 | tf_op jit(solution)/shard_map/ppermute | solution.py:179
  95.1 0.0 copy-done.1
  95.1 4.8 %shard_map.64 = (f32[16,256]{1,0:T(8,128)}, f32[16,256]{1,0:T(8,128)}, f32[16,32]{1,0:T(8,128)}) custom-call(f32[640,128]{1,0:T(8,128)S(1)} %bitcast.5, f32[640,128]{1,0:T(8,128)S(1)} %collective-permute-done.5.other_ref, f32[2,256,256]{2,1,0:T(8,128)S(1)} %get-tuple-element.6.rows_ref, f32[16,256]{1,0:T(8,128)S(1)} %copy-done.1), custom_call_target="tpu_custom_call" | custom-call | tf_op jit(solution)/shard_map/pallas_call | solution.py:180
  (5 shorter events, 0.1 us)
Async XLA Ops:
  0.6 1.0 copy-start
  1.6 9.9 %collective-permute-start = (f32[4,4,16,256]{3,2,1,0:T(8,128)S(1)}, f32[4,4,16,256]{3,2,1,0:T(8,128)S(1)}, u32[]{:S(2)}, u32[]{:S(2)}) collective-permute-start(f32[4,4,16,256]{3,2,1,0:T(8,128)S(1)} %shard_map.58), channel_id=1, source_target_pairs={{0,16},{16,0},{32,48},{48,32},{64,80},{80,64},{96,112},{112,96},{1... | collective-permute-start | bytes 786440 | tf_op jit(solution)/shard_map/ppermute | solution.py:170
  11.6 10.7 %copy-start.2 = (f32[16,256]{1,0:T(8,128)S(1)}, f32[16,256]{1,0:T(8,128)}, u32[]{:S(2)}) copy-start(f32[16,256]{1,0:T(8,128)} %momentum_ref.1) | copy-start | bytes 49156
  22.3 16.2 %collective-permute-start.3 = (f32[4,16,256]{2,1,0:T(8,128)S(1)}, f32[4,16,256]{2,1,0:T(8,128)S(1)}, u32[]{:S(2)}, u32[]{:S(2)}) collective-permute-start(f32[4,16,256]{2,1,0:T(8,128)S(1)} %shard_map.60.own_ref), channel_id=1, source_target_pairs={{0,256},{16,272},{32,288},{48,304},{64,320},{80,336},{96,352},{112... | collective-permute-start | bytes 196616 | tf_op jit(solution)/shard_map/ppermute | solution.py:172
  31.4 13.7 %collective-permute-start.2 = (f32[4,16,256]{2,1,0:T(8,128)S(1)}, f32[4,16,256]{2,1,0:T(8,128)S(1)}, u32[]{:S(2)}, u32[]{:S(2)}) collective-permute-start(f32[4,16,256]{2,1,0:T(8,128)S(1)} %shard_map.60.own_ref), channel_id=1, source_target_pairs={{0,384},{16,400},{32,416},{48,432},{64,448},{80,464},{96,480},{112... | collective-permute-start | bytes 196616 | tf_op jit(solution)/shard_map/ppermute | solution.py:172
  34.5 10.6 %collective-permute-start.1 = (f32[4,16,256]{2,1,0:T(8,128)S(1)}, f32[4,16,256]{2,1,0:T(8,128)S(1)}, u32[]{:S(2)}, u32[]{:S(2)}) collective-permute-start(f32[4,16,256]{2,1,0:T(8,128)S(1)} %shard_map.60.own_ref), channel_id=1, source_target_pairs={{0,128},{16,144},{32,160},{48,176},{64,192},{80,208},{96,224},{112... | collective-permute-start | bytes 196616 | tf_op jit(solution)/shard_map/ppermute | solution.py:172
  54.8 7.7 %collective-permute-start.4 = (f32[256,256]{1,0:T(8,128)S(1)}, f32[256,256]{1,0:T(8,128)S(1)}, u32[]{:S(2)}, u32[]{:S(2)}) collective-permute-start(f32[256,256]{1,0:T(8,128)S(1)} %bitcast.8), channel_id=1, source_target_pairs={{0,16},{16,0},{32,48},{48,32},{64,80},{80,64},{96,112},{112,96},{1... | collective-permute-start | bytes 786440 | tf_op jit(solution)/shard_map/ppermute | solution.py:175
  78.5 16.6 %copy-start.1 = (f32[16,256]{1,0:T(8,128)S(1)}, f32[16,256]{1,0:T(8,128)}, u32[]{:S(2)}) copy-start(f32[16,256]{1,0:T(8,128)} %weight_ref.1) | copy-start | bytes 49156
  89.2 5.8 %collective-permute-start.5 = (f32[640,128]{1,0:T(8,128)S(1)}, f32[640,128]{1,0:T(8,128)S(1)}, u32[]{:S(2)}, u32[]{:S(2)}) collective-permute-start(f32[640,128]{1,0:T(8,128)S(1)} %bitcast.4), channel_id=1, source_target_pairs={{0,16},{16,0},{32,48},{48,32},{64,80},{80,64},{96,112},{112,96},{1... | collective-permute-start | bytes 983048 | tf_op jit(solution)/shard_map/ppermute | solution.py:179

commit v7 on v6

--- a/solution.py
+++ b/solution.py
@@ -20,7 +20,7 @@
 bf16 = jnp.bfloat16
 
 CORE = [(i, i ^ 1) for i in range(32)]
-NEAR = [[8 * far + 2 * near + core for near in range(4)] for far in range(4) for core in range(2)]
+NEAR = [[(i, i ^ (2 * step)) for i in range(32)] for step in (1, 2, 3)]
 FAR = [[(i, i ^ (8 * step)) for i in range(32)] for step in (1, 3, 2)]
 
 NT = (((1,), (1,)), ((), ()))
@@ -50,25 +50,30 @@
             send_ref[near, far] = grad_ref[far, near, 1 - core].astype(f32)
 
 
-def core_sum_kernel(grad_ref, got_ref, out_ref):
-    _, _, core = place()
-    for near in range(4):
+def core_sum_kernel(grad_ref, got_ref, *out_refs):
+    near, _, core = place()
+    for step in range(4):
+        other = near ^ step
         for far in range(4):
-            out_ref[near, far] = grad_ref[far, near, core].astype(f32) + got_ref[near, far]
-
-
-def near_sum_kernel(parts_ref, momentum_ref, out_ref):
+            out_refs[step][far] = grad_ref[far, other, core].astype(f32) + got_ref[other, far]
+
+
+def near_sum_kernel(own_ref, first_ref, second_ref, third_ref, momentum_ref, out_ref):
     _, mine, _ = place()
     for far in range(4):
-        total = (parts_ref[0, far] + parts_ref[1, far]) + (parts_ref[2, far] + parts_ref[3, far])
+        total = (own_ref[far] + first_ref[far]) + (second_ref[far] + third_ref[far])
         out_ref[far] = total + jnp.where(mine == far, f32(decay_rate), f32(0.0)) * momentum_ref[...]
 
 
 def far_sum_kernel(own_ref, first_ref, third_ref, second_ref, out_ref):
     for far in range(4):
-        total = (own_ref[far] + first_ref[far]) + (second_ref[far] + third_ref[far])
-        for other in range(4):
-            out_ref[other, far] = total
+        out_ref[far] = (own_ref[far] + first_ref[far]) + (second_ref[far] + third_ref[far])
+
+
+def near_join_kernel(own_ref, first_ref, second_ref, third_ref, out_ref):
+    near, _, _ = place()
+    for step, part_ref in enumerate((own_ref, first_ref, second_ref, third_ref)):
+        out_ref[near ^ step] = part_ref[...]
 
 
 def gram_kernel(mine_ref, other_ref, out_ref, rows_ref):
@@ -159,23 +164,27 @@
     )
 
 
-def exchange(value, axis, groups=None):
-    return lax.all_to_all(value, axis, 0, 0, tiled=True, axis_index_groups=groups)
+def exchange(value):
+    return lax.all_to_all(value, "tensor", 0, 0, tiled=True)
 
 
 def per_device(gradients, momentum, weight):
     chunks = (4, 4, 16, 256)
     gradients = gradients.reshape(4, 4, 2, 16, 256)
     (send,) = call(send_kernel, [chunks])(gradients)
-    (parts,) = call(core_sum_kernel, [chunks])(gradients, lax.ppermute(send, "dp", CORE))
-    (parts,) = call(near_sum_kernel, [chunks[1:]])(exchange(parts, "dp", NEAR), momentum)
-    others = [lax.ppermute(parts, "dp", pairs) for pairs in FAR]
-    (spread,) = call(far_sum_kernel, [chunks])(parts, *others)
-    mine = exchange(spread, "dp", NEAR).reshape(256, 256)
+    piece = chunks[1:]
+    parts = call(core_sum_kernel, [piece] * 4)(gradients, lax.ppermute(send, "dp", CORE))
+    others = [lax.ppermute(part, "dp", pairs) for part, pairs in zip(parts[1:], NEAR)]
+    (part,) = call(near_sum_kernel, [piece])(parts[0], *others, momentum)
+    others = [lax.ppermute(part, "dp", pairs) for pairs in FAR]
+    (part,) = call(far_sum_kernel, [piece])(part, *others)
+    others = [lax.ppermute(part, "dp", pairs) for pairs in NEAR]
+    (mine,) = call(near_join_kernel, [chunks])(part, *others)
+    mine = mine.reshape(256, 256)
     other = lax.ppermute(mine, "dp", CORE)
     blocks, rows = call(gram_kernel, [(640, 128), (2, 256, 256)], limit=8 << 20)(mine, other)
-    (spread,) = call(tensor_sum_kernel, [(16, 40, 128)])(exchange(blocks.reshape(16, 40, 128), "tensor"))
-    mine = exchange(spread, "tensor").reshape(640, 128)
+    (spread,) = call(tensor_sum_kernel, [(16, 40, 128)])(exchange(blocks.reshape(16, 40, 128)))
+    mine = exchange(spread).reshape(640, 128)
     other = lax.ppermute(mine, "dp", CORE)
     return call(
         final_kernel,

time: 100 us -> 105 us (1.050)
  blocking collectives: 46.6 us -> 26.1 us
  starting transfers between devices: 36.2 us -> 55.2 us
  waiting for transfers between devices: 10.1 us -> 15.7 us
    all_to_all x4 -> x2, blocking collectives: 46.6 us -> 26.1 us  [exchange(): return lax.all_to_all(value, 'tensor', 0, 0, tiled=True)]
    ppermute x3 -> x9, starting transfers between devices: 16.2 us -> 36.2 us  [the longest x3 17.6 us: per_device(): others = [lax.ppermute(part, 'dp', pairs) for pairs in FAR]]
    ppermute x3 -> x9, waiting for transfers between devices: 6.6 us -> 12.2 us  [the longest x3 8.06 us: per_device(): others = [lax.ppermute(part, 'dp', pairs) for pairs in FAR]]
  transfers between devices with their start and end apart: 6 -> 12, of which waited for: 4 -> 8; matrix products, arithmetic and copies ran while one was open for 0% -> 0% of each run, Pallas kernels for 0% -> 0%
where the time goes in v7:
time: 105 us; the launch traced here: 104 us
  starting transfers between devices  55.2 us (53%)
  blocking collectives  26.1 us (25%)
  waiting for transfers between devices  15.7 us (15%)
  Pallas kernels  5.4 us (5%)
    all_to_all x2, blocking collectives, exchange(): return lax.all_to_all(value, 'tensor', 0, 0, tiled=True)  26.1 us
    ppermute x3, starting transfers between devices, per_device(): others = [lax.ppermute(part, 'dp', pairs) for pairs in FAR]  17.6 us
    ppermute x2, starting transfers between devices, per_device(): other = lax.ppermute(mine, 'dp', CORE)  10.2 us
    ppermute x3, starting transfers between devices, per_device(): others = [lax.ppermute(part, 'dp', pairs) for pairs in NEAR]  9.27 us
    ppermute x3, starting transfers between devices, per_device(): lax.ppermute(part, 'dp', pairs)  9.27 us
    ppermute x1, starting transfers between devices, per_device(): lax.ppermute(send, 'dp', CORE)  8.79 us
    ppermute x3, waiting for transfers between devices, per_device(): others = [lax.ppermute(part, 'dp', pairs) for pairs in FAR]  8.06 us
    pallas_call x1, Pallas kernels, per_device(): call(final_kernel, [(16, 256), (16, 256), (16, 32)], [pltpu.VMEM((IN, IN)...  4.83 us
  transfers between devices with their start and end apart: 12, of which 8 were waited for; matrix products, arithmetic and copies ran while one was open for 0% of the time, Pallas kernels for 0%

profile of v7, /device:TPU:1, one launch (start us, length us, event | category | flops | bytes accessed | tf_op | source)
XLA Modules:
  0.0 104.1 jit_solution(13836912417260565004)
XLA Ops:
  0.6 0.0 copy-start
  0.6 0.9 copy-done
  1.6 8.8 %collective-permute-start = (f32[4,4,16,256]{3,2,1,0:T(8,128)S(1)}, f32[4,4,16,256]{3,2,1,0:T(8,128)S(1)}, u32[]{:S(2)}, u32[]{:S(2)}) collective-permute-start(f32[4,4,16,256]{3,2,1,0:T(8,128)S(1)} %shard_map.58), channel_id=1, source_target_pairs={{0,16},{16,0},{32,48},{48,32},{64,80},{80,64},{96,112},{112,96},{1... | collective-permute-start | bytes 786440 | tf_op jit(solution)/shard_map/ppermute | solution.py:176
  10.4 1.1 %collective-permute-done.got_ref = f32[4,4,16,256]{3,2,1,0:T(8,128)S(1)} collective-permute-done((f32[4,4,16,256]{3,2,1,0:T(8,128)S(1)}, f32[4,4,16,256]{3,2,1,0:T(8,128)S(1)}, u32[]{:S(2)}, u32[]{:S(2)}) %collective-permute-start) | collective-permute-done | bytes 262176 | tf_op jit(solution)/shard_map/ppermute | solution.py:176
  11.5 0.0 copy-start.2
  11.6 1.9 %collective-permute-start.1 = (f32[4,16,256]{2,1,0:T(8,128)S(1)}, f32[4,16,256]{2,1,0:T(8,128)S(1)}, u32[]{:S(2)}, u32[]{:S(2)}) collective-permute-start(f32[4,16,256]{2,1,0:T(8,128)S(1)} %get-tuple-element.10), channel_id=1, source_target_pairs={{0,32},{16,48},{32,0},{48,16},{64,96},{80,112},{96,64},{112,80},{1... | collective-permute-start | bytes 196616 | tf_op jit(solution)/shard_map/ppermute | solution.py:177
  13.5 1.9 %collective-permute-start.2 = (f32[4,16,256]{2,1,0:T(8,128)S(1)}, f32[4,16,256]{2,1,0:T(8,128)S(1)}, u32[]{:S(2)}, u32[]{:S(2)}) collective-permute-start(f32[4,16,256]{2,1,0:T(8,128)S(1)} %get-tuple-element.11), channel_id=1, source_target_pairs={{0,64},{16,80},{32,96},{48,112},{64,0},{80,16},{96,32},{112,48},{1... | collective-permute-start | bytes 196616 | tf_op jit(solution)/shard_map/ppermute | solution.py:177
  15.4 5.4 %collective-permute-start.3 = (f32[4,16,256]{2,1,0:T(8,128)S(1)}, f32[4,16,256]{2,1,0:T(8,128)S(1)}, u32[]{:S(2)}, u32[]{:S(2)}) collective-permute-start(f32[4,16,256]{2,1,0:T(8,128)S(1)} %get-tuple-element.12), channel_id=1, source_target_pairs={{0,96},{16,112},{32,64},{48,80},{64,32},{80,48},{96,0},{112,16},{1... | collective-permute-start | bytes 196616 | tf_op jit(solution)/shard_map/ppermute | solution.py:177
  20.9 0.0 collective-permute-done.1.first_ref
  20.9 0.0 collective-permute-done.2.second_ref
  20.9 1.7 %collective-permute-done.3.third_ref = f32[4,16,256]{2,1,0:T(8,128)S(1)} collective-permute-done((f32[4,16,256]{2,1,0:T(8,128)S(1)}, f32[4,16,256]{2,1,0:T(8,128)S(1)}, u32[]{:S(2)}, u32[]{:S(2)}) %collective-permute-start.3) | collective-permute-done | bytes 65568 | tf_op jit(solution)/shard_map/ppermute | solution.py:177
  22.6 0.0 copy-done.2
  22.6 11.7 %collective-permute-start.6 = (f32[4,16,256]{2,1,0:T(8,128)S(1)}, f32[4,16,256]{2,1,0:T(8,128)S(1)}, u32[]{:S(2)}, u32[]{:S(2)}) collective-permute-start(f32[4,16,256]{2,1,0:T(8,128)S(1)} %shard_map.60.own_ref), channel_id=1, source_target_pairs={{0,256},{16,272},{32,288},{48,304},{64,320},{80,336},{96,352},{112... | collective-permute-start | bytes 196616 | tf_op jit(solution)/shard_map/ppermute | solution.py:179
  34.3 3.0 %collective-permute-start.5 = (f32[4,16,256]{2,1,0:T(8,128)S(1)}, f32[4,16,256]{2,1,0:T(8,128)S(1)}, u32[]{:S(2)}, u32[]{:S(2)}) collective-permute-start(f32[4,16,256]{2,1,0:T(8,128)S(1)} %shard_map.60.own_ref), channel_id=1, source_target_pairs={{0,384},{16,400},{32,416},{48,432},{64,448},{80,464},{96,480},{112... | collective-permute-start | bytes 196616 | tf_op jit(solution)/shard_map/ppermute | solution.py:179
  37.3 2.9 %collective-permute-start.4 = (f32[4,16,256]{2,1,0:T(8,128)S(1)}, f32[4,16,256]{2,1,0:T(8,128)S(1)}, u32[]{:S(2)}, u32[]{:S(2)}) collective-permute-start(f32[4,16,256]{2,1,0:T(8,128)S(1)} %shard_map.60.own_ref), channel_id=1, source_target_pairs={{0,128},{16,144},{32,160},{48,176},{64,192},{80,208},{96,224},{112... | collective-permute-start | bytes 196616 | tf_op jit(solution)/shard_map/ppermute | solution.py:179
  40.3 0.0 collective-permute-done.6.second_ref
  40.3 5.4 %collective-permute-done.5.third_ref = f32[4,16,256]{2,1,0:T(8,128)S(1)} collective-permute-done((f32[4,16,256]{2,1,0:T(8,128)S(1)}, f32[4,16,256]{2,1,0:T(8,128)S(1)}, u32[]{:S(2)}, u32[]{:S(2)}) %collective-permute-start.5) | collective-permute-done | bytes 65568 | tf_op jit(solution)/shard_map/ppermute | solution.py:179
  45.7 2.6 %collective-permute-done.4.first_ref = f32[4,16,256]{2,1,0:T(8,128)S(1)} collective-permute-done((f32[4,16,256]{2,1,0:T(8,128)S(1)}, f32[4,16,256]{2,1,0:T(8,128)S(1)}, u32[]{:S(2)}, u32[]{:S(2)}) %collective-permute-start.4) | collective-permute-done | bytes 65568 | tf_op jit(solution)/shard_map/ppermute | solution.py:179
  48.4 2.7 %collective-permute-start.9 = (f32[4,16,256]{2,1,0:T(8,128)S(1)}, f32[4,16,256]{2,1,0:T(8,128)S(1)}, u32[]{:S(2)}, u32[]{:S(2)}) collective-permute-start(f32[4,16,256]{2,1,0:T(8,128)S(1)} %shard_map.61.own_ref), channel_id=1, source_target_pairs={{0,96},{16,112},{32,64},{48,80},{64,32},{80,48},{96,0},{112,16},{1... | collective-permute-start | bytes 196616 | tf_op jit(solution)/shard_map/ppermute | solution.py:181
  51.1 1.9 %collective-permute-start.8 = (f32[4,16,256]{2,1,0:T(8,128)S(1)}, f32[4,16,256]{2,1,0:T(8,128)S(1)}, u32[]{:S(2)}, u32[]{:S(2)}) collective-permute-start(f32[4,16,256]{2,1,0:T(8,128)S(1)} %shard_map.61.own_ref), channel_id=1, source_target_pairs={{0,64},{16,80},{32,96},{48,112},{64,0},{80,16},{96,32},{112,48},{1... | collective-permute-start | bytes 196616 | tf_op jit(solution)/shard_map/ppermute | solution.py:181
  53.0 4.6 %collective-permute-start.7 = (f32[4,16,256]{2,1,0:T(8,128)S(1)}, f32[4,16,256]{2,1,0:T(8,128)S(1)}, u32[]{:S(2)}, u32[]{:S(2)}) collective-permute-start(f32[4,16,256]{2,1,0:T(8,128)S(1)} %shard_map.61.own_ref), channel_id=1, source_target_pairs={{0,32},{16,48},{32,0},{48,16},{64,96},{80,112},{96,64},{112,80},{1... | collective-permute-start | bytes 196616 | tf_op jit(solution)/shard_map/ppermute | solution.py:181
  57.7 0.0 collective-permute-done.9.third_ref
  57.7 0.1 collective-permute-done.8.second_ref
  57.8 2.3 %collective-permute-done.7.first_ref = f32[4,16,256]{2,1,0:T(8,128)S(1)} collective-permute-done((f32[4,16,256]{2,1,0:T(8,128)S(1)}, f32[4,16,256]{2,1,0:T(8,128)S(1)}, u32[]{:S(2)}, u32[]{:S(2)}) %collective-permute-start.7) | collective-permute-done | bytes 65568 | tf_op jit(solution)/shard_map/ppermute | solution.py:181
  60.1 5.6 %collective-permute-start.10 = (f32[256,256]{1,0:T(8,128)S(1)}, f32[256,256]{1,0:T(8,128)S(1)}, u32[]{:S(2)}, u32[]{:S(2)}) collective-permute-start(f32[256,256]{1,0:T(8,128)S(1)} %bitcast.8), channel_id=1, source_target_pairs={{0,16},{16,0},{32,48},{48,32},{64,80},{80,64},{96,112},{112,96},{1... | collective-permute-start | bytes 786440 | tf_op jit(solution)/shard_map/ppermute | solution.py:184
  65.7 1.1 %collective-permute-done.10.other_ref = f32[256,256]{1,0:T(8,128)S(1)} collective-permute-done((f32[256,256]{1,0:T(8,128)S(1)}, f32[256,256]{1,0:T(8,128)S(1)}, u32[]{:S(2)}, u32[]{:S(2)}) %collective-permute-start.10) | collective-permute-done | bytes 262176 | tf_op jit(solution)/shard_map/ppermute | solution.py:184
  66.9 0.4 shard_map.63
  67.3 15.3 %all_to_all.10.parts_ref = f32[16,40,128]{2,1,0:T(8,128)S(1)} all-to-all(f32[16,40,128]{2,1,0:T(8,128)S(1)} %bitcast.10), channel_id=1, replica_groups=mesh['dp'=32,'tensor'=16] {'tensor'}, dimensions={0} | all-to-all | bytes 655360 | tf_op jit(solution)/shard_map/all_to_all | solution.py:168
  82.7 0.0 copy-start.1
  82.7 10.7 %all_to_all.11 = f32[16,40,128]{2,1,0:T(8,128)S(1)} all-to-all(f32[16,40,128]{2,1,0:T(8,128)S(1)} %shard_map.64), channel_id=1, replica_groups=mesh['dp'=32,'tensor'=16] {'tensor'}, dimensions={0} | all-to-all | bytes 655360 | tf_op jit(solution)/shard_map/all_to_all | solution.py:168
  93.4 4.6 %collective-permute-start.11 = (f32[640,128]{1,0:T(8,128)S(1)}, f32[640,128]{1,0:T(8,128)S(1)}, u32[]{:S(2)}, u32[]{:S(2)}) collective-permute-start(f32[640,128]{1,0:T(8,128)S(1)} %bitcast.4), channel_id=1, source_target_pairs={{0,16},{16,0},{32,48},{48,32},{64,80},{80,64},{96,112},{112,96},{1... | collective-permute-start | bytes 983048 | tf_op jit(solution)/shard_map/ppermute | solution.py:188
  98.0 1.2 %collective-permute-done.11.other_ref = f32[640,128]{1,0:T(8,128)S(1)} collective-permute-done((f32[640,128]{1,0:T(8,128)S(1)}, f32[640,128]{1,0:T(8,128)S(1)}, u32[]{:S(2)}, u32[]{:S(2)}) %collective-permute-start.11) | collective-permute-done | bytes 327712 | tf_op jit(solution)/shard_map/ppermute | solution.py:188
  99.3 0.0 copy-done.1
  99.3 4.8 %shard_map.65 = (f32[16,256]{1,0:T(8,128)}, f32[16,256]{1,0:T(8,128)}, f32[16,32]{1,0:T(8,128)}) custom-call(f32[640,128]{1,0:T(8,128)S(1)} %bitcast.5, f32[640,128]{1,0:T(8,128)S(1)} %collective-permute-done.11.other_ref, f32[2,256,256]{2,1,0:T(8,128)S(1)} %get-tuple-element.14.rows_ref, f32[16,256]{1,0:T(8,128)S(1)} %copy-done.1), custom_call_target="tpu_custom_call" | custom-call | tf_op jit(solution)/shard_map/pallas_call | solution.py:189
  (6 shorter events, 0.2 us)
Async XLA Ops:
  0.6 1.0 copy-start
  1.6 9.9 %collective-permute-start = (f32[4,4,16,256]{3,2,1,0:T(8,128)S(1)}, f32[4,4,16,256]{3,2,1,0:T(8,128)S(1)}, u32[]{:S(2)}, u32[]{:S(2)}) collective-permute-start(f32[4,4,16,256]{3,2,1,0:T(8,128)S(1)} %shard_map.58), channel_id=1, source_target_pairs={{0,16},{16,0},{32,48},{48,32},{64,80},{80,64},{96,112},{112,96},{1... | collective-permute-start | bytes 786440 | tf_op jit(solution)/shard_map/ppermute | solution.py:176
  11.5 11.0 %copy-start.2 = (f32[16,256]{1,0:T(8,128)S(1)}, f32[16,256]{1,0:T(8,128)}, u32[]{:S(2)}) copy-start(f32[16,256]{1,0:T(8,128)} %momentum_ref.1) | copy-start | bytes 49156
  11.6 9.3 %collective-permute-start.1 = (f32[4,16,256]{2,1,0:T(8,128)S(1)}, f32[4,16,256]{2,1,0:T(8,128)S(1)}, u32[]{:S(2)}, u32[]{:S(2)}) collective-permute-start(f32[4,16,256]{2,1,0:T(8,128)S(1)} %get-tuple-element.10), channel_id=1, source_target_pairs={{0,32},{16,48},{32,0},{48,16},{64,96},{80,112},{96,64},{112,80},{1... | collective-permute-start | bytes 196616 | tf_op jit(solution)/shard_map/ppermute | solution.py:177
  13.5 7.4 %collective-permute-start.2 = (f32[4,16,256]{2,1,0:T(8,128)S(1)}, f32[4,16,256]{2,1,0:T(8,128)S(1)}, u32[]{:S(2)}, u32[]{:S(2)}) collective-permute-start(f32[4,16,256]{2,1,0:T(8,128)S(1)} %get-tuple-element.11), channel_id=1, source_target_pairs={{0,64},{16,80},{32,96},{48,112},{64,0},{80,16},{96,32},{112,48},{1... | collective-permute-start | bytes 196616 | tf_op jit(solution)/shard_map/ppermute | solution.py:177
  15.4 7.1 %collective-permute-start.3 = (f32[4,16,256]{2,1,0:T(8,128)S(1)}, f32[4,16,256]{2,1,0:T(8,128)S(1)}, u32[]{:S(2)}, u32[]{:S(2)}) collective-permute-start(f32[4,16,256]{2,1,0:T(8,128)S(1)} %get-tuple-element.12), channel_id=1, source_target_pairs={{0,96},{16,112},{32,64},{48,80},{64,32},{80,48},{96,0},{112,16},{1... | collective-permute-start | bytes 196616 | tf_op jit(solution)/shard_map/ppermute | solution.py:177
  22.6 17.7 %collective-permute-start.6 = (f32[4,16,256]{2,1,0:T(8,128)S(1)}, f32[4,16,256]{2,1,0:T(8,128)S(1)}, u32[]{:S(2)}, u32[]{:S(2)}) collective-permute-start(f32[4,16,256]{2,1,0:T(8,128)S(1)} %shard_map.60.own_ref), channel_id=1, source_target_pairs={{0,256},{16,272},{32,288},{48,304},{64,320},{80,336},{96,352},{112... | collective-permute-start | bytes 196616 | tf_op jit(solution)/shard_map/ppermute | solution.py:179
  34.3 11.4 %collective-permute-start.5 = (f32[4,16,256]{2,1,0:T(8,128)S(1)}, f32[4,16,256]{2,1,0:T(8,128)S(1)}, u32[]{:S(2)}, u32[]{:S(2)}) collective-permute-start(f32[4,16,256]{2,1,0:T(8,128)S(1)} %shard_map.60.own_ref), channel_id=1, source_target_pairs={{0,384},{16,400},{32,416},{48,432},{64,448},{80,464},{96,480},{112... | collective-permute-start | bytes 196616 | tf_op jit(solution)/shard_map/ppermute | solution.py:179
  37.3 11.0 %collective-permute-start.4 = (f32[4,16,256]{2,1,0:T(8,128)S(1)}, f32[4,16,256]{2,1,0:T(8,128)S(1)}, u32[]{:S(2)}, u32[]{:S(2)}) collective-permute-start(f32[4,16,256]{2,1,0:T(8,128)S(1)} %shard_map.60.own_ref), channel_id=1, source_target_pairs={{0,128},{16,144},{32,160},{48,176},{64,192},{80,208},{96,224},{112... | collective-permute-start | bytes 196616 | tf_op jit(solution)/shard_map/ppermute | solution.py:179
  48.4 9.3 %collective-permute-start.9 = (f32[4,16,256]{2,1,0:T(8,128)S(1)}, f32[4,16,256]{2,1,0:T(8,128)S(1)}, u32[]{:S(2)}, u32[]{:S(2)}) collective-permute-start(f32[4,16,256]{2,1,0:T(8,128)S(1)} %shard_map.61.own_ref), channel_id=1, source_target_pairs={{0,96},{16,112},{32,64},{48,80},{64,32},{80,48},{96,0},{112,16},{1... | collective-permute-start | bytes 196616 | tf_op jit(solution)/shard_map/ppermute | solution.py:181
  51.1 6.7 %collective-permute-start.8 = (f32[4,16,256]{2,1,0:T(8,128)S(1)}, f32[4,16,256]{2,1,0:T(8,128)S(1)}, u32[]{:S(2)}, u32[]{:S(2)}) collective-permute-start(f32[4,16,256]{2,1,0:T(8,128)S(1)} %shard_map.61.own_ref), channel_id=1, source_target_pairs={{0,64},{16,80},{32,96},{48,112},{64,0},{80,16},{96,32},{112,48},{1... | collective-permute-start | bytes 196616 | tf_op jit(solution)/shard_map/ppermute | solution.py:181
  53.0 7.1 %collective-permute-start.7 = (f32[4,16,256]{2,1,0:T(8,128)S(1)}, f32[4,16,256]{2,1,0:T(8,128)S(1)}, u32[]{:S(2)}, u32[]{:S(2)}) collective-permute-start(f32[4,16,256]{2,1,0:T(8,128)S(1)} %shard_map.61.own_ref), channel_id=1, source_target_pairs={{0,32},{16,48},{32,0},{48,16},{64,96},{80,112},{96,64},{112,80},{1... | collective-permute-start | bytes 196616 | tf_op jit(solution)/shard_map/ppermute | solution.py:181
  60.1 6.8 %collective-permute-start.10 = (f32[256,256]{1,0:T(8,128)S(1)}, f32[256,256]{1,0:T(8,128)S(1)}, u32[]{:S(2)}, u32[]{:S(2)}) collective-permute-start(f32[256,256]{1,0:T(8,128)S(1)} %bitcast.8), channel_id=1, source_target_pairs={{0,16},{16,0},{32,48},{48,32},{64,80},{80,64},{96,112},{112,96},{1... | collective-permute-start | bytes 786440 | tf_op jit(solution)/shard_map/ppermute | solution.py:184
  82.7 16.6 %copy-start.1 = (f32[16,256]{1,0:T(8,128)S(1)}, f32[16,256]{1,0:T(8,128)}, u32[]{:S(2)}) copy-start(f32[16,256]{1,0:T(8,128)} %weight_ref.1) | copy-start | bytes 49156
  93.4 5.8 %collective-permute-start.11 = (f32[640,128]{1,0:T(8,128)S(1)}, f32[640,128]{1,0:T(8,128)S(1)}, u32[]{:S(2)}, u32[]{:S(2)}) collective-permute-start(f32[640,128]{1,0:T(8,128)S(1)} %bitcast.4), channel_id=1, source_target_pairs={{0,16},{16,0},{32,48},{48,32},{64,80},{80,64},{96,112},{112,96},{1... | collective-permute-start | bytes 983048 | tf_op jit(solution)/shard_map/ppermute | solution.py:188

commit v8 on v6

v8 whole, which is shorter than its diff:
```python
import functools

import jax
import jax.numpy as jnp
from jax import lax
from jax.experimental import pallas as pl
from jax.experimental.pallas import tpu as pltpu
from jax.sharding import PartitionSpec as P

IN = 512
OUT = 4096

decay_rate = 0.95
learn_rate = 0.02
weight_decay = 0.1
epsilon = 1e-07
quintic_a = 3.4445
quintic_b = -4.775
quintic_c = 2.0315

f32 = jnp.float32
bf16 = jnp.bfloat16

ROWS = (64, 64)
MOST = max(ROWS)
BLOCKS = (((0, 0), (0, 1), (1, 1)), ((0, 2), (0, 3), (1, 2), (1, 3), (2, 2), (2, 3), (3, 3)))
TALL = 128 * max(len(blocks) for blocks in BLOCKS)

CORE = [(i, i ^ 1) for i in range(32)]
NEAR = [[8 * far + 2 * near + core for near in range(4)] for far in range(4) for core in range(2)]
FAR = [[[(i, i ^ (8 * step)) for i in range(core, 32, 2)] for step in (1, 3, 2)] for core in range(2)]

NT = (((1,), (1,)), ((), ()))
NN = (((1,), (0,)), ((), ()))


def place():
    index = lax.axis_index("dp")
    return lax.rem(lax.div(index, 2), 4), lax.div(index, 8), lax.rem(index, 2)


def halves(value):
    high = value.astype(bf16)
    low = (value - high.astype(f32)).astype(bf16)
    return high, low


def mul3(left, right, dims):
    dot = lambda x, y: lax.dot_general(x, y, dims, preferred_element_type=f32)
    return dot(left[0], right[0]) + (dot(left[0], right[1]) + dot(left[1], right[0]))


def local_rows(grad_ref, momentum_ref, side):
    near, far, core = place()
    first, last = (0, ROWS[0]) if side == 0 else (ROWS[0], 128)
    for piece in range(4):
        for chunk in range(8):
            low, high = max(first, 16 * chunk), min(last, 16 * chunk + 16)
            if low >= high:
                continue
            own = (near == piece) & (far == chunk // 2) & (core == chunk % 2)
            value = grad_ref[chunk // 2, piece, chunk % 2].astype(f32)
            value = value + jnp.where(own, f32(decay_rate), f32(0.0)) * momentum_ref[...]
            yield piece, low - first, value[low - 16 * chunk : high - 16 * chunk]


def send_kernel(grad_ref, momentum_ref, send_ref):
    _, _, core = place()
    for side in range(2):

        @pl.when(core != side)
        def _():
            for piece, start, value in local_rows(grad_ref, momentum_ref, side):
                send_ref[piece, start : start + value.shape[0]] = value
            if ROWS[side] < MOST:
                send_ref[:, ROWS[side] :] = jnp.zeros((4, MOST - ROWS[side], 256), f32)


def core_sum_kernel(side, grad_ref, momentum_ref, got_ref, out_ref):
    for piece, start, value in local_rows(grad_ref, momentum_ref, side):
        stop = start + value.shape[0]
        out_ref[piece, start:stop] = value + got_ref[piece, start:stop]


def near_sum_kernel(parts_ref, out_ref):
    out_ref[...] = (parts_ref[0] + parts_ref[1]) + (parts_ref[2] + parts_ref[3])


def far_sum_kernel(own_ref, first_ref, third_ref, second_ref, out_ref):
    total = (own_ref[...] + first_ref[...]) + (second_ref[...] + third_ref[...])
    for other in range(4):
        out_ref[other] = total


def join_kernel(mine_ref, other_ref, rows_ref):
    _, _, core = place()
    for side in range(2):

        @pl.when(core == side)
        def _():
            pair = (mine_ref, other_ref) if side == 0 else (other_ref, mine_ref)
            for piece in range(4):
                rows_ref[128 * piece : 128 * piece + ROWS[0]] = pair[0][piece, : ROWS[0]]
                rows_ref[128 * piece + ROWS[0] : 128 * piece + 128] = pair[1][piece, : ROWS[1]]


def gram_kernel(side, rows_ref, out_ref):
    pieces = {}
    for index, block in enumerate(BLOCKS[side]):
        for piece in block:
            if piece not in pieces:
                pieces[piece] = halves(rows_ref[128 * piece : 128 * piece + 128])
        out_ref[128 * index : 128 * index + 128] = mul3(pieces[block[0]], pieces[block[1]], NT)


def tensor_sum_kernel(parts_ref, out_ref):
    total = parts_ref[0]
    for index in range(1, 16):
        total = total + parts_ref[index]
    for index in range(16):
        out_ref[index] = total


def diagonal(start_row, start_column, shape):
    rows = start_row + lax.broadcasted_iota(jnp.int32, shape, 0)
    columns = start_column + lax.broadcasted_iota(jnp.int32, shape, 1)
    return rows == columns


def final_kernel(
    mine_ref, other_ref, rows_ref, weight_ref, new_momentum_ref, new_weight_ref, residual_ref,
    gram_ref, gram_high, gram_low, first_high, first_low, inner_high, inner_low, after_high, after_low,
):
    near, far, core = place()
    tensor = lax.axis_index("tensor")
    spot = pl.multiple_of(near * 128 + far * 32 + core * 16, 16)
    new_momentum_ref[...] = rows_ref[pl.ds(spot, 16)]
    trace = jnp.zeros((128, 128), f32)
    for side in range(2):
        for index, (row, column) in enumerate(BLOCKS[side]):
            start = 128 * index
            block = jnp.where(core == side, mine_ref[start : start + 128], other_ref[start : start + 128])
            gram_ref[128 * row : 128 * row + 128, 128 * column : 128 * column + 128] = block
            if row == column:
                trace = trace + block
            else:
                gram_ref[128 * column : 128 * column + 128, 128 * row : 128 * row + 128] = block.T
    trace = jnp.where(diagonal(0, 0, (128, 128)), trace, 0.0)
    squares = jnp.sum(jnp.sum(trace, axis=0, keepdims=True), axis=1, keepdims=True)
    inverse = 1.0 / (jnp.sqrt(squares) + epsilon)
    gram = (gram_ref[...] * inverse) * inverse
    gram_high[...], gram_low[...] = halves(gram)
    pair = (gram_high[...], gram_low[...])
    unit = jnp.where(diagonal(0, 0, (IN, IN)), f32(quintic_a), f32(0.0))
    first_high[...], first_low[...] = halves(quintic_b * gram + quintic_c * mul3(pair, pair, NN) + unit)
    first_pair = (first_high[...], first_low[...])
    inner_high[...], inner_low[...] = halves(mul3(first_pair, pair, NN))
    after_high[...], after_low[...] = halves(mul3(first_pair, (inner_high[...], inner_low[...]), NN))
    after_pair = (after_high[...], after_low[...])
    block_start = pl.multiple_of(lax.rem(tensor, 4) * 128 + lax.div(tensor, 4) * 32, 16)
    bands = ((spot, 16), (block_start, 32))
    slab = tuple(jnp.concatenate([part[pl.ds(*band)] for band in bands], axis=0) for part in (after_high, after_low))
    units = jnp.concatenate([diagonal(start, 0, (size, IN)) for start, size in bands], axis=0)
    second = quintic_b * (slab[0].astype(f32) + slab[1].astype(f32))
    second = second + quintic_c * mul3(slab, after_pair, NN) + jnp.where(units, f32(quintic_a), f32(0.0))
    second_pair = halves(second)
    own = tuple(part[0:16] for part in second_pair)
    total = mul3(own, first_pair, NN)
    update = mul3(halves(total), halves(rows_ref[...]), NN) * inverse
    scale = learn_rate * 0.2 * float(max(IN, OUT)) ** 0.5
    new_weight_ref[...] = weight_ref[...] * (1.0 - learn_rate * weight_decay) - scale * update
    product = mul3(own, after_pair, NN)
    final = mul3(halves(product), tuple(part[16:48] for part in second_pair), NT)
    identity = diagonal(lax.axis_index("dp") * 16, tensor * 32, (16, 32))
    residual_ref[...] = final - jnp.where(identity, f32(1.0), f32(0.0))


def call(kernel, outs, scratch=(), limit=4 << 20):
    return pl.pallas_call(
        kernel,
        out_shape=tuple(jax.ShapeDtypeStruct(shape, f32) for shape in outs),
        scratch_shapes=list(scratch),
        compiler_params=pltpu.CompilerParams(vmem_limit_bytes=limit),
    )


def exchange(value, axis, groups=None):
    return lax.all_to_all(value, axis, 0, 0, tiled=True, axis_index_groups=groups)


def pad(value, axis, size):
    widths = [(0, size - value.shape[axis] if index == axis else 0) for index in range(value.ndim)]
    return jnp.pad(value, widths)


def sum_replicas(side, gradients, momentum, got):
    parts, part = (4, ROWS[side], 256), (ROWS[side], 256)
    (value,) = call(functools.partial(core_sum_kernel, side), [parts])(gradients, momentum, got)
    (value,) = call(near_sum_kernel, [part])(exchange(value, "dp", NEAR))
    others = [lax.ppermute(value, "dp", pairs) for pairs in FAR[side]]
    (value,) = call(far_sum_kernel, [parts])(value, *others)
    return pad(exchange(value, "dp", NEAR), 1, MOST)


def sum_gram(side, rows):
    tall = 128 * len(BLOCKS[side])
    split = (16, tall // 16, 128)
    (blocks,) = call(functools.partial(gram_kernel, side), [(tall, 128)])(rows)
    (value,) = call(tensor_sum_kernel, [split])(exchange(blocks.reshape(split), "tensor"))
    return pad(exchange(value, "tensor").reshape(tall, 128), 0, TALL)


def per_core(function, *operands):
    first, second = (functools.partial(function, side) for side in range(2))
    return lax.cond(place()[2] == 0, first, second, *operands)


def per_device(gradients, momentum, weight):
    gradients = gradients.reshape(4, 4, 2, 16, 256)
    (send,) = call(send_kernel, [(4, MOST, 256)])(gradients, momentum)
    mine = per_core(sum_replicas, gradients, momentum, lax.ppermute(send, "dp", CORE))
    (rows,) = call(join_kernel, [(IN, 256)])(mine, lax.ppermute(mine, "dp", CORE))
    mine = per_core(sum_gram, rows)
    return call(
        final_kernel,
        [(16, 256), (16, 256), (16, 32)],
        [pltpu.VMEM((IN, IN), f32)] + [pltpu.VMEM((IN, IN), bf16)] * 8,
        limit=24 << 20,
    )(mine, lax.ppermute(mine, "dp", CORE), rows, weight)


def solution(mesh):
    return jax.shard_map(
        per_device,
        mesh=mesh,
        in_specs=(P("dp", None, "tensor"), P("dp", "tensor"), P("dp", "tensor")),
        out_specs=(P("dp", "tensor"), P("dp", "tensor"), P("dp", "tensor")),
        check_vma=False,
    )
```

time: 100 us -> 101 us (1.010)
  blocking collectives: 46.6 us -> 49.1 us
  starting transfers between devices: 36.2 us -> 33.9 us
  Pallas kernels: 5.38 us -> 6.58 us
    all_to_all x4, blocking collectives: 46.6 us -> 49.1 us  [exchange(): lax.all_to_all(value, axis, 0, 0, tiled=True, axis_index_groups=groups)]
    ppermute x5, starting transfers between devices: 27.4 us -> 25.1 us  [the longest x3 16.2 us: sum_replicas(): others = [lax.ppermute(value, 'dp', pairs) for pairs in FAR[side]]]
    pallas_call x6 -> x7, Pallas kernels: 0.54 us -> 1.76 us  [the longest x1 1.05 us: per_device(): send, = call(send_kernel, [(4, MOST, 256)])(gradients, momentum)]
where the time goes in v8:
time: 101 us
  blocking collectives  49.1 us (49%)
  starting transfers between devices  33.9 us (34%)
  waiting for transfers between devices  10.3 us (10%)
  Pallas kernels  6.58 us (7%)
    all_to_all x4, blocking collectives, exchange(): lax.all_to_all(value, axis, 0, 0, tiled=True, axis_index_groups=groups)  49.1 us
    ppermute x3, starting transfers between devices, sum_replicas(): others = [lax.ppermute(value, 'dp', pairs) for pairs in FAR[side]]  16.2 us
    ppermute x1, starting transfers between devices, per_device(): lax.ppermute(send, 'dp', CORE)  8.78 us
    ppermute x3, waiting for transfers between devices, sum_replicas(): others = [lax.ppermute(value, 'dp', pairs) for pairs in FAR[side]]  6.59 us
    ppermute x1, starting transfers between devices, per_device(): rows, = call(join_kernel, [(IN, 256)])(mine, lax.ppermute(mine, 'dp', CORE))  6.58 us
    pallas_call x1, Pallas kernels, per_device(): call(final_kernel, [(16, 256), (16, 256), (16, 32)], [pltpu.VMEM((IN, IN)...  4.82 us
    ppermute x1, starting transfers between devices, per_device(): lax.ppermute(mine, 'dp', CORE)  2.34 us
  transfers between devices with their start and end apart: 6, of which 4 were waited for; matrix products, arithmetic and copies ran while one was open for 0% of the time, Pallas kernels for 0%

profile of v8, /device:TPU:1, one launch (start us, length us, event | category | flops | bytes accessed | tf_op | source)
XLA Modules:
  0.0 100.6 jit_solution(6694592515173210408)
XLA Ops:
  0.6 0.0 copy-start.1
  0.6 1.1 %shard_map.58 = f32[4,64,256]{2,1,0:T(8,128)S(1)} custom-call(bf16[4,4,2,16,256]{4,3,2,1,0:T(8,128)(2,1)} %bitcast.7, f32[16,256]{1,0:T(8,128)} %momentum_ref.1), custom_call_target="tpu_custom_call" | custom-call | tf_op jit(solution)/shard_map/pallas_call | solution.py:220
  1.7 0.0 copy-start.2
  1.7 8.8 %collective-permute-start.6 = (f32[4,64,256]{2,1,0:T(8,128)S(1)}, f32[4,64,256]{2,1,0:T(8,128)S(1)}, u32[]{:S(2)}, u32[]{:S(2)}) collective-permute-start(f32[4,64,256]{2,1,0:T(8,128)S(1)} %shard_map.58), channel_id=1, source_target_pairs={{0,16},{16,0},{32,48},{48,32},{64,80},{80,64},{96,112},{112,96},{1... | collective-permute-start | bytes 786440 | tf_op jit(solution)/shard_map/ppermute | solution.py:221
  10.5 1.1 %collective-permute-done.6 = f32[4,64,256]{2,1,0:T(8,128)S(1)} collective-permute-done((f32[4,64,256]{2,1,0:T(8,128)S(1)}, f32[4,64,256]{2,1,0:T(8,128)S(1)}, u32[]{:S(2)}, u32[]{:S(2)}) %collective-permute-start.6) | collective-permute-done | bytes 262176 | tf_op jit(solution)/shard_map/ppermute | solution.py:221
  11.6 0.0 copy-done.1
  11.6 0.0 copy-done.2
  11.6 43.3 %conditional.2 = (f32[4,64,256]{2,1,0:T(8,128)S(1)}) conditional(s32[]{:T(128)} %convert_element_type.6, (bf16[4,4,2,16,256]{4,3,2,1,0:T(8,128)(2,1)S(1)}, f32[16,256]{1,0:T(8,128)S(1)}, f32[4,64,256]{2,1,0:T(8,128)S(1)}) %tuple.26, (bf16[4,4,2,16,256]{4,3,2,1,0:T(8,128)(2,1)S(1)}, f32[16,256]{1,0:T(8,128)S(1)}, f32[4,64,256]{2,1,0:T(8,128)S(1)}) %tuple.27), branch_computations={%region_0.1_spmd, %region_1.2_spmd} | conditional | bytes 1835136 | solution.py:215
  11.6 0.1 branch_0_fun.5
  11.7 10.7 %all_to_all.32.parts_ref = f32[4,64,256]{2,1,0:T(8,128)S(1)} all-to-all(f32[4,64,256]{2,1,0:T(8,128)S(1)} %branch_0_fun.5), channel_id=1, replica_groups={{0,32,64,96},{16,48,80,112},{128,160,192,224},{144,176,208,240},{256,28..., dimensions={0} | all-to-all | bytes 524288 | tf_op jit(solution)/shard_map/cond/branch_0_fun/all_to_all | solution.py:188
  22.4 9.1 %collective-permute-start.2 = (f32[64,256]{1,0:T(8,128)S(1)}, f32[64,256]{1,0:T(8,128)S(1)}, u32[]{:S(2)}, u32[]{:S(2)}) collective-permute-start(f32[64,256]{1,0:T(8,128)S(1)} %branch_0_fun.6.own_ref), channel_id=1, source_target_pairs={{16,272},{48,304},{80,336},{112,368},{144,400},{176,432},{208,464}... | collective-permute-start | bytes 196616 | tf_op jit(solution)/shard_map/cond/branch_0_fun/ppermute | solution.py:200
  31.5 3.1 %collective-permute-start.1 = (f32[64,256]{1,0:T(8,128)S(1)}, f32[64,256]{1,0:T(8,128)S(1)}, u32[]{:S(2)}, u32[]{:S(2)}) collective-permute-start(f32[64,256]{1,0:T(8,128)S(1)} %branch_0_fun.6.own_ref), channel_id=1, source_target_pairs={{16,400},{48,432},{80,464},{112,496},{144,272},{176,304},{208,336}... | collective-permute-start | bytes 196616 | tf_op jit(solution)/shard_map/cond/branch_0_fun/ppermute | solution.py:200
  34.6 4.0 %collective-permute-start = (f32[64,256]{1,0:T(8,128)S(1)}, f32[64,256]{1,0:T(8,128)S(1)}, u32[]{:S(2)}, u32[]{:S(2)}) collective-permute-start(f32[64,256]{1,0:T(8,128)S(1)} %branch_0_fun.6.own_ref), channel_id=1, source_target_pairs={{16,144},{48,176},{80,208},{112,240},{144,16},{176,48},{208,80},{2... | collective-permute-start | bytes 196616 | tf_op jit(solution)/shard_map/cond/branch_0_fun/ppermute | solution.py:200
  38.6 0.0 collective-permute-done.2.second_ref
  38.6 6.6 %collective-permute-done.1.third_ref = f32[64,256]{1,0:T(8,128)S(1)} collective-permute-done((f32[64,256]{1,0:T(8,128)S(1)}, f32[64,256]{1,0:T(8,128)S(1)}, u32[]{:S(2)}, u32[]{:S(2)}) %collective-permute-start.1) | collective-permute-done | bytes 65568 | tf_op jit(solution)/shard_map/cond/branch_0_fun/ppermute | solution.py:200
  45.2 0.0 collective-permute-done.first_ref
  45.2 9.7 %all_to_all.33 = f32[4,64,256]{2,1,0:T(8,128)S(1)} all-to-all(f32[4,64,256]{2,1,0:T(8,128)S(1)} %branch_0_fun.7), channel_id=1, replica_groups={{0,32,64,96},{16,48,80,112},{128,160,192,224},{144,176,208,240},{256,28..., dimensions={0} | all-to-all | bytes 524288 | tf_op jit(solution)/shard_map/cond/branch_0_fun/all_to_all | solution.py:188
  55.0 6.6 %collective-permute-start.7 = (f32[4,64,256]{2,1,0:T(8,128)S(1)}, f32[4,64,256]{2,1,0:T(8,128)S(1)}, u32[]{:S(2)}, u32[]{:S(2)}) collective-permute-start(f32[4,64,256]{2,1,0:T(8,128)S(1)} %get-tuple-element.29.mine_ref), channel_id=1, source_target_pairs={{0,16},{16,0},{32,48},{48,32},{64,80},{80,64},{96,112},{112,96},{1... | collective-permute-start | bytes 786440 | tf_op jit(solution)/shard_map/ppermute | solution.py:222
  61.5 1.1 %collective-permute-done.7.other_ref = f32[4,64,256]{2,1,0:T(8,128)S(1)} collective-permute-done((f32[4,64,256]{2,1,0:T(8,128)S(1)}, f32[4,64,256]{2,1,0:T(8,128)S(1)}, u32[]{:S(2)}, u32[]{:S(2)}) %collective-permute-start.7) | collective-permute-done | bytes 262176 | tf_op jit(solution)/shard_map/ppermute | solution.py:222
  62.7 0.0 copy-start
  62.7 29.3 %conditional.3 = (f32[896,128]{1,0:T(8,128)S(1)}) conditional(s32[]{:T(128)} %convert_element_type.6, f32[512,256]{1,0:T(8,128)S(1)} %shard_map.59.rows_ref, f32[512,256]{1,0:T(8,128)S(1)} %shard_map.59.rows_ref), branch_computations={%region_2.3_spmd, %region_3.4_spmd} | conditional | bytes 1835016 | solution.py:215
  62.7 0.5 branch_0_fun.8
  63.3 16.3 %all_to_all.36.parts_ref = f32[16,56,128]{2,1,0:T(8,128)S(1)} all-to-all(f32[16,56,128]{2,1,0:T(8,128)S(1)} %bitcast.5), channel_id=1, replica_groups=mesh['dp'=32,'tensor'=16] {'tensor'}, dimensions={0} | all-to-all | bytes 917504 | tf_op jit(solution)/shard_map/cond/branch_0_fun/all_to_all | solution.py:188
  79.7 12.3 %all_to_all.37 = f32[16,56,128]{2,1,0:T(8,128)S(1)} all-to-all(f32[16,56,128]{2,1,0:T(8,128)S(1)} %branch_0_fun.9), channel_id=1, replica_groups=mesh['dp'=32,'tensor'=16] {'tensor'}, dimensions={0} | all-to-all | bytes 917504 | tf_op jit(solution)/shard_map/cond/branch_0_fun/all_to_all | solution.py:188
  92.0 2.3 %collective-permute-start.8 = (f32[896,128]{1,0:T(8,128)S(1)}, f32[896,128]{1,0:T(8,128)S(1)}, u32[]{:S(2)}, u32[]{:S(2)}) collective-permute-start(f32[896,128]{1,0:T(8,128)S(1)} %get-tuple-element.30.mine_ref), channel_id=1, source_target_pairs={{0,16},{16,0},{32,48},{48,32},{64,80},{80,64},{96,112},{112,96},{1... | collective-permute-start | bytes 1376264 | tf_op jit(solution)/shard_map/ppermute | solution.py:229
  94.4 1.4 %collective-permute-done.8.other_ref = f32[896,128]{1,0:T(8,128)S(1)} collective-permute-done((f32[896,128]{1,0:T(8,128)S(1)}, f32[896,128]{1,0:T(8,128)S(1)}, u32[]{:S(2)}, u32[]{:S(2)}) %collective-permute-start.8) | collective-permute-done | bytes 458784 | tf_op jit(solution)/shard_map/ppermute | solution.py:229
  95.8 0.0 copy-done
  95.8 4.8 %shard_map.60 = (f32[16,256]{1,0:T(8,128)}, f32[16,256]{1,0:T(8,128)}, f32[16,32]{1,0:T(8,128)}) custom-call(f32[896,128]{1,0:T(8,128)S(1)} %get-tuple-element.30.mine_ref, f32[896,128]{1,0:T(8,128)S(1)} %collective-permute-done.8.other_ref, f32[512,256]{1,0:T(8,128)S(1)} %shard_map.59.rows_ref, f32[16,256]{1,0:T(8,128)S(1)} %copy-done), custom_call_target="tpu_custom_call" | custom-call | tf_op jit(solution)/shard_map/pallas_call | solution.py:224
  (4 shorter events, 0.1 us)
Async XLA Ops:
  0.6 11.0 %copy-start.1 = (bf16[1,512,256]{2,1,0:T(8,128)(2,1)S(1)}, bf16[1,512,256]{2,1,0:T(8,128)(2,1)}, u32[]{:S(2)}) copy-start(bf16[1,512,256]{2,1,0:T(8,128)(2,1)} %param.7) | copy-start | bytes 786436
  1.7 9.9 %copy-start.2 = (f32[16,256]{1,0:T(8,128)S(1)}, f32[16,256]{1,0:T(8,128)}, u32[]{:S(2)}) copy-start(f32[16,256]{1,0:T(8,128)} %momentum_ref.1) | copy-start | bytes 49156
  1.7 9.9 %collective-permute-start.6 = (f32[4,64,256]{2,1,0:T(8,128)S(1)}, f32[4,64,256]{2,1,0:T(8,128)S(1)}, u32[]{:S(2)}, u32[]{:S(2)}) collective-permute-start(f32[4,64,256]{2,1,0:T(8,128)S(1)} %shard_map.58), channel_id=1, source_target_pairs={{0,16},{16,0},{32,48},{48,32},{64,80},{80,64},{96,112},{112,96},{1... | collective-permute-start | bytes 786440 | tf_op jit(solution)/shard_map/ppermute | solution.py:221
  22.4 16.2 %collective-permute-start.2 = (f32[64,256]{1,0:T(8,128)S(1)}, f32[64,256]{1,0:T(8,128)S(1)}, u32[]{:S(2)}, u32[]{:S(2)}) collective-permute-start(f32[64,256]{1,0:T(8,128)S(1)} %branch_0_fun.6.own_ref), channel_id=1, source_target_pairs={{16,272},{48,304},{80,336},{112,368},{144,400},{176,432},{208,464}... | collective-permute-start | bytes 196616 | tf_op jit(solution)/shard_map/cond/branch_0_fun/ppermute | solution.py:200
  31.5 13.7 %collective-permute-start.1 = (f32[64,256]{1,0:T(8,128)S(1)}, f32[64,256]{1,0:T(8,128)S(1)}, u32[]{:S(2)}, u32[]{:S(2)}) collective-permute-start(f32[64,256]{1,0:T(8,128)S(1)} %branch_0_fun.6.own_ref), channel_id=1, source_target_pairs={{16,400},{48,432},{80,464},{112,496},{144,272},{176,304},{208,336}... | collective-permute-start | bytes 196616 | tf_op jit(solution)/shard_map/cond/branch_0_fun/ppermute | solution.py:200
  34.6 10.6 %collective-permute-start = (f32[64,256]{1,0:T(8,128)S(1)}, f32[64,256]{1,0:T(8,128)S(1)}, u32[]{:S(2)}, u32[]{:S(2)}) collective-permute-start(f32[64,256]{1,0:T(8,128)S(1)} %branch_0_fun.6.own_ref), channel_id=1, source_target_pairs={{16,144},{48,176},{80,208},{112,240},{144,16},{176,48},{208,80},{2... | collective-permute-start | bytes 196616 | tf_op jit(solution)/shard_map/cond/branch_0_fun/ppermute | solution.py:200
  55.0 7.7 %collective-permute-start.7 = (f32[4,64,256]{2,1,0:T(8,128)S(1)}, f32[4,64,256]{2,1,0:T(8,128)S(1)}, u32[]{:S(2)}, u32[]{:S(2)}) collective-permute-start(f32[4,64,256]{2,1,0:T(8,128)S(1)} %get-tuple-element.29.mine_ref), channel_id=1, source_target_pairs={{0,16},{16,0},{32,48},{48,32},{64,80},{80,64},{96,112},{112,96},{1... | collective-permute-start | bytes 786440 | tf_op jit(solution)/shard_map/ppermute | solution.py:222
  62.7 33.1 %copy-start = (f32[16,256]{1,0:T(8,128)S(1)}, f32[16,256]{1,0:T(8,128)}, u32[]{:S(2)}) copy-start(f32[16,256]{1,0:T(8,128)} %weight_ref.1) | copy-start | bytes 49156
  92.0 3.8 %collective-permute-start.8 = (f32[896,128]{1,0:T(8,128)S(1)}, f32[896,128]{1,0:T(8,128)S(1)}, u32[]{:S(2)}, u32[]{:S(2)}) collective-permute-start(f32[896,128]{1,0:T(8,128)S(1)} %get-tuple-element.30.mine_ref), channel_id=1, source_target_pairs={{0,16},{16,0},{32,48},{48,32},{64,80},{80,64},{96,112},{112,96},{1... | collective-permute-start | bytes 1376264 | tf_op jit(solution)/shard_map/ppermute | solution.py:229

commit v9 on v8

--- a/solution.py
+++ b/solution.py
@@ -21,9 +21,9 @@
 f32 = jnp.float32
 bf16 = jnp.bfloat16
 
-ROWS = (64, 64)
+ROWS = (56, 72)
 MOST = max(ROWS)
-BLOCKS = (((0, 0), (0, 1), (1, 1)), ((0, 2), (0, 3), (1, 2), (1, 3), (2, 2), (2, 3), (3, 3)))
+BLOCKS = (((0, 0), (0, 1), (0, 2), (0, 3), (1, 1)), ((1, 2), (1, 3), (2, 2), (2, 3), (3, 3)))
 TALL = 128 * max(len(blocks) for blocks in BLOCKS)
 
 CORE = [(i, i ^ 1) for i in range(32)]

time: 101 us -> 102 us (level)
    ppermute x1, starting transfers between devices: 2.34 us -> 4.62 us  [per_device(): lax.ppermute(mine, 'dp', CORE)]
    ppermute x1, starting transfers between devices: 6.58 us -> 4.97 us  [per_device(): rows, = call(join_kernel, [(IN, 256)])(mine, lax.ppermute(mine, 'dp', CORE))]
  transfers between devices with their start and end apart: 6 -> 6, of which waited for: 4 -> 5; matrix products, arithmetic and copies ran while one was open for 0% -> 0% of each run, Pallas kernels for 0% -> 0%
where the time goes in v9:
time: 102 us; the launch traced here: 101 us
  blocking collectives  48.4 us (47%)
  starting transfers between devices  34.6 us (34%)
  waiting for transfers between devices  10.9 us (11%)
  Pallas kernels  6.46 us (6%)
    all_to_all x4, blocking collectives, exchange(): lax.all_to_all(value, axis, 0, 0, tiled=True, axis_index_groups=groups)  48.4 us
    ppermute x3, starting transfers between devices, sum_replicas(): others = [lax.ppermute(value, 'dp', pairs) for pairs in FAR[side]]  16.2 us
    ppermute x1, starting transfers between devices, per_device(): lax.ppermute(send, 'dp', CORE)  8.79 us
    ppermute x3, waiting for transfers between devices, sum_replicas(): others = [lax.ppermute(value, 'dp', pairs) for pairs in FAR[side]]  7.29 us
    ppermute x1, starting transfers between devices, per_device(): rows, = call(join_kernel, [(IN, 256)])(mine, lax.ppermute(mine, 'dp', CORE))  4.97 us
    pallas_call x1, Pallas kernels, per_device(): call(final_kernel, [(16, 256), (16, 256), (16, 32)], [pltpu.VMEM((IN, IN)...  4.82 us
    ppermute x1, starting transfers between devices, per_device(): lax.ppermute(mine, 'dp', CORE)  4.62 us
  transfers between devices with their start and end apart: 6, of which 5 were waited for; matrix products, arithmetic and copies ran while one was open for 0% of the time, Pallas kernels for 0%

profile of v9, /device:TPU:1, one launch (start us, length us, event | category | flops | bytes accessed | tf_op | source)
XLA Modules:
  0.0 101.2 jit_solution(17303959314872601258)
XLA Ops:
  0.6 0.0 copy-start.1
  0.6 1.0 %shard_map.58 = f32[4,72,256]{2,1,0:T(8,128)S(1)} custom-call(bf16[4,4,2,16,256]{4,3,2,1,0:T(8,128)(2,1)} %bitcast.7, f32[16,256]{1,0:T(8,128)} %momentum_ref.1), custom_call_target="tpu_custom_call" | custom-call | tf_op jit(solution)/shard_map/pallas_call | solution.py:220
  1.7 0.0 copy-start.2
  1.7 8.8 %collective-permute-start.6 = (f32[4,72,256]{2,1,0:T(8,128)S(1)}, f32[4,72,256]{2,1,0:T(8,128)S(1)}, u32[]{:S(2)}, u32[]{:S(2)}) collective-permute-start(f32[4,72,256]{2,1,0:T(8,128)S(1)} %shard_map.58), channel_id=1, source_target_pairs={{0,16},{16,0},{32,48},{48,32},{64,80},{80,64},{96,112},{112,96},{1... | collective-permute-start | bytes 884744 | tf_op jit(solution)/shard_map/ppermute | solution.py:221
  10.5 1.2 %collective-permute-done.6 = f32[4,72,256]{2,1,0:T(8,128)S(1)} collective-permute-done((f32[4,72,256]{2,1,0:T(8,128)S(1)}, f32[4,72,256]{2,1,0:T(8,128)S(1)}, u32[]{:S(2)}, u32[]{:S(2)}) %collective-permute-start.6) | collective-permute-done | bytes 294944 | tf_op jit(solution)/shard_map/ppermute | solution.py:221
  11.7 0.0 copy-done.1
  11.7 0.0 copy-done.2
  11.7 44.8 %conditional.2 = (f32[4,72,256]{2,1,0:T(8,128)S(1)}) conditional(s32[]{:T(128)} %convert_element_type.6, (bf16[4,4,2,16,256]{4,3,2,1,0:T(8,128)(2,1)S(1)}, f32[16,256]{1,0:T(8,128)S(1)}, f32[4,72,256]{2,1,0:T(8,128)S(1)}) %tuple.31, (bf16[4,4,2,16,256]{4,3,2,1,0:T(8,128)(2,1)S(1)}, f32[16,256]{1,0:T(8,128)S(1)}, f32[4,72,256]{2,1,0:T(8,128)S(1)}) %tuple.32), branch_computations={%region_0.1_spmd, %region_1.2_spmd} | conditional | bytes 2130052 | solution.py:215
  11.7 0.1 branch_0_fun.5
  11.8 11.0 %all_to_all.32.parts_ref = f32[4,72,256]{2,1,0:T(8,128)S(1)} all-to-all(f32[4,72,256]{2,1,0:T(8,128)S(1)} %branch_0_fun.5), channel_id=1, replica_groups={{0,32,64,96},{16,48,80,112},{128,160,192,224},{144,176,208,240},{256,28..., dimensions={0} | all-to-all | bytes 589824 | tf_op jit(solution)/shard_map/cond/branch_0_fun/all_to_all | solution.py:188
  22.8 10.3 %collective-permute-start.2 = (f32[72,256]{1,0:T(8,128)S(1)}, f32[72,256]{1,0:T(8,128)S(1)}, u32[]{:S(2)}, u32[]{:S(2)}) collective-permute-start(f32[72,256]{1,0:T(8,128)S(1)} %branch_0_fun.6.own_ref), channel_id=1, source_target_pairs={{16,272},{48,304},{80,336},{112,368},{144,400},{176,432},{208,464}... | collective-permute-start | bytes 221192 | tf_op jit(solution)/shard_map/cond/branch_0_fun/ppermute | solution.py:200
  33.1 3.1 %collective-permute-start.1 = (f32[72,256]{1,0:T(8,128)S(1)}, f32[72,256]{1,0:T(8,128)S(1)}, u32[]{:S(2)}, u32[]{:S(2)}) collective-permute-start(f32[72,256]{1,0:T(8,128)S(1)} %branch_0_fun.6.own_ref), channel_id=1, source_target_pairs={{16,400},{48,432},{80,464},{112,496},{144,272},{176,304},{208,336}... | collective-permute-start | bytes 221192 | tf_op jit(solution)/shard_map/cond/branch_0_fun/ppermute | solution.py:200
  36.2 2.9 %collective-permute-start = (f32[72,256]{1,0:T(8,128)S(1)}, f32[72,256]{1,0:T(8,128)S(1)}, u32[]{:S(2)}, u32[]{:S(2)}) collective-permute-start(f32[72,256]{1,0:T(8,128)S(1)} %branch_0_fun.6.own_ref), channel_id=1, source_target_pairs={{16,144},{48,176},{80,208},{112,240},{144,16},{176,48},{208,80},{2... | collective-permute-start | bytes 221192 | tf_op jit(solution)/shard_map/cond/branch_0_fun/ppermute | solution.py:200
  39.0 0.0 collective-permute-done.2.second_ref
  39.0 6.5 %collective-permute-done.1.third_ref = f32[72,256]{1,0:T(8,128)S(1)} collective-permute-done((f32[72,256]{1,0:T(8,128)S(1)}, f32[72,256]{1,0:T(8,128)S(1)}, u32[]{:S(2)}, u32[]{:S(2)}) %collective-permute-start.1) | collective-permute-done | bytes 73760 | tf_op jit(solution)/shard_map/cond/branch_0_fun/ppermute | solution.py:200
  45.5 0.8 collective-permute-done.first_ref
  46.4 10.2 %all_to_all.33 = f32[4,72,256]{2,1,0:T(8,128)S(1)} all-to-all(f32[4,72,256]{2,1,0:T(8,128)S(1)} %branch_0_fun.7), channel_id=1, replica_groups={{0,32,64,96},{16,48,80,112},{128,160,192,224},{144,176,208,240},{256,28..., dimensions={0} | all-to-all | bytes 589824 | tf_op jit(solution)/shard_map/cond/branch_0_fun/all_to_all | solution.py:188
  56.5 5.0 %collective-permute-start.7 = (f32[4,72,256]{2,1,0:T(8,128)S(1)}, f32[4,72,256]{2,1,0:T(8,128)S(1)}, u32[]{:S(2)}, u32[]{:S(2)}) collective-permute-start(f32[4,72,256]{2,1,0:T(8,128)S(1)} %get-tuple-element.31.mine_ref), channel_id=1, source_target_pairs={{0,16},{16,0},{32,48},{48,32},{64,80},{80,64},{96,112},{112,96},{1... | collective-permute-start | bytes 884744 | tf_op jit(solution)/shard_map/ppermute | solution.py:222
  61.5 1.2 %collective-permute-done.7.other_ref = f32[4,72,256]{2,1,0:T(8,128)S(1)} collective-permute-done((f32[4,72,256]{2,1,0:T(8,128)S(1)}, f32[4,72,256]{2,1,0:T(8,128)S(1)}, u32[]{:S(2)}, u32[]{:S(2)}) %collective-permute-start.7) | collective-permute-done | bytes 294944 | tf_op jit(solution)/shard_map/ppermute | solution.py:222
  62.7 0.0 copy-start
  62.8 27.7 %conditional.3 = (f32[640,128]{1,0:T(8,128)S(1)}) conditional(s32[]{:T(128)} %convert_element_type.6, f32[512,256]{1,0:T(8,128)S(1)} %shard_map.59.rows_ref, f32[512,256]{1,0:T(8,128)S(1)} %shard_map.59.rows_ref), branch_computations={%region_2.3_spmd, %region_3.4_spmd} | conditional | bytes 1310728 | solution.py:215
  62.8 0.4 branch_0_fun.8
  63.2 16.5 %all_to_all.36.parts_ref = f32[16,40,128]{2,1,0:T(8,128)S(1)} all-to-all(f32[16,40,128]{2,1,0:T(8,128)S(1)} %bitcast.5), channel_id=1, replica_groups=mesh['dp'=32,'tensor'=16] {'tensor'}, dimensions={0} | all-to-all | bytes 655360 | tf_op jit(solution)/shard_map/cond/branch_0_fun/all_to_all | solution.py:188
  79.8 10.7 %all_to_all.37 = f32[16,40,128]{2,1,0:T(8,128)S(1)} all-to-all(f32[16,40,128]{2,1,0:T(8,128)S(1)} %branch_0_fun.9), channel_id=1, replica_groups=mesh['dp'=32,'tensor'=16] {'tensor'}, dimensions={0} | all-to-all | bytes 655360 | tf_op jit(solution)/shard_map/cond/branch_0_fun/all_to_all | solution.py:188
  90.5 4.6 %collective-permute-start.8 = (f32[640,128]{1,0:T(8,128)S(1)}, f32[640,128]{1,0:T(8,128)S(1)}, u32[]{:S(2)}, u32[]{:S(2)}) collective-permute-start(f32[640,128]{1,0:T(8,128)S(1)} %get-tuple-element.32.mine_ref), channel_id=1, source_target_pairs={{0,16},{16,0},{32,48},{48,32},{64,80},{80,64},{96,112},{112,96},{1... | collective-permute-start | bytes 983048 | tf_op jit(solution)/shard_map/ppermute | solution.py:229
  95.1 1.2 %collective-permute-done.8.other_ref = f32[640,128]{1,0:T(8,128)S(1)} collective-permute-done((f32[640,128]{1,0:T(8,128)S(1)}, f32[640,128]{1,0:T(8,128)S(1)}, u32[]{:S(2)}, u32[]{:S(2)}) %collective-permute-start.8) | collective-permute-done | bytes 327712 | tf_op jit(solution)/shard_map/ppermute | solution.py:229
  96.3 0.0 copy-done
  96.3 4.8 %shard_map.60 = (f32[16,256]{1,0:T(8,128)}, f32[16,256]{1,0:T(8,128)}, f32[16,32]{1,0:T(8,128)}) custom-call(f32[640,128]{1,0:T(8,128)S(1)} %get-tuple-element.32.mine_ref, f32[640,128]{1,0:T(8,128)S(1)} %collective-permute-done.8.other_ref, f32[512,256]{1,0:T(8,128)S(1)} %shard_map.59.rows_ref, f32[16,256]{1,0:T(8,128)S(1)} %copy-done), custom_call_target="tpu_custom_call" | custom-call | tf_op jit(solution)/shard_map/pallas_call | solution.py:224
  (4 shorter events, 0.1 us)
Async XLA Ops:
  0.6 11.1 %copy-start.1 = (bf16[1,512,256]{2,1,0:T(8,128)(2,1)S(1)}, bf16[1,512,256]{2,1,0:T(8,128)(2,1)}, u32[]{:S(2)}) copy-start(bf16[1,512,256]{2,1,0:T(8,128)(2,1)} %param.7) | copy-start | bytes 786436
  1.7 10.0 %copy-start.2 = (f32[16,256]{1,0:T(8,128)S(1)}, f32[16,256]{1,0:T(8,128)}, u32[]{:S(2)}) copy-start(f32[16,256]{1,0:T(8,128)} %momentum_ref.1) | copy-start | bytes 49156
  1.7 10.0 %collective-permute-start.6 = (f32[4,72,256]{2,1,0:T(8,128)S(1)}, f32[4,72,256]{2,1,0:T(8,128)S(1)}, u32[]{:S(2)}, u32[]{:S(2)}) collective-permute-start(f32[4,72,256]{2,1,0:T(8,128)S(1)} %shard_map.58), channel_id=1, source_target_pairs={{0,16},{16,0},{32,48},{48,32},{64,80},{80,64},{96,112},{112,96},{1... | collective-permute-start | bytes 884744 | tf_op jit(solution)/shard_map/ppermute | solution.py:221
  22.8 16.2 %collective-permute-start.2 = (f32[72,256]{1,0:T(8,128)S(1)}, f32[72,256]{1,0:T(8,128)S(1)}, u32[]{:S(2)}, u32[]{:S(2)}) collective-permute-start(f32[72,256]{1,0:T(8,128)S(1)} %branch_0_fun.6.own_ref), channel_id=1, source_target_pairs={{16,272},{48,304},{80,336},{112,368},{144,400},{176,432},{208,464}... | collective-permute-start | bytes 221192 | tf_op jit(solution)/shard_map/cond/branch_0_fun/ppermute | solution.py:200
  33.1 12.4 %collective-permute-start.1 = (f32[72,256]{1,0:T(8,128)S(1)}, f32[72,256]{1,0:T(8,128)S(1)}, u32[]{:S(2)}, u32[]{:S(2)}) collective-permute-start(f32[72,256]{1,0:T(8,128)S(1)} %branch_0_fun.6.own_ref), channel_id=1, source_target_pairs={{16,400},{48,432},{80,464},{112,496},{144,272},{176,304},{208,336}... | collective-permute-start | bytes 221192 | tf_op jit(solution)/shard_map/cond/branch_0_fun/ppermute | solution.py:200
  36.2 10.2 %collective-permute-start = (f32[72,256]{1,0:T(8,128)S(1)}, f32[72,256]{1,0:T(8,128)S(1)}, u32[]{:S(2)}, u32[]{:S(2)}) collective-permute-start(f32[72,256]{1,0:T(8,128)S(1)} %branch_0_fun.6.own_ref), channel_id=1, source_target_pairs={{16,144},{48,176},{80,208},{112,240},{144,16},{176,48},{208,80},{2... | collective-permute-start | bytes 221192 | tf_op jit(solution)/shard_map/cond/branch_0_fun/ppermute | solution.py:200
  56.5 6.2 %collective-permute-start.7 = (f32[4,72,256]{2,1,0:T(8,128)S(1)}, f32[4,72,256]{2,1,0:T(8,128)S(1)}, u32[]{:S(2)}, u32[]{:S(2)}) collective-permute-start(f32[4,72,256]{2,1,0:T(8,128)S(1)} %get-tuple-element.31.mine_ref), channel_id=1, source_target_pairs={{0,16},{16,0},{32,48},{48,32},{64,80},{80,64},{96,112},{112,96},{1... | collective-permute-start | bytes 884744 | tf_op jit(solution)/shard_map/ppermute | solution.py:222
  62.7 33.6 %copy-start = (f32[16,256]{1,0:T(8,128)S(1)}, f32[16,256]{1,0:T(8,128)}, u32[]{:S(2)}) copy-start(f32[16,256]{1,0:T(8,128)} %weight_ref.1) | copy-start | bytes 49156
  90.5 5.9 %collective-permute-start.8 = (f32[640,128]{1,0:T(8,128)S(1)}, f32[640,128]{1,0:T(8,128)S(1)}, u32[]{:S(2)}, u32[]{:S(2)}) collective-permute-start(f32[640,128]{1,0:T(8,128)S(1)} %get-tuple-element.32.mine_ref), channel_id=1, source_target_pairs={{0,16},{16,0},{32,48},{48,32},{64,80},{80,64},{96,112},{112,96},{1... | collective-permute-start | bytes 983048 | tf_op jit(solution)/shard_map/ppermute | solution.py:229

commit v10 on v6

--- a/solution.py
+++ b/solution.py
@@ -21,7 +21,7 @@
 
 CORE = [(i, i ^ 1) for i in range(32)]
 NEAR = [[8 * far + 2 * near + core for near in range(4)] for far in range(4) for core in range(2)]
-FAR = [[(i, i ^ (8 * step)) for i in range(32)] for step in (1, 3, 2)]
+FAR = [[(i, i ^ (8 * steps[i % 2])) for i in range(32)] for steps in ((1, 3), (3, 1), (2, 2))]
 
 NT = (((1,), (1,)), ((), ()))
 NN = (((1,), (0,)), ((), ()))
@@ -64,9 +64,12 @@
         out_ref[far] = total + jnp.where(mine == far, f32(decay_rate), f32(0.0)) * momentum_ref[...]
 
 
-def far_sum_kernel(own_ref, first_ref, third_ref, second_ref, out_ref):
+def far_sum_kernel(own_ref, last_ref, middle_ref, second_ref, out_ref):
+    _, _, core = place()
     for far in range(4):
-        total = (own_ref[far] + first_ref[far]) + (second_ref[far] + third_ref[far])
+        first = jnp.where(core == 0, last_ref[far], middle_ref[far])
+        third = jnp.where(core == 0, middle_ref[far], last_ref[far])
+        total = (own_ref[far] + first) + (second_ref[far] + third)
         for other in range(4):
             out_ref[other, far] = total
 

time: 100 us -> 102 us (1.020)
  blocking collectives: 46.6 us -> 49.3 us
  starting transfers between devices: 36.2 us -> 34.3 us
    all_to_all x4, blocking collectives: 46.6 us -> 49.3 us  [exchange(): lax.all_to_all(value, axis, 0, 0, tiled=True, axis_index_groups=groups)]
    ppermute x2, starting transfers between devices: 11.2 us -> 9.3 us  [per_device(): other = lax.ppermute(mine, 'dp', CORE)]
  transfers between devices with their start and end apart: 6 -> 6, of which waited for: 4 -> 5; matrix products, arithmetic and copies ran while one was open for 0% -> 0% of each run, Pallas kernels for 0% -> 0%
where the time goes in v10:
time: 102 us; the launch traced here: 101 us
  blocking collectives  49.3 us (48%)
  starting transfers between devices  34.3 us (34%)
  waiting for transfers between devices  10.7 us (10%)
  Pallas kernels  5.38 us (5%)
    all_to_all x4, blocking collectives, exchange(): lax.all_to_all(value, axis, 0, 0, tiled=True, axis_index_groups=groups)  49.3 us
    ppermute x3, starting transfers between devices, per_device(): others = [lax.ppermute(parts, 'dp', pairs) for pairs in FAR]  16.2 us
    ppermute x2, starting transfers between devices, per_device(): other = lax.ppermute(mine, 'dp', CORE)  9.3 us
    ppermute x1, starting transfers between devices, per_device(): lax.ppermute(send, 'dp', CORE)  8.79 us
    ppermute x3, waiting for transfers between devices, per_device(): others = [lax.ppermute(parts, 'dp', pairs) for pairs in FAR]  7.23 us
    pallas_call x1, Pallas kernels, per_device(): call(final_kernel, [(16, 256), (16, 256), (16, 32)], [pltpu.VMEM((IN, IN)...  4.83 us
    ppermute x2, waiting for transfers between devices, per_device(): other = lax.ppermute(mine, 'dp', CORE)  2.37 us
  transfers between devices with their start and end apart: 6, of which 5 were waited for; matrix products, arithmetic and copies ran while one was open for 0% of the time, Pallas kernels for 0%

profile of v10, /device:TPU:1, one launch (start us, length us, event | category | flops | bytes accessed | tf_op | source)
XLA Modules:
  0.0 101.4 jit_solution(9671577455526364468)
XLA Ops:
  0.6 0.0 copy-start
  0.6 0.9 copy-done
  1.6 8.8 %collective-permute-start = (f32[4,4,16,256]{3,2,1,0:T(8,128)S(1)}, f32[4,4,16,256]{3,2,1,0:T(8,128)S(1)}, u32[]{:S(2)}, u32[]{:S(2)}) collective-permute-start(f32[4,4,16,256]{3,2,1,0:T(8,128)S(1)} %shard_map.58), channel_id=1, source_target_pairs={{0,16},{16,0},{32,48},{48,32},{64,80},{80,64},{96,112},{112,96},{1... | collective-permute-start | bytes 786440 | tf_op jit(solution)/shard_map/ppermute | solution.py:173
  10.4 1.1 %collective-permute-done.got_ref = f32[4,4,16,256]{3,2,1,0:T(8,128)S(1)} collective-permute-done((f32[4,4,16,256]{3,2,1,0:T(8,128)S(1)}, f32[4,4,16,256]{3,2,1,0:T(8,128)S(1)}, u32[]{:S(2)}, u32[]{:S(2)}) %collective-permute-start) | collective-permute-done | bytes 262176 | tf_op jit(solution)/shard_map/ppermute | solution.py:173
  11.6 0.0 copy-start.2
  11.6 10.7 %all_to_all.20.parts_ref = f32[4,4,16,256]{3,2,1,0:T(8,128)S(1)} all-to-all(f32[4,4,16,256]{3,2,1,0:T(8,128)S(1)} %shard_map.59), channel_id=1, replica_groups={{0,32,64,96},{16,48,80,112},{128,160,192,224},{144,176,208,240},{256,28..., dimensions={0} | all-to-all | bytes 524288 | tf_op jit(solution)/shard_map/all_to_all | solution.py:166
  22.2 0.0 copy-done.2
  22.3 9.1 %collective-permute-start.3 = (f32[4,16,256]{2,1,0:T(8,128)S(1)}, f32[4,16,256]{2,1,0:T(8,128)S(1)}, u32[]{:S(2)}, u32[]{:S(2)}) collective-permute-start(f32[4,16,256]{2,1,0:T(8,128)S(1)} %shard_map.60.own_ref), channel_id=1, source_target_pairs={{0,256},{16,272},{32,288},{48,304},{64,320},{80,336},{96,352},{112... | collective-permute-start | bytes 196616 | tf_op jit(solution)/shard_map/ppermute | solution.py:175
  31.4 4.0 %collective-permute-start.2 = (f32[4,16,256]{2,1,0:T(8,128)S(1)}, f32[4,16,256]{2,1,0:T(8,128)S(1)}, u32[]{:S(2)}, u32[]{:S(2)}) collective-permute-start(f32[4,16,256]{2,1,0:T(8,128)S(1)} %shard_map.60.own_ref), channel_id=1, source_target_pairs={{0,384},{16,144},{32,416},{48,176},{64,448},{80,208},{96,480},{112... | collective-permute-start | bytes 196616 | tf_op jit(solution)/shard_map/ppermute | solution.py:175
  35.4 3.0 %collective-permute-start.1 = (f32[4,16,256]{2,1,0:T(8,128)S(1)}, f32[4,16,256]{2,1,0:T(8,128)S(1)}, u32[]{:S(2)}, u32[]{:S(2)}) collective-permute-start(f32[4,16,256]{2,1,0:T(8,128)S(1)} %shard_map.60.own_ref), channel_id=1, source_target_pairs={{0,128},{16,400},{32,160},{48,432},{64,192},{80,464},{96,224},{112... | collective-permute-start | bytes 196616 | tf_op jit(solution)/shard_map/ppermute | solution.py:175
  38.5 0.0 collective-permute-done.3.second_ref
  38.5 5.5 %collective-permute-done.2.middle_ref = f32[4,16,256]{2,1,0:T(8,128)S(1)} collective-permute-done((f32[4,16,256]{2,1,0:T(8,128)S(1)}, f32[4,16,256]{2,1,0:T(8,128)S(1)}, u32[]{:S(2)}, u32[]{:S(2)}) %collective-permute-start.2) | collective-permute-done | bytes 65568 | tf_op jit(solution)/shard_map/ppermute | solution.py:175
  44.0 1.7 %collective-permute-done.1.last_ref = f32[4,16,256]{2,1,0:T(8,128)S(1)} collective-permute-done((f32[4,16,256]{2,1,0:T(8,128)S(1)}, f32[4,16,256]{2,1,0:T(8,128)S(1)}, u32[]{:S(2)}, u32[]{:S(2)}) %collective-permute-start.1) | collective-permute-done | bytes 65568 | tf_op jit(solution)/shard_map/ppermute | solution.py:175
  45.8 12.9 %all_to_all.21 = f32[4,4,16,256]{3,2,1,0:T(8,128)S(1)} all-to-all(f32[4,4,16,256]{3,2,1,0:T(8,128)S(1)} %shard_map.61), channel_id=1, replica_groups={{0,32,64,96},{16,48,80,112},{128,160,192,224},{144,176,208,240},{256,28..., dimensions={0} | all-to-all | bytes 524288 | tf_op jit(solution)/shard_map/all_to_all | solution.py:166
  58.6 4.7 %collective-permute-start.4 = (f32[256,256]{1,0:T(8,128)S(1)}, f32[256,256]{1,0:T(8,128)S(1)}, u32[]{:S(2)}, u32[]{:S(2)}) collective-permute-start(f32[256,256]{1,0:T(8,128)S(1)} %bitcast.8), channel_id=1, source_target_pairs={{0,16},{16,0},{32,48},{48,32},{64,80},{80,64},{96,112},{112,96},{1... | collective-permute-start | bytes 786440 | tf_op jit(solution)/shard_map/ppermute | solution.py:178
  63.3 1.1 %collective-permute-done.4.other_ref = f32[256,256]{1,0:T(8,128)S(1)} collective-permute-done((f32[256,256]{1,0:T(8,128)S(1)}, f32[256,256]{1,0:T(8,128)S(1)}, u32[]{:S(2)}, u32[]{:S(2)}) %collective-permute-start.4) | collective-permute-done | bytes 262176 | tf_op jit(solution)/shard_map/ppermute | solution.py:178
  64.5 0.4 shard_map.62
  64.9 15.1 %all_to_all.22.parts_ref = f32[16,40,128]{2,1,0:T(8,128)S(1)} all-to-all(f32[16,40,128]{2,1,0:T(8,128)S(1)} %bitcast.10), channel_id=1, replica_groups=mesh['dp'=32,'tensor'=16] {'tensor'}, dimensions={0} | all-to-all | bytes 655360 | tf_op jit(solution)/shard_map/all_to_all | solution.py:166
  80.0 0.0 copy-start.1
  80.0 10.7 %all_to_all.23 = f32[16,40,128]{2,1,0:T(8,128)S(1)} all-to-all(f32[16,40,128]{2,1,0:T(8,128)S(1)} %shard_map.63), channel_id=1, replica_groups=mesh['dp'=32,'tensor'=16] {'tensor'}, dimensions={0} | all-to-all | bytes 655360 | tf_op jit(solution)/shard_map/all_to_all | solution.py:166
  90.8 4.6 %collective-permute-start.5 = (f32[640,128]{1,0:T(8,128)S(1)}, f32[640,128]{1,0:T(8,128)S(1)}, u32[]{:S(2)}, u32[]{:S(2)}) collective-permute-start(f32[640,128]{1,0:T(8,128)S(1)} %bitcast.4), channel_id=1, source_target_pairs={{0,16},{16,0},{32,48},{48,32},{64,80},{80,64},{96,112},{112,96},{1... | collective-permute-start | bytes 983048 | tf_op jit(solution)/shard_map/ppermute | solution.py:182
  95.4 1.2 %collective-permute-done.5.other_ref = f32[640,128]{1,0:T(8,128)S(1)} collective-permute-done((f32[640,128]{1,0:T(8,128)S(1)}, f32[640,128]{1,0:T(8,128)S(1)}, u32[]{:S(2)}, u32[]{:S(2)}) %collective-permute-start.5) | collective-permute-done | bytes 327712 | tf_op jit(solution)/shard_map/ppermute | solution.py:182
  96.6 0.0 copy-done.1
  96.6 4.8 %shard_map.64 = (f32[16,256]{1,0:T(8,128)}, f32[16,256]{1,0:T(8,128)}, f32[16,32]{1,0:T(8,128)}) custom-call(f32[640,128]{1,0:T(8,128)S(1)} %bitcast.5, f32[640,128]{1,0:T(8,128)S(1)} %collective-permute-done.5.other_ref, f32[2,256,256]{2,1,0:T(8,128)S(1)} %get-tuple-element.6.rows_ref, f32[16,256]{1,0:T(8,128)S(1)} %copy-done.1), custom_call_target="tpu_custom_call" | custom-call | tf_op jit(solution)/shard_map/pallas_call | solution.py:183
  (5 shorter events, 0.1 us)
Async XLA Ops:
  0.6 1.0 copy-start
  1.6 9.9 %collective-permute-start = (f32[4,4,16,256]{3,2,1,0:T(8,128)S(1)}, f32[4,4,16,256]{3,2,1,0:T(8,128)S(1)}, u32[]{:S(2)}, u32[]{:S(2)}) collective-permute-start(f32[4,4,16,256]{3,2,1,0:T(8,128)S(1)} %shard_map.58), channel_id=1, source_target_pairs={{0,16},{16,0},{32,48},{48,32},{64,80},{80,64},{96,112},{112,96},{1... | collective-permute-start | bytes 786440 | tf_op jit(solution)/shard_map/ppermute | solution.py:173
  11.6 10.7 %copy-start.2 = (f32[16,256]{1,0:T(8,128)S(1)}, f32[16,256]{1,0:T(8,128)}, u32[]{:S(2)}) copy-start(f32[16,256]{1,0:T(8,128)} %momentum_ref.1) | copy-start | bytes 49156
  22.3 16.2 %collective-permute-start.3 = (f32[4,16,256]{2,1,0:T(8,128)S(1)}, f32[4,16,256]{2,1,0:T(8,128)S(1)}, u32[]{:S(2)}, u32[]{:S(2)}) collective-permute-start(f32[4,16,256]{2,1,0:T(8,128)S(1)} %shard_map.60.own_ref), channel_id=1, source_target_pairs={{0,256},{16,272},{32,288},{48,304},{64,320},{80,336},{96,352},{112... | collective-permute-start | bytes 196616 | tf_op jit(solution)/shard_map/ppermute | solution.py:175
  31.4 12.6 %collective-permute-start.2 = (f32[4,16,256]{2,1,0:T(8,128)S(1)}, f32[4,16,256]{2,1,0:T(8,128)S(1)}, u32[]{:S(2)}, u32[]{:S(2)}) collective-permute-start(f32[4,16,256]{2,1,0:T(8,128)S(1)} %shard_map.60.own_ref), channel_id=1, source_target_pairs={{0,384},{16,144},{32,416},{48,176},{64,448},{80,208},{96,480},{112... | collective-permute-start | bytes 196616 | tf_op jit(solution)/shard_map/ppermute | solution.py:175
  35.4 10.3 %collective-permute-start.1 = (f32[4,16,256]{2,1,0:T(8,128)S(1)}, f32[4,16,256]{2,1,0:T(8,128)S(1)}, u32[]{:S(2)}, u32[]{:S(2)}) collective-permute-start(f32[4,16,256]{2,1,0:T(8,128)S(1)} %shard_map.60.own_ref), channel_id=1, source_target_pairs={{0,128},{16,400},{32,160},{48,432},{64,192},{80,464},{96,224},{112... | collective-permute-start | bytes 196616 | tf_op jit(solution)/shard_map/ppermute | solution.py:175
  58.6 5.9 %collective-permute-start.4 = (f32[256,256]{1,0:T(8,128)S(1)}, f32[256,256]{1,0:T(8,128)S(1)}, u32[]{:S(2)}, u32[]{:S(2)}) collective-permute-start(f32[256,256]{1,0:T(8,128)S(1)} %bitcast.8), channel_id=1, source_target_pairs={{0,16},{16,0},{32,48},{48,32},{64,80},{80,64},{96,112},{112,96},{1... | collective-permute-start | bytes 786440 | tf_op jit(solution)/shard_map/ppermute | solution.py:178
  80.0 16.6 %copy-start.1 = (f32[16,256]{1,0:T(8,128)S(1)}, f32[16,256]{1,0:T(8,128)}, u32[]{:S(2)}) copy-start(f32[16,256]{1,0:T(8,128)} %weight_ref.1) | copy-start | bytes 49156
  90.8 5.8 %collective-permute-start.5 = (f32[640,128]{1,0:T(8,128)S(1)}, f32[640,128]{1,0:T(8,128)S(1)}, u32[]{:S(2)}, u32[]{:S(2)}) collective-permute-start(f32[640,128]{1,0:T(8,128)S(1)} %bitcast.4), channel_id=1, source_target_pairs={{0,16},{16,0},{32,48},{48,32},{64,80},{80,64},{96,112},{112,96},{1... | collective-permute-start | bytes 983048 | tf_op jit(solution)/shard_map/ppermute | solution.py:182

commit v11 on v6

--- a/solution.py
+++ b/solution.py
@@ -21,7 +21,7 @@
 
 CORE = [(i, i ^ 1) for i in range(32)]
 NEAR = [[8 * far + 2 * near + core for near in range(4)] for far in range(4) for core in range(2)]
-FAR = [[(i, i ^ (8 * step)) for i in range(32)] for step in (1, 3, 2)]
+FAR = [[(i, i ^ (8 * steps[i % 2])) for i in range(32)] for steps in ((1, 3), (3, 1))]
 
 NT = (((1,), (1,)), ((), ()))
 NN = (((1,), (0,)), ((), ()))
@@ -64,9 +64,9 @@
         out_ref[far] = total + jnp.where(mine == far, f32(decay_rate), f32(0.0)) * momentum_ref[...]
 
 
-def far_sum_kernel(own_ref, first_ref, third_ref, second_ref, out_ref):
+def far_sum_kernel(own_ref, other_ref, out_ref):
     for far in range(4):
-        total = (own_ref[far] + first_ref[far]) + (second_ref[far] + third_ref[far])
+        total = own_ref[far] + other_ref[far]
         for other in range(4):
             out_ref[other, far] = total
 
@@ -169,8 +169,8 @@
     (send,) = call(send_kernel, [chunks])(gradients)
     (parts,) = call(core_sum_kernel, [chunks])(gradients, lax.ppermute(send, "dp", CORE))
     (parts,) = call(near_sum_kernel, [chunks[1:]])(exchange(parts, "dp", NEAR), momentum)
-    others = [lax.ppermute(parts, "dp", pairs) for pairs in FAR]
-    (spread,) = call(far_sum_kernel, [chunks])(parts, *others)
+    parts = parts + lax.ppermute(parts, "dp", FAR[0])
+    (spread,) = call(far_sum_kernel, [chunks])(parts, lax.ppermute(parts, "dp", FAR[1]))
     mine = exchange(spread, "dp", NEAR).reshape(256, 256)
     other = lax.ppermute(mine, "dp", CORE)
     blocks, rows = call(gram_kernel, [(640, 128), (2, 256, 256)], limit=8 << 20)(mine, other)

time: 100 us -> 95.9 us (0.959)
  starting transfers between devices: 36.2 us -> 32.8 us
  blocking collectives: 46.6 us -> 44.5 us
    ppermute x3 -> x2, starting transfers between devices: 16.2 us -> 11.6 us  [the longest x1 6.16 us: per_device(): parts = parts + lax.ppermute(parts, 'dp', FAR[0])]
    all_to_all x4, blocking collectives: 46.6 us -> 44.5 us  [exchange(): lax.all_to_all(value, axis, 0, 0, tiled=True, axis_index_groups=groups)]
    ppermute x2, starting transfers between devices: 11.2 us -> 12.5 us  [per_device(): other = lax.ppermute(mine, 'dp', CORE)]
    ppermute x3 -> x2, waiting for transfers between devices: 6.6 us -> 7.51 us  [the longest x1 4.75 us: per_device(): lax.ppermute(parts, 'dp', FAR[1])]
  transfers between devices with their start and end apart: 6 -> 5, of which waited for: 4 -> 5; matrix products, arithmetic and copies ran while one was open for 0% -> 0% of each run, Pallas kernels for 0% -> 0%
where the time goes in v11:
time: 95.9 us; the launch traced here: 95.4 us
  blocking collectives  44.5 us (46%)
  starting transfers between devices  32.8 us (34%)
  waiting for transfers between devices  11 us (11%)
  Pallas kernels  5.37 us (6%)
  local copies, waits for them, and re-layouts  0.96 us (1%)
    all_to_all x4, blocking collectives, exchange(): lax.all_to_all(value, axis, 0, 0, tiled=True, axis_index_groups=groups)  44.5 us
    ppermute x2, starting transfers between devices, per_device(): other = lax.ppermute(mine, 'dp', CORE)  12.5 us
    ppermute x1, starting transfers between devices, per_device(): lax.ppermute(send, 'dp', CORE)  8.79 us
    ppermute x1, starting transfers between devices, per_device(): parts = parts + lax.ppermute(parts, 'dp', FAR[0])  6.16 us
    ppermute x1, starting transfers between devices, per_device(): lax.ppermute(parts, 'dp', FAR[1])  5.42 us
    pallas_call x1, Pallas kernels, per_device(): call(final_kernel, [(16, 256), (16, 256), (16, 32)], [pltpu.VMEM((IN, IN)...  4.83 us
    ppermute x1, waiting for transfers between devices, per_device(): lax.ppermute(parts, 'dp', FAR[1])  4.75 us
    ppermute x1, waiting for transfers between devices, per_device(): parts = parts + lax.ppermute(parts, 'dp', FAR[0])  2.75 us
  transfers between devices with their start and end apart: 5, of which 5 were waited for; matrix products, arithmetic and copies ran while one was open for 0% of the time, Pallas kernels for 0%

profile of v11, /device:TPU:1, one launch (start us, length us, event | category | flops | bytes accessed | tf_op | source)
XLA Modules:
  0.0 95.4 jit_solution(200872641336226226)
XLA Ops:
  0.6 0.0 copy-start
  0.6 0.9 copy-done
  1.6 8.8 %collective-permute-start = (f32[4,4,16,256]{3,2,1,0:T(8,128)S(1)}, f32[4,4,16,256]{3,2,1,0:T(8,128)S(1)}, u32[]{:S(2)}, u32[]{:S(2)}) collective-permute-start(f32[4,4,16,256]{3,2,1,0:T(8,128)S(1)} %shard_map.58), channel_id=1, source_target_pairs={{0,16},{16,0},{32,48},{48,32},{64,80},{80,64},{96,112},{112,96},{1... | collective-permute-start | bytes 786440 | tf_op jit(solution)/shard_map/ppermute | solution.py:170
  10.4 1.1 %collective-permute-done.got_ref = f32[4,4,16,256]{3,2,1,0:T(8,128)S(1)} collective-permute-done((f32[4,4,16,256]{3,2,1,0:T(8,128)S(1)}, f32[4,4,16,256]{3,2,1,0:T(8,128)S(1)}, u32[]{:S(2)}, u32[]{:S(2)}) %collective-permute-start) | collective-permute-done | bytes 262176 | tf_op jit(solution)/shard_map/ppermute | solution.py:170
  11.6 0.0 copy-start.2
  11.6 10.7 %all_to_all.20.parts_ref = f32[4,4,16,256]{3,2,1,0:T(8,128)S(1)} all-to-all(f32[4,4,16,256]{3,2,1,0:T(8,128)S(1)} %shard_map.59), channel_id=1, replica_groups={{0,32,64,96},{16,48,80,112},{128,160,192,224},{144,176,208,240},{256,28..., dimensions={0} | all-to-all | bytes 524288 | tf_op jit(solution)/shard_map/all_to_all | solution.py:163
  22.2 0.0 copy-done.2
  22.3 6.2 %collective-permute-start.1 = (f32[4,16,256]{2,1,0:T(8,128)S(1)}, f32[4,16,256]{2,1,0:T(8,128)S(1)}, u32[]{:S(2)}, u32[]{:S(2)}) collective-permute-start(f32[4,16,256]{2,1,0:T(8,128)S(1)} %shard_map.60), channel_id=1, source_target_pairs={{0,128},{16,400},{32,160},{48,432},{64,192},{80,464},{96,224},{112... | collective-permute-start | bytes 196616 | tf_op jit(solution)/shard_map/ppermute | solution.py:172
  28.4 2.8 %collective-permute-done.1 = f32[4,16,256]{2,1,0:T(8,128)S(1)} collective-permute-done((f32[4,16,256]{2,1,0:T(8,128)S(1)}, f32[4,16,256]{2,1,0:T(8,128)S(1)}, u32[]{:S(2)}, u32[]{:S(2)}) %collective-permute-start.1) | collective-permute-done | bytes 65568 | tf_op jit(solution)/shard_map/ppermute | solution.py:172
  31.2 5.4 %collective-permute-start.2 = (f32[4,16,256]{2,1,0:T(8,128)S(1)}, f32[4,16,256]{2,1,0:T(8,128)S(1)}, u32[]{:S(2)}, u32[]{:S(2)}) collective-permute-start(f32[4,16,256]{2,1,0:T(8,128)S(1)} %add.3.own_ref), channel_id=1, source_target_pairs={{0,384},{16,144},{32,416},{48,176},{64,448},{80,208},{96,480},{112... | collective-permute-start | bytes 196616 | tf_op jit(solution)/shard_map/ppermute | solution.py:173
  36.6 4.8 %collective-permute-done.2.other_ref = f32[4,16,256]{2,1,0:T(8,128)S(1)} collective-permute-done((f32[4,16,256]{2,1,0:T(8,128)S(1)}, f32[4,16,256]{2,1,0:T(8,128)S(1)}, u32[]{:S(2)}, u32[]{:S(2)}) %collective-permute-start.2) | collective-permute-done | bytes 65568 | tf_op jit(solution)/shard_map/ppermute | solution.py:173
  41.4 9.5 %all_to_all.21 = f32[4,4,16,256]{3,2,1,0:T(8,128)S(1)} all-to-all(f32[4,4,16,256]{3,2,1,0:T(8,128)S(1)} %shard_map.61), channel_id=1, replica_groups={{0,32,64,96},{16,48,80,112},{128,160,192,224},{144,176,208,240},{256,28..., dimensions={0} | all-to-all | bytes 524288 | tf_op jit(solution)/shard_map/all_to_all | solution.py:163
  51.0 7.9 %collective-permute-start.3 = (f32[256,256]{1,0:T(8,128)S(1)}, f32[256,256]{1,0:T(8,128)S(1)}, u32[]{:S(2)}, u32[]{:S(2)}) collective-permute-start(f32[256,256]{1,0:T(8,128)S(1)} %bitcast.8), channel_id=1, source_target_pairs={{0,16},{16,0},{32,48},{48,32},{64,80},{80,64},{96,112},{112,96},{1... | collective-permute-start | bytes 786440 | tf_op jit(solution)/shard_map/ppermute | solution.py:175
  58.9 1.1 %collective-permute-done.3.other_ref = f32[256,256]{1,0:T(8,128)S(1)} collective-permute-done((f32[256,256]{1,0:T(8,128)S(1)}, f32[256,256]{1,0:T(8,128)S(1)}, u32[]{:S(2)}, u32[]{:S(2)}) %collective-permute-start.3) | collective-permute-done | bytes 262176 | tf_op jit(solution)/shard_map/ppermute | solution.py:175
  60.0 0.4 shard_map.62
  60.4 13.6 %all_to_all.22.parts_ref = f32[16,40,128]{2,1,0:T(8,128)S(1)} all-to-all(f32[16,40,128]{2,1,0:T(8,128)S(1)} %bitcast.10), channel_id=1, replica_groups=mesh['dp'=32,'tensor'=16] {'tensor'}, dimensions={0} | all-to-all | bytes 655360 | tf_op jit(solution)/shard_map/all_to_all | solution.py:163
  74.0 0.0 copy-start.1
  74.0 10.7 %all_to_all.23 = f32[16,40,128]{2,1,0:T(8,128)S(1)} all-to-all(f32[16,40,128]{2,1,0:T(8,128)S(1)} %shard_map.63), channel_id=1, replica_groups=mesh['dp'=32,'tensor'=16] {'tensor'}, dimensions={0} | all-to-all | bytes 655360 | tf_op jit(solution)/shard_map/all_to_all | solution.py:163
  84.8 4.6 %collective-permute-start.4 = (f32[640,128]{1,0:T(8,128)S(1)}, f32[640,128]{1,0:T(8,128)S(1)}, u32[]{:S(2)}, u32[]{:S(2)}) collective-permute-start(f32[640,128]{1,0:T(8,128)S(1)} %bitcast.4), channel_id=1, source_target_pairs={{0,16},{16,0},{32,48},{48,32},{64,80},{80,64},{96,112},{112,96},{1... | collective-permute-start | bytes 983048 | tf_op jit(solution)/shard_map/ppermute | solution.py:179
  89.4 1.2 %collective-permute-done.4.other_ref = f32[640,128]{1,0:T(8,128)S(1)} collective-permute-done((f32[640,128]{1,0:T(8,128)S(1)}, f32[640,128]{1,0:T(8,128)S(1)}, u32[]{:S(2)}, u32[]{:S(2)}) %collective-permute-start.4) | collective-permute-done | bytes 327712 | tf_op jit(solution)/shard_map/ppermute | solution.py:179
  90.6 0.0 copy-done.1
  90.6 4.8 %shard_map.64 = (f32[16,256]{1,0:T(8,128)}, f32[16,256]{1,0:T(8,128)}, f32[16,32]{1,0:T(8,128)}) custom-call(f32[640,128]{1,0:T(8,128)S(1)} %bitcast.5, f32[640,128]{1,0:T(8,128)S(1)} %collective-permute-done.4.other_ref, f32[2,256,256]{2,1,0:T(8,128)S(1)} %get-tuple-element.6.rows_ref, f32[16,256]{1,0:T(8,128)S(1)} %copy-done.1), custom_call_target="tpu_custom_call" | custom-call | tf_op jit(solution)/shard_map/pallas_call | solution.py:180
  (6 shorter events, 0.1 us)
Async XLA Ops:
  0.6 1.0 copy-start
  1.6 9.9 %collective-permute-start = (f32[4,4,16,256]{3,2,1,0:T(8,128)S(1)}, f32[4,4,16,256]{3,2,1,0:T(8,128)S(1)}, u32[]{:S(2)}, u32[]{:S(2)}) collective-permute-start(f32[4,4,16,256]{3,2,1,0:T(8,128)S(1)} %shard_map.58), channel_id=1, source_target_pairs={{0,16},{16,0},{32,48},{48,32},{64,80},{80,64},{96,112},{112,96},{1... | collective-permute-start | bytes 786440 | tf_op jit(solution)/shard_map/ppermute | solution.py:170
  11.6 10.7 %copy-start.2 = (f32[16,256]{1,0:T(8,128)S(1)}, f32[16,256]{1,0:T(8,128)}, u32[]{:S(2)}) copy-start(f32[16,256]{1,0:T(8,128)} %momentum_ref.1) | copy-start | bytes 49156
  22.3 8.9 %collective-permute-start.1 = (f32[4,16,256]{2,1,0:T(8,128)S(1)}, f32[4,16,256]{2,1,0:T(8,128)S(1)}, u32[]{:S(2)}, u32[]{:S(2)}) collective-permute-start(f32[4,16,256]{2,1,0:T(8,128)S(1)} %shard_map.60), channel_id=1, source_target_pairs={{0,128},{16,400},{32,160},{48,432},{64,192},{80,464},{96,224},{112... | collective-permute-start | bytes 196616 | tf_op jit(solution)/shard_map/ppermute | solution.py:172
  31.2 10.2 %collective-permute-start.2 = (f32[4,16,256]{2,1,0:T(8,128)S(1)}, f32[4,16,256]{2,1,0:T(8,128)S(1)}, u32[]{:S(2)}, u32[]{:S(2)}) collective-permute-start(f32[4,16,256]{2,1,0:T(8,128)S(1)} %add.3.own_ref), channel_id=1, source_target_pairs={{0,384},{16,144},{32,416},{48,176},{64,448},{80,208},{96,480},{112... | collective-permute-start | bytes 196616 | tf_op jit(solution)/shard_map/ppermute | solution.py:173
  51.0 9.0 %collective-permute-start.3 = (f32[256,256]{1,0:T(8,128)S(1)}, f32[256,256]{1,0:T(8,128)S(1)}, u32[]{:S(2)}, u32[]{:S(2)}) collective-permute-start(f32[256,256]{1,0:T(8,128)S(1)} %bitcast.8), channel_id=1, source_target_pairs={{0,16},{16,0},{32,48},{48,32},{64,80},{80,64},{96,112},{112,96},{1... | collective-permute-start | bytes 786440 | tf_op jit(solution)/shard_map/ppermute | solution.py:175
  74.0 16.6 %copy-start.1 = (f32[16,256]{1,0:T(8,128)S(1)}, f32[16,256]{1,0:T(8,128)}, u32[]{:S(2)}) copy-start(f32[16,256]{1,0:T(8,128)} %weight_ref.1) | copy-start | bytes 49156
  84.8 5.8 %collective-permute-start.4 = (f32[640,128]{1,0:T(8,128)S(1)}, f32[640,128]{1,0:T(8,128)S(1)}, u32[]{:S(2)}, u32[]{:S(2)}) collective-permute-start(f32[640,128]{1,0:T(8,128)S(1)} %bitcast.4), channel_id=1, source_target_pairs={{0,16},{16,0},{32,48},{48,32},{64,80},{80,64},{96,112},{112,96},{1... | collective-permute-start | bytes 983048 | tf_op jit(solution)/shard_map/ppermute | solution.py:179

commit v12 on v11

--- a/solution.py
+++ b/solution.py
@@ -21,7 +21,7 @@
 
 CORE = [(i, i ^ 1) for i in range(32)]
 NEAR = [[8 * far + 2 * near + core for near in range(4)] for far in range(4) for core in range(2)]
-FAR = [[(i, i ^ (8 * steps[i % 2])) for i in range(32)] for steps in ((1, 3), (3, 1))]
+FAR = [[(i, i ^ (8 * steps[(i + i // 4) % 2])) for i in range(32)] for steps in ((1, 3), (3, 1))]
 
 NT = (((1,), (1,)), ((), ()))
 NN = (((1,), (0,)), ((), ()))
@@ -100,52 +100,76 @@
     return rows == columns
 
 
-def final_kernel(mine_ref, other_ref, rows_ref, weight_ref, new_momentum_ref, new_weight_ref, residual_ref, gram_ref, first_ref, next_ref):
+def multiply(left, right, out, change):
+    top, low = slice(0, 256), slice(256, 512)
+    pick = lambda pair, rows, columns: tuple(part[rows, columns] for part in pair)
+    whole = slice(0, 512)
+    upper = change(mul3(pick(left, top, whole), pick(right, whole, whole), NN), top, whole)
+    lower = change(mul3(pick(left, low, whole), pick(right, whole, low), NN), low, low)
+    out[0][top], out[1][top] = halves(upper)
+    out[0][low, low], out[1][low, low] = halves(lower)
+    out[0][low, top], out[1][low, top] = halves(upper[:, low].T)
+
+
+def final_kernel(
+    mine_ref, other_ref, rows_ref, weight_ref, new_momentum_ref, new_weight_ref, residual_ref,
+    gram_ref, gram_high, gram_low, first_high, first_low, inner_high, inner_low, after_high, after_low,
+):
     near, far, core = place()
     tensor = lax.axis_index("tensor")
     spot = near * 64 + far * 16
     new_momentum_ref[...] = rows_ref[core, pl.ds(pl.multiple_of(spot, 16), 16)]
+    trace = jnp.zeros((128, 128), f32)
     for which in range(2):
         pick = core == which
         block = lambda start, size: jnp.where(pick, mine_ref[start : start + size], other_ref[start : start + size])
         base = 256 * which
-        corner = block(128, 128)
-        gram_ref[base : base + 128, base : base + 128] = block(0, 128)
+        head, corner, tail = block(0, 128), block(128, 128), block(256, 128)
+        trace = trace + head + tail
+        gram_ref[base : base + 128, base : base + 128] = head
         gram_ref[base : base + 128, base + 128 : base + 256] = corner
         gram_ref[base + 128 : base + 256, base : base + 128] = corner.T
-        gram_ref[base + 128 : base + 256, base + 128 : base + 256] = block(256, 128)
+        gram_ref[base + 128 : base + 256, base + 128 : base + 256] = tail
         cross = block(384, 256)
         start = 256 + 128 * which
         gram_ref[0:256, start : start + 128] = cross
         gram_ref[start : start + 128, 0:256] = cross.T
-    unit = diagonal(0, 0, (IN, IN))
-    whole = gram_ref[...]
-    squares = jnp.sum(jnp.sum(jnp.where(unit, whole, 0.0), axis=1, keepdims=True), axis=0, keepdims=True)
+    trace = jnp.where(diagonal(0, 0, (128, 128)), trace, 0.0)
+    squares = jnp.sum(jnp.sum(trace, axis=0, keepdims=True), axis=1, keepdims=True)
     inverse = 1.0 / (jnp.sqrt(squares) + epsilon)
-    gram = (whole * inverse) * inverse
-    pair = halves(gram)
-    first = quintic_b * gram + quintic_c * mul3(pair, pair, NN) + jnp.where(unit, f32(quintic_a), f32(0.0))
-    first_ref[...] = first
-    first_pair = halves(first)
-    inner = mul3(first_pair, pair, NN)
-    after = mul3(first_pair, halves(inner), NN)
-    next_ref[...] = after
-    after_pair = halves(after)
+    gram = (gram_ref[...] * inverse) * inverse
+    gram_ref[...] = gram
+    gram_high[...], gram_low[...] = halves(gram)
+    pair, first_pair = (gram_high, gram_low), (first_high, first_low)
+    inner_pair, after_pair = (inner_high, inner_low), (after_high, after_low)
+
+    def polynomial(square, rows, columns):
+        unit = diagonal(rows.start, columns.start, square.shape)
+        value = quintic_b * gram_ref[rows, columns] + quintic_c * square
+        return value + jnp.where(unit, f32(quintic_a), f32(0.0))
+
+    multiply(pair, pair, first_pair, polynomial)
+    multiply(first_pair, pair, inner_pair, lambda value, rows, columns: value)
+    multiply(first_pair, inner_pair, after_pair, lambda value, rows, columns: value)
+    first_value = (first_high[...], first_low[...])
+    after_value = (after_high[...], after_low[...])
     starts = [core * 256 + spot]
     for which in range(2):
         starts.append(256 * which + lax.rem(tensor, 4) * 64 + lax.div(tensor, 4) * 16)
-    bands = [next_ref[pl.ds(pl.multiple_of(start, 16), 16)] for start in starts]
-    slab = jnp.concatenate(bands, axis=0)
+    slab = tuple(
+        jnp.concatenate([part[pl.ds(pl.multiple_of(start, 16), 16)] for start in starts], axis=0) for part in after_pair
+    )
     units = jnp.concatenate([diagonal(start, 0, (16, IN)) for start in starts], axis=0)
-    second = quintic_b * slab + quintic_c * mul3(halves(slab), after_pair, NN) + jnp.where(units, f32(quintic_a), f32(0.0))
-    own = halves(second[0:16])
-    total = mul3(own, first_pair, NN)
-    rows = rows_ref[...].reshape(IN, 256)
-    update = mul3(halves(total), halves(rows), NN) * inverse
+    second = quintic_b * (slab[0].astype(f32) + slab[1].astype(f32))
+    second = second + quintic_c * mul3(slab, after_value, NN) + jnp.where(units, f32(quintic_a), f32(0.0))
+    second_pair = halves(second)
+    own = tuple(part[0:16] for part in second_pair)
+    total = mul3(own, first_value, NN)
+    update = mul3(halves(total), halves(rows_ref[...].reshape(IN, 256)), NN) * inverse
     scale = learn_rate * 0.2 * float(max(IN, OUT)) ** 0.5
     new_weight_ref[...] = weight_ref[...] * (1.0 - learn_rate * weight_decay) - scale * update
-    product = mul3(own, after_pair, NN)
-    final = mul3(halves(product), halves(second[16:48]), NT)
+    product = mul3(own, after_value, NN)
+    final = mul3(halves(product), tuple(part[16:48] for part in second_pair), NT)
     identity = diagonal(lax.axis_index("dp") * 16, tensor * 32, (16, 32))
     residual_ref[...] = final - jnp.where(identity, f32(1.0), f32(0.0))
 
@@ -180,7 +204,7 @@
     return call(
         final_kernel,
         [(16, 256), (16, 256), (16, 32)],
-        [pltpu.VMEM((IN, IN), f32)] * 3,
+        [pltpu.VMEM((IN, IN), f32)] + [pltpu.VMEM((IN, IN), bf16)] * 8,
         limit=24 << 20,
     )(mine, other, rows, weight)
 

time: 95.9 us -> 95 us (level)
  no operation moved by 1% of the time
where the time goes in v12:
time: 95 us; the launch traced here: 94.5 us
  blocking collectives  44.5 us (47%)
  starting transfers between devices  32.6 us (34%)
  waiting for transfers between devices  10.6 us (11%)
  Pallas kernels  5.15 us (5%)
  local copies, waits for them, and re-layouts  0.96 us (1%)
    all_to_all x4, blocking collectives, exchange(): lax.all_to_all(value, axis, 0, 0, tiled=True, axis_index_groups=groups)  44.5 us
    ppermute x2, starting transfers between devices, per_device(): other = lax.ppermute(mine, 'dp', CORE)  12.6 us
    ppermute x1, starting transfers between devices, per_device(): lax.ppermute(send, 'dp', CORE)  8.79 us
    ppermute x1, starting transfers between devices, per_device(): parts = parts + lax.ppermute(parts, 'dp', FAR[0])  6.16 us
    ppermute x1, starting transfers between devices, per_device(): lax.ppermute(parts, 'dp', FAR[1])  5.05 us
    pallas_call x1, Pallas kernels, per_device(): call(final_kernel, [(16, 256), (16, 256), (16, 32)], [pltpu.VMEM((IN, IN)...  4.61 us
    ppermute x1, waiting for transfers between devices, per_device(): lax.ppermute(parts, 'dp', FAR[1])  4.13 us
    ppermute x1, waiting for transfers between devices, per_device(): parts = parts + lax.ppermute(parts, 'dp', FAR[0])  2.91 us
  transfers between devices with their start and end apart: 5, of which 5 were waited for; matrix products, arithmetic and copies ran while one was open for 0% of the time, Pallas kernels for 0%

profile of v12, /device:TPU:1, one launch (start us, length us, event | category | flops | bytes accessed | tf_op | source)
XLA Modules:
  0.0 94.5 jit_solution(11871281136936597881)
XLA Ops:
  0.6 0.0 copy-start
  0.6 0.9 copy-done
  1.6 8.8 %collective-permute-start = (f32[4,4,16,256]{3,2,1,0:T(8,128)S(1)}, f32[4,4,16,256]{3,2,1,0:T(8,128)S(1)}, u32[]{:S(2)}, u32[]{:S(2)}) collective-permute-start(f32[4,4,16,256]{3,2,1,0:T(8,128)S(1)} %shard_map.58), channel_id=1, source_target_pairs={{0,16},{16,0},{32,48},{48,32},{64,80},{80,64},{96,112},{112,96},{1... | collective-permute-start | bytes 786440 | tf_op jit(solution)/shard_map/ppermute | solution.py:194
  10.4 1.1 %collective-permute-done.got_ref = f32[4,4,16,256]{3,2,1,0:T(8,128)S(1)} collective-permute-done((f32[4,4,16,256]{3,2,1,0:T(8,128)S(1)}, f32[4,4,16,256]{3,2,1,0:T(8,128)S(1)}, u32[]{:S(2)}, u32[]{:S(2)}) %collective-permute-start) | collective-permute-done | bytes 262176 | tf_op jit(solution)/shard_map/ppermute | solution.py:194
  11.6 0.0 copy-start.2
  11.6 10.7 %all_to_all.20.parts_ref = f32[4,4,16,256]{3,2,1,0:T(8,128)S(1)} all-to-all(f32[4,4,16,256]{3,2,1,0:T(8,128)S(1)} %shard_map.59), channel_id=1, replica_groups={{0,32,64,96},{16,48,80,112},{128,160,192,224},{144,176,208,240},{256,28..., dimensions={0} | all-to-all | bytes 524288 | tf_op jit(solution)/shard_map/all_to_all | solution.py:187
  22.2 0.0 copy-done.2
  22.3 6.2 %collective-permute-start.1 = (f32[4,16,256]{2,1,0:T(8,128)S(1)}, f32[4,16,256]{2,1,0:T(8,128)S(1)}, u32[]{:S(2)}, u32[]{:S(2)}) collective-permute-start(f32[4,16,256]{2,1,0:T(8,128)S(1)} %shard_map.60), channel_id=1, source_target_pairs={{0,128},{16,400},{32,160},{48,432},{64,448},{80,208},{96,480},{112... | collective-permute-start | bytes 196616 | tf_op jit(solution)/shard_map/ppermute | solution.py:196
  28.4 2.9 %collective-permute-done.1 = f32[4,16,256]{2,1,0:T(8,128)S(1)} collective-permute-done((f32[4,16,256]{2,1,0:T(8,128)S(1)}, f32[4,16,256]{2,1,0:T(8,128)S(1)}, u32[]{:S(2)}, u32[]{:S(2)}) %collective-permute-start.1) | collective-permute-done | bytes 65568 | tf_op jit(solution)/shard_map/ppermute | solution.py:196
  31.4 5.1 %collective-permute-start.2 = (f32[4,16,256]{2,1,0:T(8,128)S(1)}, f32[4,16,256]{2,1,0:T(8,128)S(1)}, u32[]{:S(2)}, u32[]{:S(2)}) collective-permute-start(f32[4,16,256]{2,1,0:T(8,128)S(1)} %add.3.own_ref), channel_id=1, source_target_pairs={{0,384},{16,144},{32,416},{48,176},{64,192},{80,464},{96,224},{112... | collective-permute-start | bytes 196616 | tf_op jit(solution)/shard_map/ppermute | solution.py:197
  36.4 4.1 %collective-permute-done.2.other_ref = f32[4,16,256]{2,1,0:T(8,128)S(1)} collective-permute-done((f32[4,16,256]{2,1,0:T(8,128)S(1)}, f32[4,16,256]{2,1,0:T(8,128)S(1)}, u32[]{:S(2)}, u32[]{:S(2)}) %collective-permute-start.2) | collective-permute-done | bytes 65568 | tf_op jit(solution)/shard_map/ppermute | solution.py:197
  40.6 8.9 %all_to_all.21 = f32[4,4,16,256]{3,2,1,0:T(8,128)S(1)} all-to-all(f32[4,4,16,256]{3,2,1,0:T(8,128)S(1)} %shard_map.61), channel_id=1, replica_groups={{0,32,64,96},{16,48,80,112},{128,160,192,224},{144,176,208,240},{256,28..., dimensions={0} | all-to-all | bytes 524288 | tf_op jit(solution)/shard_map/all_to_all | solution.py:187
  49.5 8.0 %collective-permute-start.3 = (f32[256,256]{1,0:T(8,128)S(1)}, f32[256,256]{1,0:T(8,128)S(1)}, u32[]{:S(2)}, u32[]{:S(2)}) collective-permute-start(f32[256,256]{1,0:T(8,128)S(1)} %bitcast.8), channel_id=1, source_target_pairs={{0,16},{16,0},{32,48},{48,32},{64,80},{80,64},{96,112},{112,96},{1... | collective-permute-start | bytes 786440 | tf_op jit(solution)/shard_map/ppermute | solution.py:199
  57.5 1.1 %collective-permute-done.3.other_ref = f32[256,256]{1,0:T(8,128)S(1)} collective-permute-done((f32[256,256]{1,0:T(8,128)S(1)}, f32[256,256]{1,0:T(8,128)S(1)}, u32[]{:S(2)}, u32[]{:S(2)}) %collective-permute-start.3) | collective-permute-done | bytes 262176 | tf_op jit(solution)/shard_map/ppermute | solution.py:199
  58.6 0.4 shard_map.62
  59.0 14.2 %all_to_all.22.parts_ref = f32[16,40,128]{2,1,0:T(8,128)S(1)} all-to-all(f32[16,40,128]{2,1,0:T(8,128)S(1)} %bitcast.10), channel_id=1, replica_groups=mesh['dp'=32,'tensor'=16] {'tensor'}, dimensions={0} | all-to-all | bytes 655360 | tf_op jit(solution)/shard_map/all_to_all | solution.py:187
  73.3 0.0 copy-start.1
  73.3 10.7 %all_to_all.23 = f32[16,40,128]{2,1,0:T(8,128)S(1)} all-to-all(f32[16,40,128]{2,1,0:T(8,128)S(1)} %shard_map.63), channel_id=1, replica_groups=mesh['dp'=32,'tensor'=16] {'tensor'}, dimensions={0} | all-to-all | bytes 655360 | tf_op jit(solution)/shard_map/all_to_all | solution.py:187
  84.1 4.6 %collective-permute-start.4 = (f32[640,128]{1,0:T(8,128)S(1)}, f32[640,128]{1,0:T(8,128)S(1)}, u32[]{:S(2)}, u32[]{:S(2)}) collective-permute-start(f32[640,128]{1,0:T(8,128)S(1)} %bitcast.4), channel_id=1, source_target_pairs={{0,16},{16,0},{32,48},{48,32},{64,80},{80,64},{96,112},{112,96},{1... | collective-permute-start | bytes 983048 | tf_op jit(solution)/shard_map/ppermute | solution.py:203
  88.6 1.2 %collective-permute-done.4.other_ref = f32[640,128]{1,0:T(8,128)S(1)} collective-permute-done((f32[640,128]{1,0:T(8,128)S(1)}, f32[640,128]{1,0:T(8,128)S(1)}, u32[]{:S(2)}, u32[]{:S(2)}) %collective-permute-start.4) | collective-permute-done | bytes 327712 | tf_op jit(solution)/shard_map/ppermute | solution.py:203
  89.9 0.0 copy-done.1
  89.9 4.6 %shard_map.64 = (f32[16,256]{1,0:T(8,128)}, f32[16,256]{1,0:T(8,128)}, f32[16,32]{1,0:T(8,128)}) custom-call(f32[640,128]{1,0:T(8,128)S(1)} %bitcast.5, f32[640,128]{1,0:T(8,128)S(1)} %collective-permute-done.4.other_ref, f32[2,256,256]{2,1,0:T(8,128)S(1)} %get-tuple-element.6.rows_ref, f32[16,256]{1,0:T(8,128)S(1)} %copy-done.1), custom_call_target="tpu_custom_call" | custom-call | tf_op jit(solution)/shard_map/pallas_call | solution.py:204
  (6 shorter events, 0.1 us)
Async XLA Ops:
  0.6 1.0 %copy-start = (bf16[1,512,256]{2,1,0:T(8,128)(2,1)S(1)}, bf16[1,512,256]{2,1,0:T(8,128)(2,1)}, u32[]{:S(2)}) copy-start(bf16[1,512,256]{2,1,0:T(8,128)(2,1)} %param.3) | copy-start | bytes 786436
  1.6 9.9 %collective-permute-start = (f32[4,4,16,256]{3,2,1,0:T(8,128)S(1)}, f32[4,4,16,256]{3,2,1,0:T(8,128)S(1)}, u32[]{:S(2)}, u32[]{:S(2)}) collective-permute-start(f32[4,4,16,256]{3,2,1,0:T(8,128)S(1)} %shard_map.58), channel_id=1, source_target_pairs={{0,16},{16,0},{32,48},{48,32},{64,80},{80,64},{96,112},{112,96},{1... | collective-permute-start | bytes 786440 | tf_op jit(solution)/shard_map/ppermute | solution.py:194
  11.6 10.7 %copy-start.2 = (f32[16,256]{1,0:T(8,128)S(1)}, f32[16,256]{1,0:T(8,128)}, u32[]{:S(2)}) copy-start(f32[16,256]{1,0:T(8,128)} %momentum_ref.1) | copy-start | bytes 49156
  22.3 9.1 %collective-permute-start.1 = (f32[4,16,256]{2,1,0:T(8,128)S(1)}, f32[4,16,256]{2,1,0:T(8,128)S(1)}, u32[]{:S(2)}, u32[]{:S(2)}) collective-permute-start(f32[4,16,256]{2,1,0:T(8,128)S(1)} %shard_map.60), channel_id=1, source_target_pairs={{0,128},{16,400},{32,160},{48,432},{64,448},{80,208},{96,480},{112... | collective-permute-start | bytes 196616 | tf_op jit(solution)/shard_map/ppermute | solution.py:196
  31.4 9.2 %collective-permute-start.2 = (f32[4,16,256]{2,1,0:T(8,128)S(1)}, f32[4,16,256]{2,1,0:T(8,128)S(1)}, u32[]{:S(2)}, u32[]{:S(2)}) collective-permute-start(f32[4,16,256]{2,1,0:T(8,128)S(1)} %add.3.own_ref), channel_id=1, source_target_pairs={{0,384},{16,144},{32,416},{48,176},{64,192},{80,464},{96,224},{112... | collective-permute-start | bytes 196616 | tf_op jit(solution)/shard_map/ppermute | solution.py:197
  49.5 9.1 %collective-permute-start.3 = (f32[256,256]{1,0:T(8,128)S(1)}, f32[256,256]{1,0:T(8,128)S(1)}, u32[]{:S(2)}, u32[]{:S(2)}) collective-permute-start(f32[256,256]{1,0:T(8,128)S(1)} %bitcast.8), channel_id=1, source_target_pairs={{0,16},{16,0},{32,48},{48,32},{64,80},{80,64},{96,112},{112,96},{1... | collective-permute-start | bytes 786440 | tf_op jit(solution)/shard_map/ppermute | solution.py:199
  73.3 16.6 %copy-start.1 = (f32[16,256]{1,0:T(8,128)S(1)}, f32[16,256]{1,0:T(8,128)}, u32[]{:S(2)}) copy-start(f32[16,256]{1,0:T(8,128)} %weight_ref.1) | copy-start | bytes 49156
  84.1 5.8 %collective-permute-start.4 = (f32[640,128]{1,0:T(8,128)S(1)}, f32[640,128]{1,0:T(8,128)S(1)}, u32[]{:S(2)}, u32[]{:S(2)}) collective-permute-start(f32[640,128]{1,0:T(8,128)S(1)} %bitcast.4), channel_id=1, source_target_pairs={{0,16},{16,0},{32,48},{48,32},{64,80},{80,64},{96,112},{112,96},{1... | collective-permute-start | bytes 983048 | tf_op jit(solution)/shard_map/ppermute | solution.py:203

commit v13 on v12

--- a/solution.py
+++ b/solution.py
@@ -20,6 +20,9 @@
 bf16 = jnp.bfloat16
 
 CORE = [(i, i ^ 1) for i in range(32)]
+DOWN = [(i, i + 1) for i in range(0, 32, 2)]
+BACK = [(i + 1, i) for i in range(0, 32, 2)]
+BLOCKS = [(row, column) for row in range(4) for column in range(row, 4)]
 NEAR = [[8 * far + 2 * near + core for near in range(4)] for far in range(4) for core in range(2)]
 FAR = [[(i, i ^ (8 * steps[(i + i // 4) % 2])) for i in range(32)] for steps in ((1, 3), (3, 1))]
 
@@ -71,19 +74,10 @@
             out_ref[other, far] = total
 
 
-def gram_kernel(mine_ref, other_ref, out_ref, rows_ref):
-    _, _, core = place()
-    rows_ref[core] = mine_ref[...]
-    rows_ref[1 - core] = other_ref[...]
-    own = halves(mine_ref[...])
-    upper = tuple(part[:128] for part in own)
-    lower = tuple(part[128:] for part in own)
-    out_ref[0:128] = mul3(upper, upper, NT)
-    out_ref[128:256] = mul3(upper, lower, NT)
-    out_ref[256:384] = mul3(lower, lower, NT)
-    left = halves(rows_ref[0])
-    right = halves(rows_ref[1, pl.ds(pl.multiple_of(core * 128, 128), 128)])
-    out_ref[384:640] = mul3(left, right, NT)
+def gram_kernel(first_ref, last_ref, out_ref):
+    pieces = [halves(ref[start : start + 128]) for ref in (first_ref, last_ref) for start in (0, 128)]
+    for index, (row, column) in enumerate(BLOCKS):
+        out_ref[128 * index : 128 * index + 128] = mul3(pieces[row], pieces[column], NT)
 
 
 def tensor_sum_kernel(parts_ref, out_ref):
@@ -112,28 +106,19 @@
 
 
 def final_kernel(
-    mine_ref, other_ref, rows_ref, weight_ref, new_momentum_ref, new_weight_ref, residual_ref,
+    blocks_ref, first_ref, last_ref, own_ref, other_ref,
     gram_ref, gram_high, gram_low, first_high, first_low, inner_high, inner_low, after_high, after_low,
 ):
-    near, far, core = place()
+    near, far, _ = place()
     tensor = lax.axis_index("tensor")
-    spot = near * 64 + far * 16
-    new_momentum_ref[...] = rows_ref[core, pl.ds(pl.multiple_of(spot, 16), 16)]
     trace = jnp.zeros((128, 128), f32)
-    for which in range(2):
-        pick = core == which
-        block = lambda start, size: jnp.where(pick, mine_ref[start : start + size], other_ref[start : start + size])
-        base = 256 * which
-        head, corner, tail = block(0, 128), block(128, 128), block(256, 128)
-        trace = trace + head + tail
-        gram_ref[base : base + 128, base : base + 128] = head
-        gram_ref[base : base + 128, base + 128 : base + 256] = corner
-        gram_ref[base + 128 : base + 256, base : base + 128] = corner.T
-        gram_ref[base + 128 : base + 256, base + 128 : base + 256] = tail
-        cross = block(384, 256)
-        start = 256 + 128 * which
-        gram_ref[0:256, start : start + 128] = cross
-        gram_ref[start : start + 128, 0:256] = cross.T
+    for index, (row, column) in enumerate(BLOCKS):
+        block = blocks_ref[128 * index : 128 * index + 128]
+        gram_ref[128 * row : 128 * row + 128, 128 * column : 128 * column + 128] = block
+        if row == column:
+            trace = trace + block
+        else:
+            gram_ref[128 * column : 128 * column + 128, 128 * row : 128 * row + 128] = block.T
     trace = jnp.where(diagonal(0, 0, (128, 128)), trace, 0.0)
     squares = jnp.sum(jnp.sum(trace, axis=0, keepdims=True), axis=1, keepdims=True)
     inverse = 1.0 / (jnp.sqrt(squares) + epsilon)
@@ -153,25 +138,35 @@
     multiply(first_pair, inner_pair, after_pair, lambda value, rows, columns: value)
     first_value = (first_high[...], first_low[...])
     after_value = (after_high[...], after_low[...])
-    starts = [core * 256 + spot]
-    for which in range(2):
-        starts.append(256 * which + lax.rem(tensor, 4) * 64 + lax.div(tensor, 4) * 16)
-    slab = tuple(
-        jnp.concatenate([part[pl.ds(pl.multiple_of(start, 16), 16)] for start in starts], axis=0) for part in after_pair
-    )
+    spot = pl.multiple_of(near * 64 + far * 16, 16)
+    column = pl.multiple_of(lax.rem(tensor, 4) * 64 + lax.div(tensor, 4) * 16, 16)
+    starts = [pl.multiple_of(256 * side + start, 16) for start in (spot, column) for side in range(2)]
+    slab = tuple(jnp.concatenate([part[pl.ds(start, 16)] for start in starts], axis=0) for part in after_pair)
     units = jnp.concatenate([diagonal(start, 0, (16, IN)) for start in starts], axis=0)
     second = quintic_b * (slab[0].astype(f32) + slab[1].astype(f32))
     second = second + quintic_c * mul3(slab, after_value, NN) + jnp.where(units, f32(quintic_a), f32(0.0))
     second_pair = halves(second)
-    own = tuple(part[0:16] for part in second_pair)
-    total = mul3(own, first_value, NN)
-    update = mul3(halves(total), halves(rows_ref[...].reshape(IN, 256)), NN) * inverse
+    chip = tuple(part[0:32] for part in second_pair)
+    total = mul3(chip, first_value, NN)
     scale = learn_rate * 0.2 * float(max(IN, OUT)) ** 0.5
-    new_weight_ref[...] = weight_ref[...] * (1.0 - learn_rate * weight_decay) - scale * update
-    product = mul3(own, after_value, NN)
-    final = mul3(halves(product), tuple(part[16:48] for part in second_pair), NT)
-    identity = diagonal(lax.axis_index("dp") * 16, tensor * 32, (16, 32))
-    residual_ref[...] = final - jnp.where(identity, f32(1.0), f32(0.0))
+    update = mul3(halves(total), halves(jnp.concatenate([first_ref[...], last_ref[...]], axis=0)), NN) * (inverse * scale)
+    product = mul3(chip, after_value, NN)
+    final = mul3(halves(product), tuple(part[32:64] for part in second_pair), NT)
+    identity = diagonal(2 * spot, 2 * column, (32, 32))
+    residual = final - jnp.where(identity, f32(1.0), f32(0.0))
+    for side, (out_ref, rows_ref) in enumerate(((other_ref, first_ref), (own_ref, last_ref))):
+        out_ref[0:16] = rows_ref[pl.ds(spot, 16)]
+        out_ref[16:32] = update[16 * side : 16 * side + 16]
+        out_ref[32:48, 0:32] = residual[16 * side : 16 * side + 16]
+        out_ref[32:48, 32:256] = jnp.zeros((16, 224), f32)
+
+
+def finish_kernel(own_ref, got_ref, weight_ref, new_momentum_ref, new_weight_ref, residual_ref):
+    _, _, core = place()
+    results = jnp.where(core == 1, own_ref[...], got_ref[...])
+    new_momentum_ref[...] = results[0:16]
+    new_weight_ref[...] = weight_ref[...] * (1.0 - learn_rate * weight_decay) - results[16:32]
+    residual_ref[...] = results[32:48, 0:32]
 
 
 def call(kernel, outs, scratch=(), limit=4 << 20):
@@ -185,6 +180,22 @@
 
 def exchange(value, axis, groups=None):
     return lax.all_to_all(value, axis, 0, 0, tiled=True, axis_index_groups=groups)
+
+
+def both_cores(first, last):
+    split = (16, 80, 128)
+    (value,) = call(gram_kernel, [(1280, 128)], limit=8 << 20)(first, last)
+    (value,) = call(tensor_sum_kernel, [split])(exchange(value.reshape(split), "tensor"))
+    return call(
+        final_kernel,
+        [(48, 256), (48, 256)],
+        [pltpu.VMEM((IN, IN), f32)] + [pltpu.VMEM((IN, IN), bf16)] * 8,
+        limit=24 << 20,
+    )(exchange(value, "tensor").reshape(1280, 128), first, last)
+
+
+def no_core(first, last):
+    return jnp.zeros((48, 256), f32), jnp.zeros((48, 256), f32)
 
 
 def per_device(gradients, momentum, weight):
@@ -196,17 +207,9 @@
     parts = parts + lax.ppermute(parts, "dp", FAR[0])
     (spread,) = call(far_sum_kernel, [chunks])(parts, lax.ppermute(parts, "dp", FAR[1]))
     mine = exchange(spread, "dp", NEAR).reshape(256, 256)
-    other = lax.ppermute(mine, "dp", CORE)
-    blocks, rows = call(gram_kernel, [(640, 128), (2, 256, 256)], limit=8 << 20)(mine, other)
-    (spread,) = call(tensor_sum_kernel, [(16, 40, 128)])(exchange(blocks.reshape(16, 40, 128), "tensor"))
-    mine = exchange(spread, "tensor").reshape(640, 128)
-    other = lax.ppermute(mine, "dp", CORE)
-    return call(
-        final_kernel,
-        [(16, 256), (16, 256), (16, 32)],
-        [pltpu.VMEM((IN, IN), f32)] + [pltpu.VMEM((IN, IN), bf16)] * 8,
-        limit=24 << 20,
-    )(mine, other, rows, weight)
+    first = lax.ppermute(mine, "dp", DOWN)
+    own, other = lax.cond(place()[2] == 1, both_cores, no_core, first, mine)
+    return call(finish_kernel, [(16, 256), (16, 256), (16, 32)])(own, lax.ppermute(other, "dp", BACK), weight)
 
 
 def solution(mesh):

time: 95 us -> 93.5 us (0.984)
  starting transfers between devices: 32.6 us -> 22.6 us
  waiting for transfers between devices: 10.6 us -> 16.1 us
  blocking collectives: 44.5 us -> 47.2 us
    ppermute x2, starting transfers between devices: 12.6 us -> 2.58 us  [the longest x1 1.3 us: per_device(): lax.ppermute(other, 'dp', BACK)]
    ppermute x2, waiting for transfers between devices: 2.37 us -> 7.94 us  [the longest x1 7.08 us: per_device(): first = lax.ppermute(mine, 'dp', DOWN)]
    all_to_all x4, blocking collectives: 44.5 us -> 47.2 us  [exchange(): lax.all_to_all(value, axis, 0, 0, tiled=True, axis_index_groups=groups)]
    pallas_call x3 -> x4, Pallas kernels: 5.06 us -> 5.46 us  [the longest x1 4.1 us: both_cores(): call(final_kernel, [(48, 256), (48, 256)], [pltpu.VMEM((IN, IN), f32)] +...]
where the time goes in v13:
time: 93.5 us; the launch traced here: 93.1 us
  blocking collectives  47.2 us (50%)
  starting transfers between devices  22.6 us (24%)
  waiting for transfers between devices  16.1 us (17%)
  Pallas kernels  5.55 us (6%)
  local copies, waits for them, and re-layouts  0.95 us (1%)
    all_to_all x4, blocking collectives, exchange(): lax.all_to_all(value, axis, 0, 0, tiled=True, axis_index_groups=groups)  47.2 us
    ppermute x1, starting transfers between devices, per_device(): lax.ppermute(send, 'dp', CORE)  8.79 us
    ppermute x1, waiting for transfers between devices, per_device(): first = lax.ppermute(mine, 'dp', DOWN)  7.08 us
    ppermute x1, starting transfers between devices, per_device(): parts = parts + lax.ppermute(parts, 'dp', FAR[0])  6.16 us
    ppermute x1, starting transfers between devices, per_device(): lax.ppermute(parts, 'dp', FAR[1])  5.05 us
    ppermute x1, waiting for transfers between devices, per_device(): lax.ppermute(parts, 'dp', FAR[1])  4.13 us
    pallas_call x1, Pallas kernels, both_cores(): call(final_kernel, [(48, 256), (48, 256)], [pltpu.VMEM((IN, IN), f32)] +...  4.1 us
    ppermute x1, waiting for transfers between devices, per_device(): parts = parts + lax.ppermute(parts, 'dp', FAR[0])  2.91 us
  transfers between devices with their start and end apart: 5, of which 5 were waited for; matrix products, arithmetic and copies ran while one was open for 0% of the time, Pallas kernels for 0%

profile of v13, /device:TPU:1, one launch (start us, length us, event | category | flops | bytes accessed | tf_op | source)
XLA Modules:
  0.0 93.1 jit_solution(12929518553863965502)
XLA Ops:
  0.6 0.0 copy-start
  0.6 0.9 %copy-done = bf16[1,512,256]{2,1,0:T(8,128)(2,1)S(1)} copy-done((bf16[1,512,256]{2,1,0:T(8,128)(2,1)S(1)}, bf16[1,512,256]{2,1,0:T(8,128)(2,1)}, u32[]{:S(2)}) %copy-start) | copy-done | bytes 262168
  1.6 8.8 %collective-permute-start = (f32[4,4,16,256]{3,2,1,0:T(8,128)S(1)}, f32[4,4,16,256]{3,2,1,0:T(8,128)S(1)}, u32[]{:S(2)}, u32[]{:S(2)}) collective-permute-start(f32[4,4,16,256]{3,2,1,0:T(8,128)S(1)} %shard_map.58), channel_id=1, source_target_pairs={{0,16},{16,0},{32,48},{48,32},{64,80},{80,64},{96,112},{112,96},{1... | collective-permute-start | bytes 786440 | tf_op jit(solution)/shard_map/ppermute | solution.py:205
  10.4 1.1 %collective-permute-done.got_ref = f32[4,4,16,256]{3,2,1,0:T(8,128)S(1)} collective-permute-done((f32[4,4,16,256]{3,2,1,0:T(8,128)S(1)}, f32[4,4,16,256]{3,2,1,0:T(8,128)S(1)}, u32[]{:S(2)}, u32[]{:S(2)}) %collective-permute-start) | collective-permute-done | bytes 262176 | tf_op jit(solution)/shard_map/ppermute | solution.py:205
  11.6 0.0 copy-start.2
  11.6 10.7 %all_to_all.20.parts_ref = f32[4,4,16,256]{3,2,1,0:T(8,128)S(1)} all-to-all(f32[4,4,16,256]{3,2,1,0:T(8,128)S(1)} %shard_map.59), channel_id=1, replica_groups={{0,32,64,96},{16,48,80,112},{128,160,192,224},{144,176,208,240},{256,28..., dimensions={0} | all-to-all | bytes 524288 | tf_op jit(solution)/shard_map/all_to_all | solution.py:182
  22.2 0.0 copy-done.2
  22.3 6.2 %collective-permute-start.1 = (f32[4,16,256]{2,1,0:T(8,128)S(1)}, f32[4,16,256]{2,1,0:T(8,128)S(1)}, u32[]{:S(2)}, u32[]{:S(2)}) collective-permute-start(f32[4,16,256]{2,1,0:T(8,128)S(1)} %shard_map.60), channel_id=1, source_target_pairs={{0,128},{16,400},{32,160},{48,432},{64,448},{80,208},{96,480},{112... | collective-permute-start | bytes 196616 | tf_op jit(solution)/shard_map/ppermute | solution.py:207
  28.4 2.9 %collective-permute-done.1 = f32[4,16,256]{2,1,0:T(8,128)S(1)} collective-permute-done((f32[4,16,256]{2,1,0:T(8,128)S(1)}, f32[4,16,256]{2,1,0:T(8,128)S(1)}, u32[]{:S(2)}, u32[]{:S(2)}) %collective-permute-start.1) | collective-permute-done | bytes 65568 | tf_op jit(solution)/shard_map/ppermute | solution.py:207
  31.4 5.1 %collective-permute-start.2 = (f32[4,16,256]{2,1,0:T(8,128)S(1)}, f32[4,16,256]{2,1,0:T(8,128)S(1)}, u32[]{:S(2)}, u32[]{:S(2)}) collective-permute-start(f32[4,16,256]{2,1,0:T(8,128)S(1)} %add.3.own_ref), channel_id=1, source_target_pairs={{0,384},{16,144},{32,416},{48,176},{64,192},{80,464},{96,224},{112... | collective-permute-start | bytes 196616 | tf_op jit(solution)/shard_map/ppermute | solution.py:208
  36.4 4.1 %collective-permute-done.2.other_ref = f32[4,16,256]{2,1,0:T(8,128)S(1)} collective-permute-done((f32[4,16,256]{2,1,0:T(8,128)S(1)}, f32[4,16,256]{2,1,0:T(8,128)S(1)}, u32[]{:S(2)}, u32[]{:S(2)}) %collective-permute-start.2) | collective-permute-done | bytes 65568 | tf_op jit(solution)/shard_map/ppermute | solution.py:208
  40.6 8.9 %all_to_all.21 = f32[4,4,16,256]{3,2,1,0:T(8,128)S(1)} all-to-all(f32[4,4,16,256]{3,2,1,0:T(8,128)S(1)} %shard_map.61), channel_id=1, replica_groups={{0,32,64,96},{16,48,80,112},{128,160,192,224},{144,176,208,240},{256,28..., dimensions={0} | all-to-all | bytes 524288 | tf_op jit(solution)/shard_map/all_to_all | solution.py:182
  49.5 1.3 %collective-permute-start.3 = (f32[256,256]{1,0:T(8,128)S(1)}, f32[256,256]{1,0:T(8,128)S(1)}, u32[]{:S(2)}, u32[]{:S(2)}) collective-permute-start(f32[256,256]{1,0:T(8,128)S(1)} %bitcast.8), channel_id=1, source_target_pairs={{0,16},{32,48},{64,80},{96,112},{128,144},{160,176},{192,208},{224... | collective-permute-start | bytes 786440 | tf_op jit(solution)/shard_map/ppermute | solution.py:210
  50.8 7.1 %collective-permute-done.3 = f32[256,256]{1,0:T(8,128)S(1)} collective-permute-done((f32[256,256]{1,0:T(8,128)S(1)}, f32[256,256]{1,0:T(8,128)S(1)}, u32[]{:S(2)}, u32[]{:S(2)}) %collective-permute-start.3) | collective-permute-done | bytes 262176 | tf_op jit(solution)/shard_map/ppermute | solution.py:210
  57.9 0.0 copy-start.1
  57.9 32.4 %conditional.1 = ((f32[48,256]{1,0:T(8,128)S(1)}, f32[48,256]{1,0:T(8,128)S(1)})) conditional(s32[]{:T(128)} %convert_element_type.3, () %tuple.14, (f32[256,256]{1,0:T(8,128)S(1)}, f32[256,256]{1,0:T(8,128)S(1)}) %tuple.20), branch_computations={%region_0.0_spmd, %region_1.0_spmd} | conditional | bytes 2621448 | solution.py:211
  57.9 0.7 branch_1_fun.3
  58.5 15.1 %all_to_all.18.parts_ref = f32[16,80,128]{2,1,0:T(8,128)S(1)} all-to-all(f32[16,80,128]{2,1,0:T(8,128)S(1)} %bitcast.5), channel_id=1, replica_groups=mesh['dp'=32,'tensor'=16] {'tensor'}, dimensions={0} | all-to-all | bytes 1310720 | tf_op jit(solution)/shard_map/cond/branch_1_fun/all_to_all | solution.py:182
  73.6 0.1 branch_1_fun.4
  73.7 12.5 %all_to_all.19 = f32[16,80,128]{2,1,0:T(8,128)S(1)} all-to-all(f32[16,80,128]{2,1,0:T(8,128)S(1)} %branch_1_fun.4), channel_id=1, replica_groups=mesh['dp'=32,'tensor'=16] {'tensor'}, dimensions={0} | all-to-all | bytes 1310720 | tf_op jit(solution)/shard_map/cond/branch_1_fun/all_to_all | solution.py:182
  86.2 4.1 %branch_1_fun.5 = (f32[48,256]{1,0:T(8,128)S(1)}, f32[48,256]{1,0:T(8,128)S(1)}) custom-call(f32[1280,128]{1,0:T(8,128)S(1)} %bitcast.4, f32[256,256]{1,0:T(8,128)S(1)} %get-tuple-element.4.first_ref, f32[256,256]{1,0:T(8,128)S(1)} %get-tuple-element.5.last_ref), custom_call_target="tpu_custom_call" | custom-call | tf_op jit(solution)/shard_map/cond/branch_1_fun/pallas_call | solution.py:189
  90.3 1.3 %collective-permute-start.4 = (f32[48,256]{1,0:T(8,128)S(1)}, f32[48,256]{1,0:T(8,128)S(1)}, u32[]{:S(2)}, u32[]{:S(2)}) collective-permute-start(f32[48,256]{1,0:T(8,128)S(1)} %get-tuple-element.12), channel_id=1, source_target_pairs={{16,0},{48,32},{80,64},{112,96},{144,128},{176,160},{208,192},{240... | collective-permute-start | bytes 147464 | tf_op jit(solution)/shard_map/ppermute | solution.py:212
  91.6 0.9 collective-permute-done.4.got_ref
  92.5 0.0 copy-done.1
  92.5 0.6 shard_map.62
  (5 shorter events, 0.1 us)
Async XLA Ops:
  0.6 1.0 %copy-start = (bf16[1,512,256]{2,1,0:T(8,128)(2,1)S(1)}, bf16[1,512,256]{2,1,0:T(8,128)(2,1)}, u32[]{:S(2)}) copy-start(bf16[1,512,256]{2,1,0:T(8,128)(2,1)} %param.5) | copy-start | bytes 786436
  1.6 9.9 %collective-permute-start = (f32[4,4,16,256]{3,2,1,0:T(8,128)S(1)}, f32[4,4,16,256]{3,2,1,0:T(8,128)S(1)}, u32[]{:S(2)}, u32[]{:S(2)}) collective-permute-start(f32[4,4,16,256]{3,2,1,0:T(8,128)S(1)} %shard_map.58), channel_id=1, source_target_pairs={{0,16},{16,0},{32,48},{48,32},{64,80},{80,64},{96,112},{112,96},{1... | collective-permute-start | bytes 786440 | tf_op jit(solution)/shard_map/ppermute | solution.py:205
  11.6 10.7 %copy-start.2 = (f32[16,256]{1,0:T(8,128)S(1)}, f32[16,256]{1,0:T(8,128)}, u32[]{:S(2)}) copy-start(f32[16,256]{1,0:T(8,128)} %momentum_ref.1) | copy-start | bytes 49156
  22.3 9.1 %collective-permute-start.1 = (f32[4,16,256]{2,1,0:T(8,128)S(1)}, f32[4,16,256]{2,1,0:T(8,128)S(1)}, u32[]{:S(2)}, u32[]{:S(2)}) collective-permute-start(f32[4,16,256]{2,1,0:T(8,128)S(1)} %shard_map.60), channel_id=1, source_target_pairs={{0,128},{16,400},{32,160},{48,432},{64,448},{80,208},{96,480},{112... | collective-permute-start | bytes 196616 | tf_op jit(solution)/shard_map/ppermute | solution.py:207
  31.4 9.2 %collective-permute-start.2 = (f32[4,16,256]{2,1,0:T(8,128)S(1)}, f32[4,16,256]{2,1,0:T(8,128)S(1)}, u32[]{:S(2)}, u32[]{:S(2)}) collective-permute-start(f32[4,16,256]{2,1,0:T(8,128)S(1)} %add.3.own_ref), channel_id=1, source_target_pairs={{0,384},{16,144},{32,416},{48,176},{64,192},{80,464},{96,224},{112... | collective-permute-start | bytes 196616 | tf_op jit(solution)/shard_map/ppermute | solution.py:208
  49.5 8.4 %collective-permute-start.3 = (f32[256,256]{1,0:T(8,128)S(1)}, f32[256,256]{1,0:T(8,128)S(1)}, u32[]{:S(2)}, u32[]{:S(2)}) collective-permute-start(f32[256,256]{1,0:T(8,128)S(1)} %bitcast.8), channel_id=1, source_target_pairs={{0,16},{32,48},{64,80},{96,112},{128,144},{160,176},{192,208},{224... | collective-permute-start | bytes 786440 | tf_op jit(solution)/shard_map/ppermute | solution.py:210
  57.9 34.6 %copy-start.1 = (f32[16,256]{1,0:T(8,128)S(1)}, f32[16,256]{1,0:T(8,128)}, u32[]{:S(2)}) copy-start(f32[16,256]{1,0:T(8,128)} %weight_ref.1) | copy-start | bytes 49156
  90.3 2.2 %collective-permute-start.4 = (f32[48,256]{1,0:T(8,128)S(1)}, f32[48,256]{1,0:T(8,128)S(1)}, u32[]{:S(2)}, u32[]{:S(2)}) collective-permute-start(f32[48,256]{1,0:T(8,128)S(1)} %get-tuple-element.12), channel_id=1, source_target_pairs={{16,0},{48,32},{80,64},{112,96},{144,128},{176,160},{208,192},{240... | collective-permute-start | bytes 147464 | tf_op jit(solution)/shard_map/ppermute | solution.py:212

commit v14 on v13

--- a/solution.py
+++ b/solution.py
@@ -20,7 +20,7 @@
 bf16 = jnp.bfloat16
 
 CORE = [(i, i ^ 1) for i in range(32)]
-DOWN = [(i, i + 1) for i in range(0, 32, 2)]
+DOWN = [[(i, (i + 1) ^ (2 * step)) for i in range(0, 32, 2)] for step in range(4)]
 BACK = [(i + 1, i) for i in range(0, 32, 2)]
 BLOCKS = [(row, column) for row in range(4) for column in range(row, 4)]
 NEAR = [[8 * far + 2 * near + core for near in range(4)] for far in range(4) for core in range(2)]
@@ -74,7 +74,15 @@
             out_ref[other, far] = total
 
 
-def gram_kernel(first_ref, last_ref, out_ref):
+def far_part_kernel(own_ref, other_ref, out_ref):
+    out_ref[...] = own_ref[...] + other_ref[...]
+
+
+def gram_kernel(last_ref, part_0, part_1, part_2, part_3, out_ref, first_ref):
+    near, _, _ = place()
+    for step, part_ref in enumerate((part_0, part_1, part_2, part_3)):
+        start = pl.multiple_of((near ^ step) * 64, 64)
+        first_ref[pl.ds(start, 64)] = part_ref[...].reshape(64, 256)
     pieces = [halves(ref[start : start + 128]) for ref in (first_ref, last_ref) for start in (0, 128)]
     for index, (row, column) in enumerate(BLOCKS):
         out_ref[128 * index : 128 * index + 128] = mul3(pieces[row], pieces[column], NT)
@@ -182,9 +190,18 @@
     return lax.all_to_all(value, axis, 0, 0, tiled=True, axis_index_groups=groups)
 
 
-def both_cores(first, last):
+def near_gather(own, other):
+    (spread,) = call(far_sum_kernel, [(4, 4, 16, 256)])(own, other)
+    return exchange(spread, "dp", NEAR).reshape(256, 256)
+
+
+def no_gather(own, other):
+    return jnp.zeros((256, 256), f32)
+
+
+def both_cores(last, *parts):
     split = (16, 80, 128)
-    (value,) = call(gram_kernel, [(1280, 128)], limit=8 << 20)(first, last)
+    value, first = call(gram_kernel, [(1280, 128), (256, 256)], limit=8 << 20)(last, *parts)
     (value,) = call(tensor_sum_kernel, [split])(exchange(value.reshape(split), "tensor"))
     return call(
         final_kernel,
@@ -194,7 +211,7 @@
     )(exchange(value, "tensor").reshape(1280, 128), first, last)
 
 
-def no_core(first, last):
+def no_core(last, *parts):
     return jnp.zeros((48, 256), f32), jnp.zeros((48, 256), f32)
 
 
@@ -205,10 +222,11 @@
     (parts,) = call(core_sum_kernel, [chunks])(gradients, lax.ppermute(send, "dp", CORE))
     (parts,) = call(near_sum_kernel, [chunks[1:]])(exchange(parts, "dp", NEAR), momentum)
     parts = parts + lax.ppermute(parts, "dp", FAR[0])
-    (spread,) = call(far_sum_kernel, [chunks])(parts, lax.ppermute(parts, "dp", FAR[1]))
-    mine = exchange(spread, "dp", NEAR).reshape(256, 256)
-    first = lax.ppermute(mine, "dp", DOWN)
-    own, other = lax.cond(place()[2] == 1, both_cores, no_core, first, mine)
+    other = lax.ppermute(parts, "dp", FAR[1])
+    (part,) = call(far_part_kernel, [chunks[1:]])(parts, other)
+    pieces = [lax.ppermute(part, "dp", pairs) for pairs in DOWN]
+    last = lax.cond(place()[2] == 1, near_gather, no_gather, parts, other)
+    own, other = lax.cond(place()[2] == 1, both_cores, no_core, last, *pieces)
     return call(finish_kernel, [(16, 256), (16, 256), (16, 32)])(own, lax.ppermute(other, "dp", BACK), weight)
 
 

time: 93.5 us -> 91.6 us (0.980)
  waiting for transfers between devices: 16.1 us -> 9.05 us
  starting transfers between devices: 22.6 us -> 26.5 us
  blocking collectives: 47.2 us -> 48.3 us
    ppermute x2 -> x5, waiting for transfers between devices: 11.2 us -> 4.14 us  [the longest x1 4.13 us: per_device(): other = lax.ppermute(parts, 'dp', FAR[1])]
    ppermute x2 -> x5, starting transfers between devices: 6.34 us -> 10.2 us  [the longest x4 5.17 us: per_device(): pieces = [lax.ppermute(part, 'dp', pairs) for pairs in DOWN]]
    all_to_all x4, blocking collectives: 47.2 us -> 48.3 us  [exchange(): lax.all_to_all(value, axis, 0, 0, tiled=True, axis_index_groups=groups)]
  transfers between devices with their start and end apart: 5 -> 8, of which waited for: 5 -> 4; matrix products, arithmetic and copies ran while one was open for 0% -> 0% of each run, Pallas kernels for 0% -> 0%
where the time goes in v14:
time: 91.6 us; the launch traced here: 91.2 us
  blocking collectives  48.3 us (53%)
  starting transfers between devices  26.5 us (29%)
  waiting for transfers between devices  9.05 us (10%)
  Pallas kernels  5.58 us (6%)
  local copies, waits for them, and re-layouts  0.96 us (1%)
    all_to_all x4, blocking collectives, exchange(): lax.all_to_all(value, axis, 0, 0, tiled=True, axis_index_groups=groups)  48.3 us
    ppermute x1, starting transfers between devices, per_device(): lax.ppermute(send, 'dp', CORE)  8.79 us
    ppermute x1, starting transfers between devices, per_device(): parts = parts + lax.ppermute(parts, 'dp', FAR[0])  6.16 us
    ppermute x4, starting transfers between devices, per_device(): pieces = [lax.ppermute(part, 'dp', pairs) for pairs in DOWN]  5.17 us
    ppermute x1, starting transfers between devices, per_device(): other = lax.ppermute(parts, 'dp', FAR[1])  5.05 us
    ppermute x1, waiting for transfers between devices, per_device(): other = lax.ppermute(parts, 'dp', FAR[1])  4.13 us
    pallas_call x1, Pallas kernels, both_cores(): call(final_kernel, [(48, 256), (48, 256)], [pltpu.VMEM((IN, IN), f32)] +...  4.1 us
    ppermute x1, waiting for transfers between devices, per_device(): parts = parts + lax.ppermute(parts, 'dp', FAR[0])  2.91 us
  transfers between devices with their start and end apart: 8, of which 4 were waited for; matrix products, arithmetic and copies ran while one was open for 0% of the time, Pallas kernels for 0%

profile of v14, /device:TPU:1, one launch (start us, length us, event | category | flops | bytes accessed | tf_op | source)
XLA Modules:
  0.0 91.2 jit_solution(12838434423851711103)
XLA Ops:
  0.6 0.0 copy-start
  0.6 0.9 %copy-done = bf16[1,512,256]{2,1,0:T(8,128)(2,1)S(1)} copy-done((bf16[1,512,256]{2,1,0:T(8,128)(2,1)S(1)}, bf16[1,512,256]{2,1,0:T(8,128)(2,1)}, u32[]{:S(2)}) %copy-start) | copy-done | bytes 262168
  1.6 8.8 %collective-permute-start = (f32[4,4,16,256]{3,2,1,0:T(8,128)S(1)}, f32[4,4,16,256]{3,2,1,0:T(8,128)S(1)}, u32[]{:S(2)}, u32[]{:S(2)}) collective-permute-start(f32[4,4,16,256]{3,2,1,0:T(8,128)S(1)} %shard_map.58), channel_id=1, source_target_pairs={{0,16},{16,0},{32,48},{48,32},{64,80},{80,64},{96,112},{112,96},{1... | collective-permute-start | bytes 786440 | tf_op jit(solution)/shard_map/ppermute | solution.py:222
  10.4 1.1 %collective-permute-done.got_ref = f32[4,4,16,256]{3,2,1,0:T(8,128)S(1)} collective-permute-done((f32[4,4,16,256]{3,2,1,0:T(8,128)S(1)}, f32[4,4,16,256]{3,2,1,0:T(8,128)S(1)}, u32[]{:S(2)}, u32[]{:S(2)}) %collective-permute-start) | collective-permute-done | bytes 262176 | tf_op jit(solution)/shard_map/ppermute | solution.py:222
  11.6 0.0 copy-start.2
  11.6 10.7 %all_to_all.20.parts_ref = f32[4,4,16,256]{3,2,1,0:T(8,128)S(1)} all-to-all(f32[4,4,16,256]{3,2,1,0:T(8,128)S(1)} %shard_map.59), channel_id=1, replica_groups={{0,32,64,96},{16,48,80,112},{128,160,192,224},{144,176,208,240},{256,28..., dimensions={0} | all-to-all | bytes 524288 | tf_op jit(solution)/shard_map/all_to_all | solution.py:190
  22.2 0.0 copy-done.2
  22.3 6.2 %collective-permute-start.1 = (f32[4,16,256]{2,1,0:T(8,128)S(1)}, f32[4,16,256]{2,1,0:T(8,128)S(1)}, u32[]{:S(2)}, u32[]{:S(2)}) collective-permute-start(f32[4,16,256]{2,1,0:T(8,128)S(1)} %shard_map.60), channel_id=1, source_target_pairs={{0,128},{16,400},{32,160},{48,432},{64,448},{80,208},{96,480},{112... | collective-permute-start | bytes 196616 | tf_op jit(solution)/shard_map/ppermute | solution.py:224
  28.4 2.9 %collective-permute-done.1 = f32[4,16,256]{2,1,0:T(8,128)S(1)} collective-permute-done((f32[4,16,256]{2,1,0:T(8,128)S(1)}, f32[4,16,256]{2,1,0:T(8,128)S(1)}, u32[]{:S(2)}, u32[]{:S(2)}) %collective-permute-start.1) | collective-permute-done | bytes 65568 | tf_op jit(solution)/shard_map/ppermute | solution.py:224
  31.4 5.1 %collective-permute-start.2 = (f32[4,16,256]{2,1,0:T(8,128)S(1)}, f32[4,16,256]{2,1,0:T(8,128)S(1)}, u32[]{:S(2)}, u32[]{:S(2)}) collective-permute-start(f32[4,16,256]{2,1,0:T(8,128)S(1)} %add.3.own_ref), channel_id=1, source_target_pairs={{0,384},{16,144},{32,416},{48,176},{64,192},{80,464},{96,224},{112... | collective-permute-start | bytes 196616 | tf_op jit(solution)/shard_map/ppermute | solution.py:225
  36.4 4.1 %collective-permute-done.2.other_ref = f32[4,16,256]{2,1,0:T(8,128)S(1)} collective-permute-done((f32[4,16,256]{2,1,0:T(8,128)S(1)}, f32[4,16,256]{2,1,0:T(8,128)S(1)}, u32[]{:S(2)}, u32[]{:S(2)}) %collective-permute-start.2) | collective-permute-done | bytes 65568 | tf_op jit(solution)/shard_map/ppermute | solution.py:225
  40.6 1.3 %collective-permute-start.6 = (f32[4,16,256]{2,1,0:T(8,128)S(1)}, f32[4,16,256]{2,1,0:T(8,128)S(1)}, u32[]{:S(2)}, u32[]{:S(2)}) collective-permute-start(f32[4,16,256]{2,1,0:T(8,128)S(1)} %shard_map.61), channel_id=1, source_target_pairs={{0,112},{32,80},{64,48},{96,16},{128,240},{160,208},{192,176},{224... | collective-permute-start | bytes 196616 | tf_op jit(solution)/shard_map/ppermute | solution.py:227
  41.9 1.3 %collective-permute-start.5 = (f32[4,16,256]{2,1,0:T(8,128)S(1)}, f32[4,16,256]{2,1,0:T(8,128)S(1)}, u32[]{:S(2)}, u32[]{:S(2)}) collective-permute-start(f32[4,16,256]{2,1,0:T(8,128)S(1)} %shard_map.61), channel_id=1, source_target_pairs={{0,80},{32,112},{64,16},{96,48},{128,208},{160,240},{192,144},{224... | collective-permute-start | bytes 196616 | tf_op jit(solution)/shard_map/ppermute | solution.py:227
  43.2 1.3 %collective-permute-start.4 = (f32[4,16,256]{2,1,0:T(8,128)S(1)}, f32[4,16,256]{2,1,0:T(8,128)S(1)}, u32[]{:S(2)}, u32[]{:S(2)}) collective-permute-start(f32[4,16,256]{2,1,0:T(8,128)S(1)} %shard_map.61), channel_id=1, source_target_pairs={{0,48},{32,16},{64,112},{96,80},{128,176},{160,144},{192,240},{224... | collective-permute-start | bytes 196616 | tf_op jit(solution)/shard_map/ppermute | solution.py:227
  44.5 1.3 %collective-permute-start.3 = (f32[4,16,256]{2,1,0:T(8,128)S(1)}, f32[4,16,256]{2,1,0:T(8,128)S(1)}, u32[]{:S(2)}, u32[]{:S(2)}) collective-permute-start(f32[4,16,256]{2,1,0:T(8,128)S(1)} %shard_map.61), channel_id=1, source_target_pairs={{0,16},{32,48},{64,80},{96,112},{128,144},{160,176},{192,208},{224... | collective-permute-start | bytes 196616 | tf_op jit(solution)/shard_map/ppermute | solution.py:227
  45.8 8.9 %conditional.2 = (f32[256,256]{1,0:T(8,128)S(1)}) conditional(s32[]{:T(128)} %convert_element_type.4, () %tuple.21, (f32[4,16,256]{2,1,0:T(8,128)S(1)}, f32[4,16,256]{2,1,0:T(8,128)S(1)}) %tuple.22), branch_computations={%region_0.0_spmd, %region_1.0_spmd} | conditional | bytes 524296 | solution.py:228
  45.8 8.9 %all_to_all.17 = f32[4,4,16,256]{3,2,1,0:T(8,128)S(1)} all-to-all(f32[4,4,16,256]{3,2,1,0:T(8,128)S(1)} %branch_1_fun.4), channel_id=1, replica_groups={{0,32,64,96},{16,48,80,112},{128,160,192,224},{144,176,208,240},{256,28..., dimensions={0} | all-to-all | bytes 524288 | tf_op jit(solution)/shard_map/cond/branch_1_fun/all_to_all | solution.py:190
  54.7 0.0 collective-permute-done.6
  54.7 0.0 collective-permute-done.5
  54.7 0.0 collective-permute-done.4
  54.7 0.0 collective-permute-done.3
  54.7 0.0 copy-start.1
  54.8 33.6 %conditional.3 = ((f32[48,256]{1,0:T(8,128)S(1)}, f32[48,256]{1,0:T(8,128)S(1)})) conditional(s32[]{:T(128)} %convert_element_type.4, () %tuple.20, (f32[256,256]{1,0:T(8,128)S(1)}, f32[4,16,256]{2,1,0:T(8,128)S(1)}, f32[4,16,256]{2,1,0:T(8,128)S(1)}, f32[4,16,256]{2,1,0:T(8,128)S(1)}, f32[4,16,256]{2,1,0:T(8,128)S(1)}) %tuple.23), branch_computations={%region_2.0_spmd, %region_3.0_spmd} | conditional | bytes 2621448 | solution.py:229
  54.8 0.7 branch_1_fun.5
  55.5 16.3 %all_to_all.18.parts_ref = f32[16,80,128]{2,1,0:T(8,128)S(1)} all-to-all(f32[16,80,128]{2,1,0:T(8,128)S(1)} %bitcast.7), channel_id=1, replica_groups=mesh['dp'=32,'tensor'=16] {'tensor'}, dimensions={0} | all-to-all | bytes 1310720 | tf_op jit(solution)/shard_map/cond/branch_1_fun/all_to_all | solution.py:190
  71.7 0.1 branch_1_fun.6
  71.8 12.5 %all_to_all.19 = f32[16,80,128]{2,1,0:T(8,128)S(1)} all-to-all(f32[16,80,128]{2,1,0:T(8,128)S(1)} %branch_1_fun.6), channel_id=1, replica_groups=mesh['dp'=32,'tensor'=16] {'tensor'}, dimensions={0} | all-to-all | bytes 1310720 | tf_op jit(solution)/shard_map/cond/branch_1_fun/all_to_all | solution.py:190
  84.3 4.1 %branch_1_fun.7 = (f32[48,256]{1,0:T(8,128)S(1)}, f32[48,256]{1,0:T(8,128)S(1)}) custom-call(f32[1280,128]{1,0:T(8,128)S(1)} %bitcast.4, f32[256,256]{1,0:T(8,128)S(1)} %get-tuple-element.25.first_ref, f32[256,256]{1,0:T(8,128)S(1)} %get-tuple-element.19.last_ref), custom_call_target="tpu_custom_call" | custom-call | tf_op jit(solution)/shard_map/cond/branch_1_fun/pallas_call | solution.py:206
  88.4 1.3 %collective-permute-start.7 = (f32[48,256]{1,0:T(8,128)S(1)}, f32[48,256]{1,0:T(8,128)S(1)}, u32[]{:S(2)}, u32[]{:S(2)}) collective-permute-start(f32[48,256]{1,0:T(8,128)S(1)} %get-tuple-element.32), channel_id=1, source_target_pairs={{16,0},{48,32},{80,64},{112,96},{144,128},{176,160},{208,192},{240... | collective-permute-start | bytes 147464 | tf_op jit(solution)/shard_map/ppermute | solution.py:230
  89.7 0.9 collective-permute-done.7.got_ref
  90.6 0.0 copy-done.1
  90.6 0.6 shard_map.62
  (6 shorter events, 0.1 us)
Async XLA Ops:
  0.6 1.0 %copy-start = (bf16[1,512,256]{2,1,0:T(8,128)(2,1)S(1)}, bf16[1,512,256]{2,1,0:T(8,128)(2,1)}, u32[]{:S(2)}) copy-start(bf16[1,512,256]{2,1,0:T(8,128)(2,1)} %param.7) | copy-start | bytes 786436
  1.6 9.9 %collective-permute-start = (f32[4,4,16,256]{3,2,1,0:T(8,128)S(1)}, f32[4,4,16,256]{3,2,1,0:T(8,128)S(1)}, u32[]{:S(2)}, u32[]{:S(2)}) collective-permute-start(f32[4,4,16,256]{3,2,1,0:T(8,128)S(1)} %shard_map.58), channel_id=1, source_target_pairs={{0,16},{16,0},{32,48},{48,32},{64,80},{80,64},{96,112},{112,96},{1... | collective-permute-start | bytes 786440 | tf_op jit(solution)/shard_map/ppermute | solution.py:222
  11.6 10.7 %copy-start.2 = (f32[16,256]{1,0:T(8,128)S(1)}, f32[16,256]{1,0:T(8,128)}, u32[]{:S(2)}) copy-start(f32[16,256]{1,0:T(8,128)} %momentum_ref.1) | copy-start | bytes 49156
  22.3 9.1 %collective-permute-start.1 = (f32[4,16,256]{2,1,0:T(8,128)S(1)}, f32[4,16,256]{2,1,0:T(8,128)S(1)}, u32[]{:S(2)}, u32[]{:S(2)}) collective-permute-start(f32[4,16,256]{2,1,0:T(8,128)S(1)} %shard_map.60), channel_id=1, source_target_pairs={{0,128},{16,400},{32,160},{48,432},{64,448},{80,208},{96,480},{112... | collective-permute-start | bytes 196616 | tf_op jit(solution)/shard_map/ppermute | solution.py:224
  31.4 9.2 %collective-permute-start.2 = (f32[4,16,256]{2,1,0:T(8,128)S(1)}, f32[4,16,256]{2,1,0:T(8,128)S(1)}, u32[]{:S(2)}, u32[]{:S(2)}) collective-permute-start(f32[4,16,256]{2,1,0:T(8,128)S(1)} %add.3.own_ref), channel_id=1, source_target_pairs={{0,384},{16,144},{32,416},{48,176},{64,192},{80,464},{96,224},{112... | collective-permute-start | bytes 196616 | tf_op jit(solution)/shard_map/ppermute | solution.py:225
  40.6 14.2 %collective-permute-start.6 = (f32[4,16,256]{2,1,0:T(8,128)S(1)}, f32[4,16,256]{2,1,0:T(8,128)S(1)}, u32[]{:S(2)}, u32[]{:S(2)}) collective-permute-start(f32[4,16,256]{2,1,0:T(8,128)S(1)} %shard_map.61), channel_id=1, source_target_pairs={{0,112},{32,80},{64,48},{96,16},{128,240},{160,208},{192,176},{224... | collective-permute-start | bytes 196616 | tf_op jit(solution)/shard_map/ppermute | solution.py:227
  41.9 12.9 %collective-permute-start.5 = (f32[4,16,256]{2,1,0:T(8,128)S(1)}, f32[4,16,256]{2,1,0:T(8,128)S(1)}, u32[]{:S(2)}, u32[]{:S(2)}) collective-permute-start(f32[4,16,256]{2,1,0:T(8,128)S(1)} %shard_map.61), channel_id=1, source_target_pairs={{0,80},{32,112},{64,16},{96,48},{128,208},{160,240},{192,144},{224... | collective-permute-start | bytes 196616 | tf_op jit(solution)/shard_map/ppermute | solution.py:227
  43.2 11.6 %collective-permute-start.4 = (f32[4,16,256]{2,1,0:T(8,128)S(1)}, f32[4,16,256]{2,1,0:T(8,128)S(1)}, u32[]{:S(2)}, u32[]{:S(2)}) collective-permute-start(f32[4,16,256]{2,1,0:T(8,128)S(1)} %shard_map.61), channel_id=1, source_target_pairs={{0,48},{32,16},{64,112},{96,80},{128,176},{160,144},{192,240},{224... | collective-permute-start | bytes 196616 | tf_op jit(solution)/shard_map/ppermute | solution.py:227
  44.5 10.3 %collective-permute-start.3 = (f32[4,16,256]{2,1,0:T(8,128)S(1)}, f32[4,16,256]{2,1,0:T(8,128)S(1)}, u32[]{:S(2)}, u32[]{:S(2)}) collective-permute-start(f32[4,16,256]{2,1,0:T(8,128)S(1)} %shard_map.61), channel_id=1, source_target_pairs={{0,16},{32,48},{64,80},{96,112},{128,144},{160,176},{192,208},{224... | collective-permute-start | bytes 196616 | tf_op jit(solution)/shard_map/ppermute | solution.py:227
  54.7 35.8 %copy-start.1 = (f32[16,256]{1,0:T(8,128)S(1)}, f32[16,256]{1,0:T(8,128)}, u32[]{:S(2)}) copy-start(f32[16,256]{1,0:T(8,128)} %weight_ref.1) | copy-start | bytes 49156
  88.4 2.2 %collective-permute-start.7 = (f32[48,256]{1,0:T(8,128)S(1)}, f32[48,256]{1,0:T(8,128)S(1)}, u32[]{:S(2)}, u32[]{:S(2)}) collective-permute-start(f32[48,256]{1,0:T(8,128)S(1)} %get-tuple-element.32), channel_id=1, source_target_pairs={{16,0},{48,32},{80,64},{112,96},{144,128},{176,160},{208,192},{240... | collective-permute-start | bytes 147464 | tf_op jit(solution)/shard_map/ppermute | solution.py:230

commit v15 on v14

--- a/solution.py
+++ b/solution.py
@@ -53,11 +53,11 @@
             send_ref[near, far] = grad_ref[far, near, 1 - core].astype(f32)
 
 
-def core_sum_kernel(grad_ref, got_ref, out_ref):
+def core_sum_kernel(grad_ref, up_ref, down_ref, out_ref):
     _, _, core = place()
     for near in range(4):
         for far in range(4):
-            out_ref[near, far] = grad_ref[far, near, core].astype(f32) + got_ref[near, far]
+            out_ref[near, far] = grad_ref[far, near, core].astype(f32) + (up_ref[near, far] + down_ref[near, far])
 
 
 def near_sum_kernel(parts_ref, momentum_ref, out_ref):
@@ -219,7 +219,9 @@
     chunks = (4, 4, 16, 256)
     gradients = gradients.reshape(4, 4, 2, 16, 256)
     (send,) = call(send_kernel, [chunks])(gradients)
-    (parts,) = call(core_sum_kernel, [chunks])(gradients, lax.ppermute(send, "dp", CORE))
+    (parts,) = call(core_sum_kernel, [chunks])(
+        gradients, lax.ppermute(send, "dp", BACK), lax.ppermute(send, "dp", DOWN[0])
+    )
     (parts,) = call(near_sum_kernel, [chunks[1:]])(exchange(parts, "dp", NEAR), momentum)
     parts = parts + lax.ppermute(parts, "dp", FAR[0])
     other = lax.ppermute(parts, "dp", FAR[1])

time: 91.6 us -> 93.4 us (1.020)
  starting transfers between devices: 26.5 us -> 28.8 us
    ppermute x1 -> x2, starting transfers between devices: 8.79 us -> 10.1 us  [the longest x1 8.81 us: per_device(): lax.ppermute(send, 'dp', BACK)]
  transfers between devices with their start and end apart: 8 -> 9, of which waited for: 4 -> 4; matrix products, arithmetic and copies ran while one was open for 0% -> 0% of each run, Pallas kernels for 0% -> 0%
where the time goes in v15:
time: 93.4 us; the launch traced here: 93 us
  blocking collectives  48.3 us (52%)
  starting transfers between devices  28.8 us (31%)
  waiting for transfers between devices  8.46 us (9%)
  Pallas kernels  5.6 us (6%)
  local copies, waits for them, and re-layouts  0.96 us (1%)
    all_to_all x4, blocking collectives, exchange(): lax.all_to_all(value, axis, 0, 0, tiled=True, axis_index_groups=groups)  48.3 us
    ppermute x1, starting transfers between devices, per_device(): lax.ppermute(send, 'dp', BACK)  8.81 us
    ppermute x1, starting transfers between devices, per_device(): parts = parts + lax.ppermute(parts, 'dp', FAR[0])  6.61 us
    ppermute x1, starting transfers between devices, per_device(): other = lax.ppermute(parts, 'dp', FAR[1])  5.59 us
    ppermute x4, starting transfers between devices, per_device(): pieces = [lax.ppermute(part, 'dp', pairs) for pairs in DOWN]  5.17 us
    pallas_call x1, Pallas kernels, both_cores(): call(final_kernel, [(48, 256), (48, 256)], [pltpu.VMEM((IN, IN), f32)] +...  4.1 us
    ppermute x1, waiting for transfers between devices, per_device(): other = lax.ppermute(parts, 'dp', FAR[1])  4.08 us
    ppermute x1, waiting for transfers between devices, per_device(): parts = parts + lax.ppermute(parts, 'dp', FAR[0])  2.38 us
  transfers between devices with their start and end apart: 9, of which 4 were waited for; matrix products, arithmetic and copies ran while one was open for 0% of the time, Pallas kernels for 0%

profile of v15, /device:TPU:1, one launch (start us, length us, event | category | flops | bytes accessed | tf_op | source)
XLA Modules:
  0.0 93.0 jit_solution(11022044772055854761)
XLA Ops:
  0.6 0.0 copy-start
  0.6 0.9 %copy-done = bf16[1,512,256]{2,1,0:T(8,128)(2,1)S(1)} copy-done((bf16[1,512,256]{2,1,0:T(8,128)(2,1)S(1)}, bf16[1,512,256]{2,1,0:T(8,128)(2,1)}, u32[]{:S(2)}) %copy-start) | copy-done | bytes 262168
  1.6 1.3 %collective-permute-start.1 = (f32[4,4,16,256]{3,2,1,0:T(8,128)S(1)}, f32[4,4,16,256]{3,2,1,0:T(8,128)S(1)}, u32[]{:S(2)}, u32[]{:S(2)}) collective-permute-start(f32[4,4,16,256]{3,2,1,0:T(8,128)S(1)} %shard_map.58), channel_id=1, source_target_pairs={{0,16},{32,48},{64,80},{96,112},{128,144},{160,176},{192,208},{224... | collective-permute-start | bytes 786440 | tf_op jit(solution)/shard_map/ppermute | solution.py:223
  2.9 8.8 %collective-permute-start = (f32[4,4,16,256]{3,2,1,0:T(8,128)S(1)}, f32[4,4,16,256]{3,2,1,0:T(8,128)S(1)}, u32[]{:S(2)}, u32[]{:S(2)}) collective-permute-start(f32[4,4,16,256]{3,2,1,0:T(8,128)S(1)} %shard_map.58), channel_id=1, source_target_pairs={{16,0},{48,32},{80,64},{112,96},{144,128},{176,160},{208,192},{240... | collective-permute-start | bytes 786440 | tf_op jit(solution)/shard_map/ppermute | solution.py:223
  11.7 0.0 collective-permute-done.1.down_ref
  11.7 1.1 %collective-permute-done.up_ref = f32[4,4,16,256]{3,2,1,0:T(8,128)S(1)} collective-permute-done((f32[4,4,16,256]{3,2,1,0:T(8,128)S(1)}, f32[4,4,16,256]{3,2,1,0:T(8,128)S(1)}, u32[]{:S(2)}, u32[]{:S(2)}) %collective-permute-start) | collective-permute-done | bytes 262176 | tf_op jit(solution)/shard_map/ppermute | solution.py:223
  12.9 0.0 copy-start.2
  12.9 10.7 %all_to_all.20.parts_ref = f32[4,4,16,256]{3,2,1,0:T(8,128)S(1)} all-to-all(f32[4,4,16,256]{3,2,1,0:T(8,128)S(1)} %shard_map.59), channel_id=1, replica_groups={{0,32,64,96},{16,48,80,112},{128,160,192,224},{144,176,208,240},{256,28..., dimensions={0} | all-to-all | bytes 524288 | tf_op jit(solution)/shard_map/all_to_all | solution.py:190
  23.6 0.0 copy-done.2
  23.6 6.6 %collective-permute-start.2 = (f32[4,16,256]{2,1,0:T(8,128)S(1)}, f32[4,16,256]{2,1,0:T(8,128)S(1)}, u32[]{:S(2)}, u32[]{:S(2)}) collective-permute-start(f32[4,16,256]{2,1,0:T(8,128)S(1)} %shard_map.60), channel_id=1, source_target_pairs={{0,128},{16,400},{32,160},{48,432},{64,448},{80,208},{96,480},{112... | collective-permute-start | bytes 196616 | tf_op jit(solution)/shard_map/ppermute | solution.py:226
  30.2 2.4 %collective-permute-done.2 = f32[4,16,256]{2,1,0:T(8,128)S(1)} collective-permute-done((f32[4,16,256]{2,1,0:T(8,128)S(1)}, f32[4,16,256]{2,1,0:T(8,128)S(1)}, u32[]{:S(2)}, u32[]{:S(2)}) %collective-permute-start.2) | collective-permute-done | bytes 65568 | tf_op jit(solution)/shard_map/ppermute | solution.py:226
  32.6 5.6 %collective-permute-start.3 = (f32[4,16,256]{2,1,0:T(8,128)S(1)}, f32[4,16,256]{2,1,0:T(8,128)S(1)}, u32[]{:S(2)}, u32[]{:S(2)}) collective-permute-start(f32[4,16,256]{2,1,0:T(8,128)S(1)} %add.3.own_ref), channel_id=1, source_target_pairs={{0,384},{16,144},{32,416},{48,176},{64,192},{80,464},{96,224},{112... | collective-permute-start | bytes 196616 | tf_op jit(solution)/shard_map/ppermute | solution.py:227
  38.2 4.1 %collective-permute-done.3.other_ref = f32[4,16,256]{2,1,0:T(8,128)S(1)} collective-permute-done((f32[4,16,256]{2,1,0:T(8,128)S(1)}, f32[4,16,256]{2,1,0:T(8,128)S(1)}, u32[]{:S(2)}, u32[]{:S(2)}) %collective-permute-start.3) | collective-permute-done | bytes 65568 | tf_op jit(solution)/shard_map/ppermute | solution.py:227
  42.3 1.3 %collective-permute-start.7 = (f32[4,16,256]{2,1,0:T(8,128)S(1)}, f32[4,16,256]{2,1,0:T(8,128)S(1)}, u32[]{:S(2)}, u32[]{:S(2)}) collective-permute-start(f32[4,16,256]{2,1,0:T(8,128)S(1)} %shard_map.61), channel_id=1, source_target_pairs={{0,112},{32,80},{64,48},{96,16},{128,240},{160,208},{192,176},{224... | collective-permute-start | bytes 196616 | tf_op jit(solution)/shard_map/ppermute | solution.py:229
  43.6 1.3 %collective-permute-start.6 = (f32[4,16,256]{2,1,0:T(8,128)S(1)}, f32[4,16,256]{2,1,0:T(8,128)S(1)}, u32[]{:S(2)}, u32[]{:S(2)}) collective-permute-start(f32[4,16,256]{2,1,0:T(8,128)S(1)} %shard_map.61), channel_id=1, source_target_pairs={{0,80},{32,112},{64,16},{96,48},{128,208},{160,240},{192,144},{224... | collective-permute-start | bytes 196616 | tf_op jit(solution)/shard_map/ppermute | solution.py:229
  44.9 1.3 %collective-permute-start.5 = (f32[4,16,256]{2,1,0:T(8,128)S(1)}, f32[4,16,256]{2,1,0:T(8,128)S(1)}, u32[]{:S(2)}, u32[]{:S(2)}) collective-permute-start(f32[4,16,256]{2,1,0:T(8,128)S(1)} %shard_map.61), channel_id=1, source_target_pairs={{0,48},{32,16},{64,112},{96,80},{128,176},{160,144},{192,240},{224... | collective-permute-start | bytes 196616 | tf_op jit(solution)/shard_map/ppermute | solution.py:229
  46.2 1.3 %collective-permute-start.4 = (f32[4,16,256]{2,1,0:T(8,128)S(1)}, f32[4,16,256]{2,1,0:T(8,128)S(1)}, u32[]{:S(2)}, u32[]{:S(2)}) collective-permute-start(f32[4,16,256]{2,1,0:T(8,128)S(1)} %shard_map.61), channel_id=1, source_target_pairs={{0,16},{32,48},{64,80},{96,112},{128,144},{160,176},{192,208},{224... | collective-permute-start | bytes 196616 | tf_op jit(solution)/shard_map/ppermute | solution.py:229
  47.5 9.0 %conditional.2 = (f32[256,256]{1,0:T(8,128)S(1)}) conditional(s32[]{:T(128)} %convert_element_type.4, () %tuple.21, (f32[4,16,256]{2,1,0:T(8,128)S(1)}, f32[4,16,256]{2,1,0:T(8,128)S(1)}) %tuple.22), branch_computations={%region_0.0_spmd, %region_1.0_spmd} | conditional | bytes 524296 | solution.py:230
  47.6 8.9 %all_to_all.17 = f32[4,4,16,256]{3,2,1,0:T(8,128)S(1)} all-to-all(f32[4,4,16,256]{3,2,1,0:T(8,128)S(1)} %branch_1_fun.4), channel_id=1, replica_groups={{0,32,64,96},{16,48,80,112},{128,160,192,224},{144,176,208,240},{256,28..., dimensions={0} | all-to-all | bytes 524288 | tf_op jit(solution)/shard_map/cond/branch_1_fun/all_to_all | solution.py:190
  56.5 0.0 collective-permute-done.7
  56.5 0.0 collective-permute-done.6
  56.5 0.0 collective-permute-done.5
  56.5 0.0 collective-permute-done.4
  56.5 0.0 copy-start.1
  56.5 33.6 %conditional.3 = ((f32[48,256]{1,0:T(8,128)S(1)}, f32[48,256]{1,0:T(8,128)S(1)})) conditional(s32[]{:T(128)} %convert_element_type.4, () %tuple.20, (f32[256,256]{1,0:T(8,128)S(1)}, f32[4,16,256]{2,1,0:T(8,128)S(1)}, f32[4,16,256]{2,1,0:T(8,128)S(1)}, f32[4,16,256]{2,1,0:T(8,128)S(1)}, f32[4,16,256]{2,1,0:T(8,128)S(1)}) %tuple.23), branch_computations={%region_2.0_spmd, %region_3.0_spmd} | conditional | bytes 2621448 | solution.py:231
  56.5 0.7 branch_1_fun.5
  57.3 16.2 %all_to_all.18.parts_ref = f32[16,80,128]{2,1,0:T(8,128)S(1)} all-to-all(f32[16,80,128]{2,1,0:T(8,128)S(1)} %bitcast.7), channel_id=1, replica_groups=mesh['dp'=32,'tensor'=16] {'tensor'}, dimensions={0} | all-to-all | bytes 1310720 | tf_op jit(solution)/shard_map/cond/branch_1_fun/all_to_all | solution.py:190
  73.5 0.1 branch_1_fun.6
  73.6 12.5 %all_to_all.19 = f32[16,80,128]{2,1,0:T(8,128)S(1)} all-to-all(f32[16,80,128]{2,1,0:T(8,128)S(1)} %branch_1_fun.6), channel_id=1, replica_groups=mesh['dp'=32,'tensor'=16] {'tensor'}, dimensions={0} | all-to-all | bytes 1310720 | tf_op jit(solution)/shard_map/cond/branch_1_fun/all_to_all | solution.py:190
  86.1 4.1 %branch_1_fun.7 = (f32[48,256]{1,0:T(8,128)S(1)}, f32[48,256]{1,0:T(8,128)S(1)}) custom-call(f32[1280,128]{1,0:T(8,128)S(1)} %bitcast.4, f32[256,256]{1,0:T(8,128)S(1)} %get-tuple-element.25.first_ref, f32[256,256]{1,0:T(8,128)S(1)} %get-tuple-element.19.last_ref), custom_call_target="tpu_custom_call" | custom-call | tf_op jit(solution)/shard_map/cond/branch_1_fun/pallas_call | solution.py:206
  90.2 1.3 %collective-permute-start.8 = (f32[48,256]{1,0:T(8,128)S(1)}, f32[48,256]{1,0:T(8,128)S(1)}, u32[]{:S(2)}, u32[]{:S(2)}) collective-permute-start(f32[48,256]{1,0:T(8,128)S(1)} %get-tuple-element.32), channel_id=1, source_target_pairs={{16,0},{48,32},{80,64},{112,96},{144,128},{176,160},{208,192},{240... | collective-permute-start | bytes 147464 | tf_op jit(solution)/shard_map/ppermute | solution.py:232
  91.5 0.9 collective-permute-done.8.got_ref
  92.3 0.0 copy-done.1
  92.3 0.6 shard_map.62
  (6 shorter events, 0.1 us)
Async XLA Ops:
  0.6 1.0 %copy-start = (bf16[1,512,256]{2,1,0:T(8,128)(2,1)S(1)}, bf16[1,512,256]{2,1,0:T(8,128)(2,1)}, u32[]{:S(2)}) copy-start(bf16[1,512,256]{2,1,0:T(8,128)(2,1)} %param.7) | copy-start | bytes 786436
  1.6 10.1 %collective-permute-start.1 = (f32[4,4,16,256]{3,2,1,0:T(8,128)S(1)}, f32[4,4,16,256]{3,2,1,0:T(8,128)S(1)}, u32[]{:S(2)}, u32[]{:S(2)}) collective-permute-start(f32[4,4,16,256]{3,2,1,0:T(8,128)S(1)} %shard_map.58), channel_id=1, source_target_pairs={{0,16},{32,48},{64,80},{96,112},{128,144},{160,176},{192,208},{224... | collective-permute-start | bytes 786440 | tf_op jit(solution)/shard_map/ppermute | solution.py:223
  2.9 9.9 %collective-permute-start = (f32[4,4,16,256]{3,2,1,0:T(8,128)S(1)}, f32[4,4,16,256]{3,2,1,0:T(8,128)S(1)}, u32[]{:S(2)}, u32[]{:S(2)}) collective-permute-start(f32[4,4,16,256]{3,2,1,0:T(8,128)S(1)} %shard_map.58), channel_id=1, source_target_pairs={{16,0},{48,32},{80,64},{112,96},{144,128},{176,160},{208,192},{240... | collective-permute-start | bytes 786440 | tf_op jit(solution)/shard_map/ppermute | solution.py:223
  12.9 10.7 %copy-start.2 = (f32[16,256]{1,0:T(8,128)S(1)}, f32[16,256]{1,0:T(8,128)}, u32[]{:S(2)}) copy-start(f32[16,256]{1,0:T(8,128)} %momentum_ref.1) | copy-start | bytes 49156
  23.6 9.0 %collective-permute-start.2 = (f32[4,16,256]{2,1,0:T(8,128)S(1)}, f32[4,16,256]{2,1,0:T(8,128)S(1)}, u32[]{:S(2)}, u32[]{:S(2)}) collective-permute-start(f32[4,16,256]{2,1,0:T(8,128)S(1)} %shard_map.60), channel_id=1, source_target_pairs={{0,128},{16,400},{32,160},{48,432},{64,448},{80,208},{96,480},{112... | collective-permute-start | bytes 196616 | tf_op jit(solution)/shard_map/ppermute | solution.py:226
  32.6 9.7 %collective-permute-start.3 = (f32[4,16,256]{2,1,0:T(8,128)S(1)}, f32[4,16,256]{2,1,0:T(8,128)S(1)}, u32[]{:S(2)}, u32[]{:S(2)}) collective-permute-start(f32[4,16,256]{2,1,0:T(8,128)S(1)} %add.3.own_ref), channel_id=1, source_target_pairs={{0,384},{16,144},{32,416},{48,176},{64,192},{80,464},{96,224},{112... | collective-permute-start | bytes 196616 | tf_op jit(solution)/shard_map/ppermute | solution.py:227
  42.3 14.2 %collective-permute-start.7 = (f32[4,16,256]{2,1,0:T(8,128)S(1)}, f32[4,16,256]{2,1,0:T(8,128)S(1)}, u32[]{:S(2)}, u32[]{:S(2)}) collective-permute-start(f32[4,16,256]{2,1,0:T(8,128)S(1)} %shard_map.61), channel_id=1, source_target_pairs={{0,112},{32,80},{64,48},{96,16},{128,240},{160,208},{192,176},{224... | collective-permute-start | bytes 196616 | tf_op jit(solution)/shard_map/ppermute | solution.py:229
  43.6 12.9 %collective-permute-start.6 = (f32[4,16,256]{2,1,0:T(8,128)S(1)}, f32[4,16,256]{2,1,0:T(8,128)S(1)}, u32[]{:S(2)}, u32[]{:S(2)}) collective-permute-start(f32[4,16,256]{2,1,0:T(8,128)S(1)} %shard_map.61), channel_id=1, source_target_pairs={{0,80},{32,112},{64,16},{96,48},{128,208},{160,240},{192,144},{224... | collective-permute-start | bytes 196616 | tf_op jit(solution)/shard_map/ppermute | solution.py:229
  44.9 11.6 %collective-permute-start.5 = (f32[4,16,256]{2,1,0:T(8,128)S(1)}, f32[4,16,256]{2,1,0:T(8,128)S(1)}, u32[]{:S(2)}, u32[]{:S(2)}) collective-permute-start(f32[4,16,256]{2,1,0:T(8,128)S(1)} %shard_map.61), channel_id=1, source_target_pairs={{0,48},{32,16},{64,112},{96,80},{128,176},{160,144},{192,240},{224... | collective-permute-start | bytes 196616 | tf_op jit(solution)/shard_map/ppermute | solution.py:229
  46.2 10.3 %collective-permute-start.4 = (f32[4,16,256]{2,1,0:T(8,128)S(1)}, f32[4,16,256]{2,1,0:T(8,128)S(1)}, u32[]{:S(2)}, u32[]{:S(2)}) collective-permute-start(f32[4,16,256]{2,1,0:T(8,128)S(1)} %shard_map.61), channel_id=1, source_target_pairs={{0,16},{32,48},{64,80},{96,112},{128,144},{160,176},{192,208},{224... | collective-permute-start | bytes 196616 | tf_op jit(solution)/shard_map/ppermute | solution.py:229
  56.5 35.8 %copy-start.1 = (f32[16,256]{1,0:T(8,128)S(1)}, f32[16,256]{1,0:T(8,128)}, u32[]{:S(2)}) copy-start(f32[16,256]{1,0:T(8,128)} %weight_ref.1) | copy-start | bytes 49156
  90.2 2.2 %collective-permute-start.8 = (f32[48,256]{1,0:T(8,128)S(1)}, f32[48,256]{1,0:T(8,128)S(1)}, u32[]{:S(2)}, u32[]{:S(2)}) collective-permute-start(f32[48,256]{1,0:T(8,128)S(1)} %get-tuple-element.32), channel_id=1, source_target_pairs={{16,0},{48,32},{80,64},{112,96},{144,128},{176,160},{208,192},{240... | collective-permute-start | bytes 147464 | tf_op jit(solution)/shard_map/ppermute | solution.py:232

commit v16 on v14

--- a/solution.py
+++ b/solution.py
@@ -24,7 +24,7 @@
 BACK = [(i + 1, i) for i in range(0, 32, 2)]
 BLOCKS = [(row, column) for row in range(4) for column in range(row, 4)]
 NEAR = [[8 * far + 2 * near + core for near in range(4)] for far in range(4) for core in range(2)]
-FAR = [[(i, i ^ (8 * steps[(i + i // 4) % 2])) for i in range(32)] for steps in ((1, 3), (3, 1))]
+FAR = [[(i, i ^ (8 * steps[(1 + i + i // 4) % 2])) for i in range(32)] for steps in ((1, 3), (3, 1))]
 
 NT = (((1,), (1,)), ((), ()))
 NN = (((1,), (0,)), ((), ()))

time: 91.6 us -> 91.7 us (level)
    ppermute x1, waiting for transfers between devices: 4.13 us -> 2.96 us  [per_device(): other = lax.ppermute(parts, 'dp', FAR[1])]
    ppermute x1, waiting for transfers between devices: 2.91 us -> 4.01 us  [per_device(): parts = parts + lax.ppermute(parts, 'dp', FAR[0])]
    ppermute x1, starting transfers between devices: 6.16 us -> 5.22 us  [per_device(): parts = parts + lax.ppermute(parts, 'dp', FAR[0])]
where the time goes in v16:
time: 91.7 us; the launch traced here: 91.3 us
  blocking collectives  48.5 us (53%)
  starting transfers between devices  26.4 us (29%)
  waiting for transfers between devices  8.98 us (10%)
  Pallas kernels  5.59 us (6%)
  local copies, waits for them, and re-layouts  0.96 us (1%)
    all_to_all x4, blocking collectives, exchange(): lax.all_to_all(value, axis, 0, 0, tiled=True, axis_index_groups=groups)  48.5 us
    ppermute x1, starting transfers between devices, per_device(): lax.ppermute(send, 'dp', CORE)  8.79 us
    ppermute x1, starting transfers between devices, per_device(): other = lax.ppermute(parts, 'dp', FAR[1])  5.95 us
    ppermute x1, starting transfers between devices, per_device(): parts = parts + lax.ppermute(parts, 'dp', FAR[0])  5.22 us
    ppermute x4, starting transfers between devices, per_device(): pieces = [lax.ppermute(part, 'dp', pairs) for pairs in DOWN]  5.17 us
    pallas_call x1, Pallas kernels, both_cores(): call(final_kernel, [(48, 256), (48, 256)], [pltpu.VMEM((IN, IN), f32)] +...  4.1 us
    ppermute x1, waiting for transfers between devices, per_device(): parts = parts + lax.ppermute(parts, 'dp', FAR[0])  4.01 us
    ppermute x1, waiting for transfers between devices, per_device(): other = lax.ppermute(parts, 'dp', FAR[1])  2.96 us
  transfers between devices with their start and end apart: 8, of which 4 were waited for; matrix products, arithmetic and copies ran while one was open for 0% of the time, Pallas kernels for 0%

profile of v16, /device:TPU:1, one launch (start us, length us, event | category | flops | bytes accessed | tf_op | source)
XLA Modules:
  0.0 91.3 jit_solution(479687954317641048)
XLA Ops:
  0.6 0.0 copy-start
  0.6 0.9 %copy-done = bf16[1,512,256]{2,1,0:T(8,128)(2,1)S(1)} copy-done((bf16[1,512,256]{2,1,0:T(8,128)(2,1)S(1)}, bf16[1,512,256]{2,1,0:T(8,128)(2,1)}, u32[]{:S(2)}) %copy-start) | copy-done | bytes 262168
  1.6 8.8 %collective-permute-start = (f32[4,4,16,256]{3,2,1,0:T(8,128)S(1)}, f32[4,4,16,256]{3,2,1,0:T(8,128)S(1)}, u32[]{:S(2)}, u32[]{:S(2)}) collective-permute-start(f32[4,4,16,256]{3,2,1,0:T(8,128)S(1)} %shard_map.58), channel_id=1, source_target_pairs={{0,16},{16,0},{32,48},{48,32},{64,80},{80,64},{96,112},{112,96},{1... | collective-permute-start | bytes 786440 | tf_op jit(solution)/shard_map/ppermute | solution.py:222
  10.4 1.1 %collective-permute-done.got_ref = f32[4,4,16,256]{3,2,1,0:T(8,128)S(1)} collective-permute-done((f32[4,4,16,256]{3,2,1,0:T(8,128)S(1)}, f32[4,4,16,256]{3,2,1,0:T(8,128)S(1)}, u32[]{:S(2)}, u32[]{:S(2)}) %collective-permute-start) | collective-permute-done | bytes 262176 | tf_op jit(solution)/shard_map/ppermute | solution.py:222
  11.6 0.0 copy-start.2
  11.6 10.7 %all_to_all.20.parts_ref = f32[4,4,16,256]{3,2,1,0:T(8,128)S(1)} all-to-all(f32[4,4,16,256]{3,2,1,0:T(8,128)S(1)} %shard_map.59), channel_id=1, replica_groups={{0,32,64,96},{16,48,80,112},{128,160,192,224},{144,176,208,240},{256,28..., dimensions={0} | all-to-all | bytes 524288 | tf_op jit(solution)/shard_map/all_to_all | solution.py:190
  22.2 0.0 copy-done.2
  22.3 5.2 %collective-permute-start.1 = (f32[4,16,256]{2,1,0:T(8,128)S(1)}, f32[4,16,256]{2,1,0:T(8,128)S(1)}, u32[]{:S(2)}, u32[]{:S(2)}) collective-permute-start(f32[4,16,256]{2,1,0:T(8,128)S(1)} %shard_map.60), channel_id=1, source_target_pairs={{0,384},{16,144},{32,416},{48,176},{64,192},{80,464},{96,224},{112... | collective-permute-start | bytes 196616 | tf_op jit(solution)/shard_map/ppermute | solution.py:224
  27.5 4.0 %collective-permute-done.1 = f32[4,16,256]{2,1,0:T(8,128)S(1)} collective-permute-done((f32[4,16,256]{2,1,0:T(8,128)S(1)}, f32[4,16,256]{2,1,0:T(8,128)S(1)}, u32[]{:S(2)}, u32[]{:S(2)}) %collective-permute-start.1) | collective-permute-done | bytes 65568 | tf_op jit(solution)/shard_map/ppermute | solution.py:224
  31.5 5.9 %collective-permute-start.2 = (f32[4,16,256]{2,1,0:T(8,128)S(1)}, f32[4,16,256]{2,1,0:T(8,128)S(1)}, u32[]{:S(2)}, u32[]{:S(2)}) collective-permute-start(f32[4,16,256]{2,1,0:T(8,128)S(1)} %add.3.own_ref), channel_id=1, source_target_pairs={{0,128},{16,400},{32,160},{48,432},{64,448},{80,208},{96,480},{112... | collective-permute-start | bytes 196616 | tf_op jit(solution)/shard_map/ppermute | solution.py:225
  37.5 3.0 %collective-permute-done.2.other_ref = f32[4,16,256]{2,1,0:T(8,128)S(1)} collective-permute-done((f32[4,16,256]{2,1,0:T(8,128)S(1)}, f32[4,16,256]{2,1,0:T(8,128)S(1)}, u32[]{:S(2)}, u32[]{:S(2)}) %collective-permute-start.2) | collective-permute-done | bytes 65568 | tf_op jit(solution)/shard_map/ppermute | solution.py:225
  40.4 1.3 %collective-permute-start.6 = (f32[4,16,256]{2,1,0:T(8,128)S(1)}, f32[4,16,256]{2,1,0:T(8,128)S(1)}, u32[]{:S(2)}, u32[]{:S(2)}) collective-permute-start(f32[4,16,256]{2,1,0:T(8,128)S(1)} %shard_map.61), channel_id=1, source_target_pairs={{0,112},{32,80},{64,48},{96,16},{128,240},{160,208},{192,176},{224... | collective-permute-start | bytes 196616 | tf_op jit(solution)/shard_map/ppermute | solution.py:227
  41.7 1.3 %collective-permute-start.5 = (f32[4,16,256]{2,1,0:T(8,128)S(1)}, f32[4,16,256]{2,1,0:T(8,128)S(1)}, u32[]{:S(2)}, u32[]{:S(2)}) collective-permute-start(f32[4,16,256]{2,1,0:T(8,128)S(1)} %shard_map.61), channel_id=1, source_target_pairs={{0,80},{32,112},{64,16},{96,48},{128,208},{160,240},{192,144},{224... | collective-permute-start | bytes 196616 | tf_op jit(solution)/shard_map/ppermute | solution.py:227
  43.0 1.3 %collective-permute-start.4 = (f32[4,16,256]{2,1,0:T(8,128)S(1)}, f32[4,16,256]{2,1,0:T(8,128)S(1)}, u32[]{:S(2)}, u32[]{:S(2)}) collective-permute-start(f32[4,16,256]{2,1,0:T(8,128)S(1)} %shard_map.61), channel_id=1, source_target_pairs={{0,48},{32,16},{64,112},{96,80},{128,176},{160,144},{192,240},{224... | collective-permute-start | bytes 196616 | tf_op jit(solution)/shard_map/ppermute | solution.py:227
  44.3 1.3 %collective-permute-start.3 = (f32[4,16,256]{2,1,0:T(8,128)S(1)}, f32[4,16,256]{2,1,0:T(8,128)S(1)}, u32[]{:S(2)}, u32[]{:S(2)}) collective-permute-start(f32[4,16,256]{2,1,0:T(8,128)S(1)} %shard_map.61), channel_id=1, source_target_pairs={{0,16},{32,48},{64,80},{96,112},{128,144},{160,176},{192,208},{224... | collective-permute-start | bytes 196616 | tf_op jit(solution)/shard_map/ppermute | solution.py:227
  45.7 9.1 %conditional.2 = (f32[256,256]{1,0:T(8,128)S(1)}) conditional(s32[]{:T(128)} %convert_element_type.4, () %tuple.21, (f32[4,16,256]{2,1,0:T(8,128)S(1)}, f32[4,16,256]{2,1,0:T(8,128)S(1)}) %tuple.22), branch_computations={%region_0.0_spmd, %region_1.0_spmd} | conditional | bytes 524296 | solution.py:228
  45.7 9.1 %all_to_all.17 = f32[4,4,16,256]{3,2,1,0:T(8,128)S(1)} all-to-all(f32[4,4,16,256]{3,2,1,0:T(8,128)S(1)} %branch_1_fun.4), channel_id=1, replica_groups={{0,32,64,96},{16,48,80,112},{128,160,192,224},{144,176,208,240},{256,28..., dimensions={0} | all-to-all | bytes 524288 | tf_op jit(solution)/shard_map/cond/branch_1_fun/all_to_all | solution.py:190
  54.8 0.0 collective-permute-done.6
  54.8 0.0 collective-permute-done.5
  54.8 0.0 collective-permute-done.4
  54.8 0.0 collective-permute-done.3
  54.8 0.0 copy-start.1
  54.8 33.7 %conditional.3 = ((f32[48,256]{1,0:T(8,128)S(1)}, f32[48,256]{1,0:T(8,128)S(1)})) conditional(s32[]{:T(128)} %convert_element_type.4, () %tuple.20, (f32[256,256]{1,0:T(8,128)S(1)}, f32[4,16,256]{2,1,0:T(8,128)S(1)}, f32[4,16,256]{2,1,0:T(8,128)S(1)}, f32[4,16,256]{2,1,0:T(8,128)S(1)}, f32[4,16,256]{2,1,0:T(8,128)S(1)}) %tuple.23), branch_computations={%region_2.0_spmd, %region_3.0_spmd} | conditional | bytes 2621448 | solution.py:229
  54.8 0.7 branch_1_fun.5
  55.5 16.3 %all_to_all.18.parts_ref = f32[16,80,128]{2,1,0:T(8,128)S(1)} all-to-all(f32[16,80,128]{2,1,0:T(8,128)S(1)} %bitcast.7), channel_id=1, replica_groups=mesh['dp'=32,'tensor'=16] {'tensor'}, dimensions={0} | all-to-all | bytes 1310720 | tf_op jit(solution)/shard_map/cond/branch_1_fun/all_to_all | solution.py:190
  71.8 0.1 branch_1_fun.6
  71.9 12.5 %all_to_all.19 = f32[16,80,128]{2,1,0:T(8,128)S(1)} all-to-all(f32[16,80,128]{2,1,0:T(8,128)S(1)} %branch_1_fun.6), channel_id=1, replica_groups=mesh['dp'=32,'tensor'=16] {'tensor'}, dimensions={0} | all-to-all | bytes 1310720 | tf_op jit(solution)/shard_map/cond/branch_1_fun/all_to_all | solution.py:190
  84.4 4.1 %branch_1_fun.7 = (f32[48,256]{1,0:T(8,128)S(1)}, f32[48,256]{1,0:T(8,128)S(1)}) custom-call(f32[1280,128]{1,0:T(8,128)S(1)} %bitcast.4, f32[256,256]{1,0:T(8,128)S(1)} %get-tuple-element.25.first_ref, f32[256,256]{1,0:T(8,128)S(1)} %get-tuple-element.19.last_ref), custom_call_target="tpu_custom_call" | custom-call | tf_op jit(solution)/shard_map/cond/branch_1_fun/pallas_call | solution.py:206
  88.5 1.3 %collective-permute-start.7 = (f32[48,256]{1,0:T(8,128)S(1)}, f32[48,256]{1,0:T(8,128)S(1)}, u32[]{:S(2)}, u32[]{:S(2)}) collective-permute-start(f32[48,256]{1,0:T(8,128)S(1)} %get-tuple-element.32), channel_id=1, source_target_pairs={{16,0},{48,32},{80,64},{112,96},{144,128},{176,160},{208,192},{240... | collective-permute-start | bytes 147464 | tf_op jit(solution)/shard_map/ppermute | solution.py:230
  89.8 0.9 collective-permute-done.7.got_ref
  90.6 0.0 copy-done.1
  90.6 0.6 shard_map.62
  (6 shorter events, 0.1 us)
Async XLA Ops:
  0.6 1.0 %copy-start = (bf16[1,512,256]{2,1,0:T(8,128)(2,1)S(1)}, bf16[1,512,256]{2,1,0:T(8,128)(2,1)}, u32[]{:S(2)}) copy-start(bf16[1,512,256]{2,1,0:T(8,128)(2,1)} %param.7) | copy-start | bytes 786436
  1.6 9.9 %collective-permute-start = (f32[4,4,16,256]{3,2,1,0:T(8,128)S(1)}, f32[4,4,16,256]{3,2,1,0:T(8,128)S(1)}, u32[]{:S(2)}, u32[]{:S(2)}) collective-permute-start(f32[4,4,16,256]{3,2,1,0:T(8,128)S(1)} %shard_map.58), channel_id=1, source_target_pairs={{0,16},{16,0},{32,48},{48,32},{64,80},{80,64},{96,112},{112,96},{1... | collective-permute-start | bytes 786440 | tf_op jit(solution)/shard_map/ppermute | solution.py:222
  11.6 10.7 %copy-start.2 = (f32[16,256]{1,0:T(8,128)S(1)}, f32[16,256]{1,0:T(8,128)}, u32[]{:S(2)}) copy-start(f32[16,256]{1,0:T(8,128)} %momentum_ref.1) | copy-start | bytes 49156
  22.3 9.2 %collective-permute-start.1 = (f32[4,16,256]{2,1,0:T(8,128)S(1)}, f32[4,16,256]{2,1,0:T(8,128)S(1)}, u32[]{:S(2)}, u32[]{:S(2)}) collective-permute-start(f32[4,16,256]{2,1,0:T(8,128)S(1)} %shard_map.60), channel_id=1, source_target_pairs={{0,384},{16,144},{32,416},{48,176},{64,192},{80,464},{96,224},{112... | collective-permute-start | bytes 196616 | tf_op jit(solution)/shard_map/ppermute | solution.py:224
  31.5 8.9 %collective-permute-start.2 = (f32[4,16,256]{2,1,0:T(8,128)S(1)}, f32[4,16,256]{2,1,0:T(8,128)S(1)}, u32[]{:S(2)}, u32[]{:S(2)}) collective-permute-start(f32[4,16,256]{2,1,0:T(8,128)S(1)} %add.3.own_ref), channel_id=1, source_target_pairs={{0,128},{16,400},{32,160},{48,432},{64,448},{80,208},{96,480},{112... | collective-permute-start | bytes 196616 | tf_op jit(solution)/shard_map/ppermute | solution.py:225
  40.4 14.3 %collective-permute-start.6 = (f32[4,16,256]{2,1,0:T(8,128)S(1)}, f32[4,16,256]{2,1,0:T(8,128)S(1)}, u32[]{:S(2)}, u32[]{:S(2)}) collective-permute-start(f32[4,16,256]{2,1,0:T(8,128)S(1)} %shard_map.61), channel_id=1, source_target_pairs={{0,112},{32,80},{64,48},{96,16},{128,240},{160,208},{192,176},{224... | collective-permute-start | bytes 196616 | tf_op jit(solution)/shard_map/ppermute | solution.py:227
  41.7 13.0 %collective-permute-start.5 = (f32[4,16,256]{2,1,0:T(8,128)S(1)}, f32[4,16,256]{2,1,0:T(8,128)S(1)}, u32[]{:S(2)}, u32[]{:S(2)}) collective-permute-start(f32[4,16,256]{2,1,0:T(8,128)S(1)} %shard_map.61), channel_id=1, source_target_pairs={{0,80},{32,112},{64,16},{96,48},{128,208},{160,240},{192,144},{224... | collective-permute-start | bytes 196616 | tf_op jit(solution)/shard_map/ppermute | solution.py:227
  43.0 11.7 %collective-permute-start.4 = (f32[4,16,256]{2,1,0:T(8,128)S(1)}, f32[4,16,256]{2,1,0:T(8,128)S(1)}, u32[]{:S(2)}, u32[]{:S(2)}) collective-permute-start(f32[4,16,256]{2,1,0:T(8,128)S(1)} %shard_map.61), channel_id=1, source_target_pairs={{0,48},{32,16},{64,112},{96,80},{128,176},{160,144},{192,240},{224... | collective-permute-start | bytes 196616 | tf_op jit(solution)/shard_map/ppermute | solution.py:227
  44.3 10.4 %collective-permute-start.3 = (f32[4,16,256]{2,1,0:T(8,128)S(1)}, f32[4,16,256]{2,1,0:T(8,128)S(1)}, u32[]{:S(2)}, u32[]{:S(2)}) collective-permute-start(f32[4,16,256]{2,1,0:T(8,128)S(1)} %shard_map.61), channel_id=1, source_target_pairs={{0,16},{32,48},{64,80},{96,112},{128,144},{160,176},{192,208},{224... | collective-permute-start | bytes 196616 | tf_op jit(solution)/shard_map/ppermute | solution.py:227
  54.8 35.8 %copy-start.1 = (f32[16,256]{1,0:T(8,128)S(1)}, f32[16,256]{1,0:T(8,128)}, u32[]{:S(2)}) copy-start(f32[16,256]{1,0:T(8,128)} %weight_ref.1) | copy-start | bytes 49156
  88.5 2.2 %collective-permute-start.7 = (f32[48,256]{1,0:T(8,128)S(1)}, f32[48,256]{1,0:T(8,128)S(1)}, u32[]{:S(2)}, u32[]{:S(2)}) collective-permute-start(f32[48,256]{1,0:T(8,128)S(1)} %get-tuple-element.32), channel_id=1, source_target_pairs={{16,0},{48,32},{80,64},{112,96},{144,128},{176,160},{208,192},{240... | collective-permute-start | bytes 147464 | tf_op jit(solution)/shard_map/ppermute | solution.py:230
